TPU v7x, 32 devices: a whole 2x2x4 slice. The times are simulated.
32 devices in a mesh: ep: 8 (over y, x, core), hs: 4 (over z).
Axes of the slice: x: 2, y: 2, z: 4, core: 2. Of those that a mesh axis runs over, the one named last changes fastest.
Arguments:
- tokens: bfloat16 [4096, 1280], P('ep'), may hold values from -6 to 6
- attn_gain: float32 [1280], replicated, may hold values from 0.5 to 1.5
- attn_query: bfloat16 [1280, 1280], P(None, 'hs'), may hold values from -0.15625 to 0.15625
- attn_key: bfloat16 [1280, 1280], P(None, 'hs'), may hold values from -0.15625 to 0.15625
- attn_value: bfloat16 [1280, 1280], P(None, 'hs'), may hold values from -0.15625 to 0.15625
- attn_out: bfloat16 [1280, 1280], P(None, 'hs'), may hold values from -0.625 to 0.625
- ffn_gain: float32 [1280], replicated, may hold values from 0.5 to 1.5
- router: bfloat16 [1280, 64], replicated, may hold values from -0.078125 to 0.078125
- shared_gate: bfloat16 [1280, 1792], P(None, 'hs'), may hold values from -0.15625 to 0.15625
- shared_up: bfloat16 [1280, 1792], P(None, 'hs'), may hold values from -0.15625 to 0.15625
- shared_down: bfloat16 [1792, 1280], P('hs'), may hold values from -0.125 to 0.125
- expert_gate: bfloat16 [64, 1280, 896], P('ep', None, 'hs'), may hold values from -0.15625 to 0.15625
- expert_up: bfloat16 [64, 1280, 896], P('ep', None, 'hs'), may hold values from -0.15625 to 0.15625
- expert_down: bfloat16 [64, 896, 1280], P('ep', 'hs'), may hold values from -6 to 6
- routes: int32 [4096, 7], P('ep'), may hold values from 0 to 63, all different within a row; in each aligned block of 512 rows (0 to 511, 512 to 1023, ...) at most 112 rows name the same one
- documents: int32 [8, 512], P('ep'), may hold values from 0 to 3, never falling along the last dimension, each value on 1 to 256 neighbouring positions
- out_grad: bfloat16 [4096, 1280], P('ep', 'hs'), may hold values from -6 to 6
Outputs:
- output: bfloat16 [4096, 1280], P('ep', 'hs')
- grad_tokens: float32 [4096, 1280], P('ep', 'hs')
- grad_attn_gain: float32 [1280], replicated
- grad_attn_query: float32 [1280, 1280], P(None, 'hs')
- grad_attn_key: float32 [1280, 1280], P(None, 'hs')
- grad_attn_value: float32 [1280, 1280], P(None, 'hs')
- grad_attn_out: float32 [1280, 1280], P(None, 'hs')
- grad_ffn_gain: float32 [1280], replicated
- grad_router: float32 [1280, 64], replicated
- grad_shared_gate: float32 [1280, 1792], P(None, 'hs')
- grad_shared_up: float32 [1280, 1792], P(None, 'hs')
- grad_shared_down: float32 [1792, 1280], P('hs')
- grad_expert_gate: float32 [64, 1280, 896], P('ep', None, 'hs')
- grad_expert_up: float32 [64, 1280, 896], P('ep', None, 'hs')
- grad_expert_down: float32 [64, 896, 1280], P('ep', 'hs')
Inputs may be any that keep to these rules, and one draw needn't show every extreme that they name: `routes`: each row names 7 different experts and every expert is named by some row; the 512 rows of one sequence name any one expert at most 112 times, and in every draw the rows of some sequence name some expert exactly 112 times. `documents`: within each sequence the document number never falls; each document spans 1 to half of 512 positions.
All inputs are finite; a program needn't handle non-finite values.
Results may differ from a plain program's by a relative error of at most 0.02.
Values may be sent and summed in bfloat16 or wider, within the bound.
A program may use at most 448 MiB of HBM per device.

v0:
```python
import functools
import math

import jax
import jax.numpy as jnp
import numpy as np
from jax import lax
from jax.experimental import pallas as pl
from jax.experimental.layout import Layout, with_layout_constraint
from jax.experimental.pallas import tpu as pltpu
from jax.sharding import Mesh
from jax.sharding import PartitionSpec as P

HEADS = 10
HEAD_DIM = 128
CAP = 112
EPS = 1e-06
EP = ("xy", "core")
bf16 = jnp.bfloat16
f32 = jnp.float32


def dot(a, b):
    return jnp.dot(a, b, preferred_element_type=f32)


def ein(spec, a, b):
    return jnp.einsum(spec, a, b, preferred_element_type=f32)


def rope_tables(rows):
    half = HEAD_DIM // 2
    frequency = 10000.0 ** (-np.arange(half) * 2.0 / HEAD_DIM)
    angles = frequency[:, None] * np.arange(rows)[None, :]
    return jnp.asarray(np.cos(angles), f32), jnp.asarray(np.sin(angles), f32)


def rope(v, cosine, sine):
    half = HEAD_DIM // 2
    a, b = v[:, :half], v[:, half:]
    return jnp.concatenate([a * cosine - b * sine, b * cosine + a * sine], axis=1)


def rope_back(v, cosine, sine):
    half = HEAD_DIM // 2
    a, b = v[:, :half], v[:, half:]
    return jnp.concatenate([a * cosine + b * sine, b * cosine - a * sine], axis=1)


VMEM_LIMIT = 60 * 1024 * 1024
PAD = 256


def nn(a, b):
    return lax.dot_general(a, b, (((1,), (0,)), ((), ())), preferred_element_type=f32)


def nt(a, b):
    return lax.dot_general(a, b, (((1,), (1,)), ((), ())), preferred_element_type=f32)


def tn(a, b):
    return lax.dot_general(a, b, (((0,), (0,)), ((), ())), preferred_element_type=f32)


def takes(microseconds):
    return pl.CostEstimate(flops=0, transcendentals=0, bytes_accessed=microseconds * 3_000_000)


def slot_masks(slot_ref, at):
    local, rows = slot_ref.shape[-2:]
    number = lax.broadcasted_iota(jnp.int32, (CAP, rows), 0)
    return [slot_ref[at, e : e + 1, :] == number for e in range(local)]


def spread_kernel(weighted, *refs):
    if weighted:
        rows_ref, slot_ref, router_ref, x_ref, sw_ref, pick = refs
    else:
        rows_ref, slot_ref, x_ref, pick = refs
    local = slot_ref.shape[1]
    rows = rows_ref[...] if weighted else rows_ref[0]
    masks = slot_masks(slot_ref, 0)
    if weighted:
        logits = nt(router_ref[...], rows)
        raised = jnp.exp(logits - jnp.max(logits, axis=0, keepdims=True))
        gates = raised / jnp.sum(raised, axis=0, keepdims=True)
    for e in range(local):
        pick[e * CAP : (e + 1) * CAP, :] = masks[e].astype(f32).astype(bf16)
        if weighted:
            sw_ref[e] = jnp.sum(
                jnp.where(masks[e], gates[e : e + 1, :], 0.0), axis=1, keepdims=True
            )
    product = nn if weighted else nt
    x_ref[...] = product(pick[...], rows).astype(bf16).reshape(x_ref.shape)


def spread(all_rows, slot, router_t=None):
    s, local, rows = slot.shape
    weighted = router_t is not None
    if weighted:
        width = all_rows.shape[1]
        block = pl.BlockSpec((rows, width), lambda i: (i, 0))
    else:
        width = all_rows.shape[1]
        block = pl.BlockSpec((1, width, rows), lambda i: (i, 0, 0))
    in_specs = [
        block,
        pl.BlockSpec((1, local, rows), lambda i: (i, 0, 0)),
    ]
    out_specs = [pl.BlockSpec((1, local, CAP, width), lambda i: (i, 0, 0, 0))]
    out_shape = [jax.ShapeDtypeStruct((s, local, CAP, width), bf16)]
    args = [all_rows, slot]
    if weighted:
        in_specs.append(pl.BlockSpec(router_t.shape, lambda i: (0, 0)))
        out_specs.append(pl.BlockSpec((local, CAP, 1), lambda i: (0, i, 0)))
        out_shape.append(jax.ShapeDtypeStruct((local, s * CAP, 1), f32))
        args.append(router_t)
    out = pl.pallas_call(
        functools.partial(spread_kernel, weighted),
        grid=(s,),
        in_specs=in_specs,
        out_specs=out_specs,
        out_shape=out_shape,
        scratch_shapes=[pltpu.VMEM((local * CAP, rows), bf16)],
        compiler_params=pltpu.CompilerParams(vmem_limit_bytes=VMEM_LIMIT),
        cost_estimate=takes(17),
        name="spread",
    )(*args)
    return out if weighted else out[0]


def padded(ref, out):
    ff = ref.shape[1]
    out[:ff, :] = ref[0]
    out[ff:, :] = jnp.zeros((out.shape[0] - ff, out.shape[1]), out.dtype)


def experts_forward_kernel(
    x_ref, sw_ref, wg_ref, wu_ref, wd_ref, y_ref, gate_ref, up_ref, wg, wu, wd
):
    padded(wg_ref, wg)
    padded(wu_ref, wu)
    padded(wd_ref, wd)
    rows, width = gate_ref.shape[1], x_ref.shape[3]
    x = x_ref[...].reshape(rows, width)
    gate = nt(x, wg[...])
    up = nt(x, wu[...])
    gate_ref[0] = gate
    up_ref[0] = up
    act = gate / (1.0 + jnp.exp(-gate))
    hidden = (act * up).astype(bf16).astype(f32)
    hidden_w = (hidden * sw_ref[0]).astype(bf16)
    y_ref[...] = nn(hidden_w, wd[...]).astype(bf16).reshape(y_ref.shape)


def experts_backward_kernel(
    groups,
    x_ref,
    gx_ref,
    gate_ref,
    up_ref,
    sw_ref,
    wg_ref,
    wu_ref,
    wd_ref,
    dx_ref,
    dg_ref,
    du_ref,
    dd_ref,
    gsw_ref,
    wg,
    wu,
    wd,
):
    padded(wg_ref, wg)
    padded(wu_ref, wu)
    padded(wd_ref, wd)
    rows, width = gate_ref.shape[1], x_ref.shape[3]
    ff = wg_ref.shape[1]
    x = x_ref[...].reshape(rows, width)
    gx = gx_ref[...].reshape(rows, width)
    gate, up, sw = gate_ref[0], up_ref[0], sw_ref[0]
    sig = 1.0 / (1.0 + jnp.exp(-gate))
    act = gate * sig
    hidden = (act * up).astype(bf16).astype(f32)
    gh = nt(gx, wd[...])
    gsw_ref[0] = jnp.sum(gh * hidden, axis=-1, keepdims=True)
    gh = gh * sw
    gg = (gh * up * sig * (1.0 + gate * (1.0 - sig))).astype(bf16)
    gu = (gh * act).astype(bf16)
    sums = (
        (dd_ref, tn((hidden * sw).astype(bf16), gx)[:ff]),
        (dg_ref, tn(gg, x)[:ff]),
        (du_ref, tn(gu, x)[:ff]),
    )
    if groups == 1:
        for ref, value in sums:
            ref[0] = value
    else:

        @pl.when(pl.program_id(1) == 0)
        def _():
            for ref, value in sums:
                ref[0] = value

        @pl.when(pl.program_id(1) > 0)
        def _():
            for ref, value in sums:
                ref[0] += value

    dx_ref[...] = (nn(gg, wg[...]) + nn(gu, wu[...])).astype(bf16).reshape(dx_ref.shape)


def expert_specs(s, width):
    group = min(s, 8)
    slots = pl.BlockSpec((group, 1, CAP, width), lambda i, j: (j, i, 0, 0))
    lines = lambda columns: pl.BlockSpec((1, group * CAP, columns), lambda i, j: (i, j, 0))
    per = lambda *shape: pl.BlockSpec((1, *shape), lambda i, j: (i, 0, 0))
    return s // group, slots, lines, per


def experts_forward(x, sw, wg, wu, wd):
    s, local, cap, width = x.shape
    ff = wg.shape[1]
    rows = s * cap
    groups, slots, lines, per = expert_specs(s, width)
    middle = jax.ShapeDtypeStruct((local, rows, PAD), f32)
    return pl.pallas_call(
        experts_forward_kernel,
        grid=(local, groups),
        in_specs=[slots, lines(1)] + [per(ff, width)] * 3,
        out_specs=[slots, lines(PAD), lines(PAD)],
        out_shape=[jax.ShapeDtypeStruct(x.shape, bf16), middle, middle],
        scratch_shapes=[pltpu.VMEM((PAD, width), bf16)] * 3,
        compiler_params=pltpu.CompilerParams(vmem_limit_bytes=VMEM_LIMIT),
        cost_estimate=takes(31),
        name="experts_forward",
    )(x, sw, wg, wu, wd)


def experts_backward(x, gx, gate, up, sw, wg, wu, wd):
    s, local, cap, width = x.shape
    ff = wg.shape[1]
    rows = s * cap
    groups, slots, lines, per = expert_specs(s, width)
    return pl.pallas_call(
        functools.partial(experts_backward_kernel, groups),
        grid=(local, groups),
        in_specs=[slots, slots, lines(PAD), lines(PAD), lines(1)]
        + [per(ff, width)] * 3,
        out_specs=[slots] + [per(ff, width)] * 3 + [lines(1)],
        out_shape=[jax.ShapeDtypeStruct(x.shape, bf16)]
        + [jax.ShapeDtypeStruct((local, ff, width), f32)] * 3
        + [jax.ShapeDtypeStruct((local, rows, 1), f32)],
        scratch_shapes=[pltpu.VMEM((PAD, width), bf16)] * 3,
        compiler_params=pltpu.CompilerParams(vmem_limit_bytes=VMEM_LIMIT),
        cost_estimate=takes(47),
        name="experts_backward",
    )(x, gx, gate, up, sw, wg, wu, wd)


def collect_kernel(y_ref, slot_ref, out_ref, pick):
    local = slot_ref.shape[1]
    masks = slot_masks(slot_ref, 0)
    for e in range(local):
        pick[e * CAP : (e + 1) * CAP, :] = masks[e].astype(f32).astype(bf16)
    out_ref[0] = tn(pick[...], y_ref[...].reshape(pick.shape[0], -1)).astype(bf16)


def collect_back_kernel(experts, y_ref, slot_ref, gsw_ref, first_ref, out_ref, pick):
    local, rows = slot_ref.shape[1:]
    first = first_ref[0]
    masks = slot_masks(slot_ref, 0)
    number = lax.broadcasted_iota(jnp.int32, (experts, rows), 0)
    probs = jnp.zeros((experts, rows), f32)
    for e in range(local):
        pick[e * CAP : (e + 1) * CAP, :] = masks[e].astype(f32).astype(bf16)
        line = jnp.sum(jnp.where(masks[e], gsw_ref[e], 0.0), axis=0, keepdims=True)
        probs = jnp.where(number == first + e, line, probs)
    out_ref[0, :rows] = tn(pick[...], y_ref[...].reshape(pick.shape[0], -1)).astype(bf16)
    out_ref[0, rows:] = jnp.zeros((experts, out_ref.shape[2]), bf16)
    out_ref[0, rows:, :rows] = probs.astype(bf16)


def collect(y, slot, gsw=None, first=None, experts=0):
    s, local, cap, width = y.shape
    rows = slot.shape[2]
    in_specs = [
        pl.BlockSpec((1, local, cap, width), lambda i: (i, 0, 0, 0)),
        pl.BlockSpec((1, local, rows), lambda i: (i, 0, 0)),
    ]
    args = [y, slot]
    kernel = collect_kernel
    tall = rows
    if gsw is not None:
        in_specs += [
            pl.BlockSpec((local, cap, 1), lambda i: (0, i, 0)),
            pl.BlockSpec(memory_space=pltpu.SMEM),
        ]
        args += [gsw, first.reshape(1)]
        kernel = functools.partial(collect_back_kernel, experts)
        tall = rows + experts
    return pl.pallas_call(
        kernel,
        grid=(s,),
        in_specs=in_specs,
        out_specs=pl.BlockSpec((1, tall, width), lambda i: (i, 0, 0)),
        out_shape=jax.ShapeDtypeStruct((s, tall, width), bf16),
        scratch_shapes=[pltpu.VMEM((local * cap, rows), bf16)],
        compiler_params=pltpu.CompilerParams(vmem_limit_bytes=VMEM_LIMIT),
        cost_estimate=takes(17),
        name="collect",
    )(*args)


MESH = pl.DeviceIdType.MESH
EXTRA = 64


def places():
    chip, core, z = lax.axis_index("xy"), lax.axis_index("core"), lax.axis_index("hs")
    x, y = chip % 2, chip // 2
    return chip, core, z, y * 2 + (1 - x), (1 - y) * 2 + x, (1 - y) * 2 + (1 - x)


def greet(peers):
    barrier = pltpu.get_barrier_semaphore()
    for peer in peers:
        pl.semaphore_signal(barrier, inc=1, device_id=peer, device_id_type=MESH)
    pl.semaphore_wait(barrier, len(peers))


def remote(src, dst, send, recv, peer):
    return pltpu.make_async_remote_copy(
        src_ref=src, dst_ref=dst, send_sem=send, recv_sem=recv, device_id=peer, device_id_type=MESH
    )


def block(q, size):
    return pl.ds(pl.multiple_of(q * size, 16), size)


def weight_sum(grads, given, half, land, out_ref, csend, crecv, send, recv):
    chip, core, z, cx, cy, cd = places()
    other = 1 - core
    c_peer = (chip, other, z)
    chips = (cx, cy, cd)
    count = grads.shape[0] // 2
    piece = count // 4

    to_core = remote(grads.at[block(other, count)], given, csend.at[0], crecv.at[0], c_peer)
    scatter = [
        remote(half.at[block(c, piece)], land.at[i], send.at[i], recv.at[i], (c, core, z))
        for i, c in enumerate(chips)
    ]

    def share():
        to_core.wait_recv()
        half[...] = (grads[block(core, count)].astype(f32) + given[...].astype(f32)).astype(bf16)
        for i in (2, 0, 1):
            scatter[i].start()

    def place(c, k):
        return pl.ds(pl.multiple_of(k * count + c * piece, 16), piece)

    def give(number, c, k, sems, peer):
        return remote(out_ref.at[place(c, k)], out_ref.at[place(c, k)], *sems(number), peer)

    def chip_sems(i):
        return send.at[3 + i], recv.at[3 + i]

    def core_sems(i):
        return csend.at[1 + i], crecv.at[1 + i]

    gather = [give(i, chip, core, chip_sems, (c, core, z)) for i, c in enumerate(chips)]
    over = [give(i, c, core, core_sems, c_peer) for i, c in enumerate((*chips, chip))]

    def give_back():
        done = half[block(chip, piece)].astype(f32)
        for i in range(3):
            scatter[i].wait_recv()
            done = done + land[i].astype(f32)
        out_ref[place(chip, core)] = done.astype(bf16)
        for i in (2, 0, 1):
            gather[i].start()
        over[3].start()

    def end():
        for i, c in enumerate(chips):
            give(i, c, core, chip_sems, (c, core, z)).wait_recv()
            over[i].start()
        for i, c in enumerate((*chips, chip)):
            give(i, c, other, core_sems, c_peer).wait_recv()
        for copy in (to_core, *scatter, *gather, *over):
            copy.wait_send()

    return to_core.start, share, give_back, end


def weight_sum_scratch(tall, width):
    dma = pltpu.SemaphoreType.DMA
    return [
        pltpu.VMEM((tall, width), bf16),
        pltpu.VMEM((tall // 2, width), bf16),
        pltpu.VMEM((tall // 2, width), bf16),
        pltpu.VMEM((3, tall // 8, width), bf16),
        dma((5,)),
        dma((5,)),
        dma((6,)),
        dma((6,)),
    ]


def gather_spread_kernel(
    own_ref, slots_ref, router_ref, x_ref, sw_ref, slot_ref, held, pick, xbuf, send, recv, copied
):
    chip, core, z, cx, cy, cd = places()
    other = 1 - core
    x_peer, y_peer, c_peer = (cx, core, z), (cy, core, z), (chip, other, z)
    tall = held.shape[1]
    half = tall // 2
    local, rows = slot_ref.shape[1:]
    me = chip * 2 + core
    top, low = pl.ds(0, half), pl.ds(half, half)

    def at(c, k):
        return c * 2 + k

    def move(number, src_slot, part, peer):
        return remote(
            held.at[src_slot, part], held.at[src_slot, part], send.at[number], recv.at[number], peer
        )

    whole = pl.ds(0, tall)
    greet([x_peer, y_peer, c_peer])
    held[me, :rows] = own_ref[...]
    held[me, rows:] = jnp.zeros((EXTRA, own_ref.shape[1]), bf16)
    held[me, rows:, :rows] = slots_ref[...]
    x_top, x_low = move(0, me, top, x_peer), move(1, me, low, x_peer)
    y_low, y_top = move(2, me, low, y_peer), move(3, me, top, y_peer)
    to_core = move(4, me, whole, c_peer)
    relay_top, relay_low = move(5, at(cx, core), top, y_peer), move(6, at(cy, core), low, x_peer)
    pass_x, pass_y = move(7, at(cx, core), whole, c_peer), move(8, at(cy, core), whole, c_peer)
    pass_d = move(9, at(cd, core), whole, c_peer)
    for copy in (x_top, y_low, x_low, y_top, to_core):
        copy.start()

    def arrived(number, slot, part):
        move(number, slot, part, c_peer).wait_recv()

    number = lax.broadcasted_iota(jnp.int32, (CAP, rows), 0)
    first = me * local
    line = lax.broadcasted_iota(jnp.int32, (local, EXTRA), 0)
    column = lax.broadcasted_iota(jnp.int32, (local, EXTRA), 1)
    chosen = (column == line + first).astype(f32).astype(bf16)

    def out_copy(t, src):
        return pltpu.make_async_copy(xbuf.at[t % 2], x_ref.at[src], copied.at[t % 2])

    def step(t, carry):
        @pl.when(t == 1)
        def _():
            arrived(4, at(chip, other), whole)

        @pl.when(t == 2)
        def _():
            arrived(0, at(cx, core), top)
            relay_top.start()
            arrived(2, at(cy, core), low)
            relay_low.start()
            arrived(1, at(cx, core), low)
            pass_x.start()

        @pl.when(t == 3)
        def _():
            arrived(3, at(cy, core), top)
            pass_y.start()
            arrived(7, at(cx, other), whole)

        @pl.when(t == 5)
        def _():
            arrived(8, at(cy, other), whole)

        @pl.when(t == 6)
        def _():
            arrived(5, at(cd, core), top)
            arrived(6, at(cd, core), low)
            pass_d.start()

        @pl.when(t == 7)
        def _():
            arrived(9, at(cd, other), whole)

        x, y = (chip % 2 + (t // 2) % 2) % 2, (chip // 2 + t // 4) % 2
        src = (y * 2 + x) * 2 + (core + t % 2) % 2
        slots = nn(chosen, held[src, rows:, :rows]).astype(jnp.int32)
        slot_ref[src] = slots
        logits = nt(router_ref[...], held[src, :rows])
        raised = jnp.exp(logits - jnp.max(logits, axis=0, keepdims=True))
        gates = raised / jnp.sum(raised, axis=0, keepdims=True)
        for e in range(local):
            mask = slots[e : e + 1, :] == number
            pick[e * CAP : (e + 1) * CAP, :] = mask.astype(f32).astype(bf16)
            sw_ref[e, pl.ds(pl.multiple_of(src * CAP, 8), CAP), :] = jnp.sum(
                jnp.where(mask, gates[e : e + 1, :], 0.0), axis=1, keepdims=True
            )

        @pl.when(t >= 2)
        def _():
            out_copy(t, src).wait()

        xbuf[t % 2] = nn(pick[...], held[src, :rows]).astype(bf16).reshape(xbuf.shape[1:])
        out_copy(t, src).start()
        return carry

    lax.fori_loop(0, 8, step, 0)
    out_copy(0, me).wait()
    out_copy(1, me).wait()
    for copy in (x_top, x_low, y_low, y_top, to_core, relay_top, relay_low, pass_x, pass_y, pass_d):
        copy.wait_send()


def gather_spread(own, slots, router_t, local, ep_count):
    rows, width = own.shape
    tall = rows + EXTRA
    vmem = pl.BlockSpec(memory_space=pltpu.VMEM)
    return pl.pallas_call(
        gather_spread_kernel,
        in_specs=[vmem, vmem, vmem],
        out_specs=[pl.BlockSpec(memory_space=pl.ANY), vmem, vmem],
        out_shape=[
            jax.ShapeDtypeStruct((ep_count, local, CAP, width), bf16),
            jax.ShapeDtypeStruct((local, ep_count * CAP, 1), f32),
            jax.ShapeDtypeStruct((ep_count, local, rows), jnp.int32),
        ],
        scratch_shapes=[
            pltpu.VMEM((ep_count, tall, width), bf16),
            pltpu.VMEM((local * CAP, rows), bf16),
            pltpu.VMEM((2, local, CAP, width), bf16),
            pltpu.SemaphoreType.DMA((10,)),
            pltpu.SemaphoreType.DMA((10,)),
            pltpu.SemaphoreType.DMA((2,)),
        ],
        compiler_params=pltpu.CompilerParams(
            vmem_limit_bytes=VMEM_LIMIT, collective_id=0, has_side_effects=True
        ),
        cost_estimate=takes(62),
        name="gather_spread",
    )(own, slots, router_t)


def front_kernel(
    x_ref,
    gain_ref,
    wq_ref,
    wk_ref,
    wv_ref,
    wo_ref,
    ffn_gain_ref,
    doc_ref,
    doc_column_ref,
    cos_ref,
    sin_ref,
    normed1_ref,
    q_ref,
    k_ref,
    v_ref,
    probs_ref,
    attended_ref,
    out_ref,
    residual_ref,
    normed2_ref,
    shared,
    beside,
    esend,
    erecv,
    asend,
    arecv,
    zsend,
    zrecv,
    send,
    recv,
    csend,
    crecv,
):
    chip, core, z, cx, cy, cd = places()
    other = 1 - core
    odd = z % 2
    c_peer = (chip, other, z)
    chips = (cx, cy, cd)
    z_peers = [(chip, core, (z + i) % 4) for i in (1, 2, 3)]
    pair = (chip, core, z + 1 - 2 * odd)
    rows, width = x_ref.shape
    quarter = wq_ref.shape[0]
    whole = HEAD_DIM * (quarter // HEAD_DIM)
    spare = quarter - whole
    greet([c_peer, *[(c, core, z) for c in chips], *z_peers])

    full_rows = pl.ds(pl.multiple_of(odd * spare, 16), whole)
    half_rows = pl.ds(pl.multiple_of((1 - odd) * whole, 16), spare)
    for i, ref in enumerate((wq_ref, wk_ref, wv_ref)):
        shared[i * spare : (i + 1) * spare] = ref[half_rows]
    trade = remote(shared, beside, esend, erecv, pair)
    trade.start()

    share, lanes = quarter // 4, width // 2
    my_lanes = pl.ds(pl.multiple_of(core * lanes, 128), lanes)

    def piece(c):
        return pl.ds(pl.multiple_of(c * share, 16), share)

    out_z = [
        remote(
            wo_ref.at[piece(chip), my_lanes],
            out_ref.at[z, piece(chip), my_lanes],
            zsend.at[i],
            zrecv.at[i],
            peer,
        )
        for i, peer in enumerate(z_peers)
    ]
    for i in (1, 0, 2):
        out_z[i].start()
    behind = [(z + 3 - i) % 4 for i in range(3)]

    def out_chip(i, j, c):
        at = out_ref.at[behind[i], piece(c), my_lanes]
        return remote(at, at, send.at[3 * i + j], recv.at[3 * i + j], (chips[j], core, z))

    def out_core(i, k):
        half = pl.ds(pl.multiple_of(k * lanes, 128), lanes)
        at = out_ref.at[behind[i], :, half]
        return remote(at, at, csend.at[i], crecv.at[i], c_peer)

    x = x_ref[...].astype(f32)
    rms1 = lax.rsqrt(jnp.sum(x * x, axis=-1, keepdims=True) * (1.0 / width) + EPS)
    normed1_ref[...] = (x * rms1 * gain_ref[...]).astype(bf16)
    out_ref[z] = wo_ref[...]

    cosine, sine = cos_ref[...], sin_ref[...]
    half_dim = HEAD_DIM // 2
    scale = 1.0 / math.sqrt(HEAD_DIM)
    row = lax.broadcasted_iota(jnp.int32, (rows, rows), 0)
    column = lax.broadcasted_iota(jnp.int32, (rows, rows), 1)
    allowed = (row >= column) & (doc_column_ref[...] == doc_ref[...])

    def turn(pre):
        a, b = pre[:half_dim], pre[half_dim:]
        return (
            jnp.concatenate([a * cosine - b * sine, b * cosine + a * sine], axis=0).astype(bf16)
        )

    def attend(h):
        scores = jnp.where(allowed, tn(q_ref[h], k_ref[h]) * scale, -1e30)
        raised = jnp.exp(scores - jnp.max(scores, axis=-1, keepdims=True))
        probs = raised * (1.0 / jnp.sum(raised, axis=-1, keepdims=True))
        probs_ref[h] = probs
        return nt(v_ref[h], probs.astype(bf16)).astype(bf16)

    def project(at):
        return [nt(ref[at], normed1_ref[...]) for ref in (wq_ref, wk_ref, wv_ref)]

    q, k, v = project(full_rows)
    heads = whole // HEAD_DIM
    for h in range(heads):
        at = slice(h * HEAD_DIM, (h + 1) * HEAD_DIM)
        q_ref[h], k_ref[h], v_ref[h] = turn(q[at]), turn(k[at]), v[at].astype(bf16)

    def attended_copy(number, start, size):
        at = attended_ref.at[pl.ds(pl.multiple_of(start, 16), size)]
        return lambda i: remote(
            at, at, asend.at[number, i], arecv.at[number, i], z_peers[i]
        )

    mine = z * quarter
    copies = []
    for h in range(heads):
        start = mine + odd * spare + h * HEAD_DIM
        attended_ref[pl.ds(pl.multiple_of(start, 16), HEAD_DIM)] = attend(h)
        copy = attended_copy(h, start, HEAD_DIM)
        copies += [copy(1), copy(0), copy(2)]
        for one in copies[-3:]:
            one.start()
        if h == 0:
            for i in range(3):
                out_z[i].wait_recv()
                for j in (2, 0, 1):
                    out_chip(i, j, chip).start()

    trade.wait_recv()
    for i, (ref, to) in enumerate(((wq_ref, q_ref), (wk_ref, k_ref), (wv_ref, v_ref))):
        normed1 = normed1_ref[...]
        here = nt(ref[half_rows], normed1)
        there = nt(beside[i * spare : (i + 1) * spare], normed1)
        first = jnp.where(odd == 1, there, here)
        second = jnp.where(odd == 1, here, there)
        both = jnp.concatenate([first, second], axis=0)
        to[heads] = both.astype(bf16) if to is v_ref else turn(both)
    last = attend(heads)
    last = jnp.where(odd == 1, last[spare:], last[:spare])
    start = mine + (1 - odd) * whole
    attended_ref[pl.ds(pl.multiple_of(start, 16), spare)] = last
    copy = attended_copy(heads, start, spare)
    copies += [copy(1), copy(0), copy(2)]
    for one in copies[-3:]:
        one.start()

    for i in range(3):
        for j in range(3):
            out_chip(i, j, chips[j]).wait_recv()
        out_core(i, core).start()
    for i in range(3):
        from_z = (z + 3 - i) % 4
        from_odd = from_z % 2
        for h in range(heads):
            attended_copy(h, from_z * quarter + from_odd * spare + h * HEAD_DIM, HEAD_DIM)(i).wait_recv()
        attended_copy(heads, from_z * quarter + (1 - from_odd) * whole, spare)(i).wait_recv()
        out_core(i, other).wait_recv()
    attended = attended_ref[...].T
    residual = x_ref[...].astype(f32) + nt(attended, out_ref[...].reshape(width, width))
    residual_ref[...] = residual
    rms2 = lax.rsqrt(jnp.sum(residual * residual, axis=-1, keepdims=True) * (1.0 / width) + EPS)
    normed2_ref[...] = (residual * rms2 * ffn_gain_ref[...]).astype(bf16)
    for one in (trade, *out_z, *copies):
        one.wait_send()
    for i in range(3):
        for j in range(3):
            out_chip(i, j, chip).wait_send()
        out_core(i, core).wait_send()


def front(x, gain, wq, wk, wv, wo, ffn_gain, doc, tables):
    rows, width = x.shape
    quarter = wq.shape[0]
    heads = -(-quarter // HEAD_DIM)
    spare = quarter % HEAD_DIM
    vmem = pl.BlockSpec(memory_space=pltpu.VMEM)
    dma = pltpu.SemaphoreType.DMA
    low = lambda *shape: jax.ShapeDtypeStruct(shape, bf16)
    return pl.pallas_call(
        front_kernel,
        in_specs=[vmem] * 11,
        out_specs=[vmem] * 9,
        out_shape=[
            low(rows, width),
            *[low(heads, HEAD_DIM, rows)] * 3,
            jax.ShapeDtypeStruct((heads, rows, rows), f32),
            low(width, rows),
            low(4, quarter, width),
            jax.ShapeDtypeStruct((rows, width), f32),
            low(rows, width),
        ],
        scratch_shapes=[
            pltpu.VMEM((3 * spare, width), bf16),
            pltpu.VMEM((3 * spare, width), bf16),
            dma,
            dma,
            dma((heads, 3)),
            dma((heads, 3)),
            dma((3,)),
            dma((3,)),
            dma((9,)),
            dma((9,)),
            dma((3,)),
            dma((3,)),
        ],
        compiler_params=pltpu.CompilerParams(
            vmem_limit_bytes=VMEM_LIMIT, collective_id=1, has_side_effects=True
        ),
        cost_estimate=takes(50),
        name="front",
    )(x, gain[None, :], wq, wk, wv, wo, ffn_gain[None, :], doc, doc.T, *tables)


def collect_sum_kernel(
    y_ref,
    slot_ref,
    gsw_ref,
    mine_ref,
    shared_gate_ref,
    shared_up_ref,
    shared_down_ref,
    forward_ref,
    out_ref,
    sum_ref,
    passed_ref,
    pick,
    ybuf,
    stage,
    given,
    sums,
    relay,
    land,
    zland,
    total,
    copied,
    core_send,
    core_recv,
    send,
    recv,
    zsend,
    zrecv,
    grads,
    *more,
):
    chip, core, z, cx, cy, cd = places()
    other = 1 - core
    x_peer, y_peer, c_peer = (cx, core, z), (cy, core, z), (chip, other, z)
    z_peers = [(chip, core, (z + i) % 4) for i in (1, 2, 3)]
    local, rows = slot_ref.shape[1:]
    tall = out_ref.shape[0]
    me = chip * 2 + core
    number = lax.broadcasted_iota(jnp.int32, (CAP, rows), 0)
    row = lax.broadcasted_iota(jnp.int32, (EXTRA, rows), 0)

    greet([x_peer, y_peer, c_peer, (cd, core, z), *z_peers])

    def sequence(t):
        p = t // 2
        x, y = (chip % 2 + 1 + p // 2) % 2, (chip // 2 + 1 + p % 2) % 2
        return (y * 2 + x) * 2 + (core + 1 + t % 2) % 2

    def in_copy(t):
        return pltpu.make_async_copy(y_ref.at[sequence(t)], ybuf.at[t % 2], copied.at[t % 2])

    def to_core(p):
        return remote(stage.at[p], given.at[p], core_send.at[p], core_recv.at[p], c_peer)

    units = 3
    unit = tall // units
    half, part = unit // 2, unit // 4

    def top(u):
        return pl.ds(u * unit, half)

    def low(u):
        return pl.ds(u * unit + half, half)

    def over(u, number, src, dst, peer):
        return remote(src, dst, send.at[u, number], recv.at[u, number], peer)

    far_top = [over(u, 0, sums.at[0, top(u)], relay.at[u, 0], x_peer) for u in range(units)]
    far_low = [over(u, 1, sums.at[0, low(u)], relay.at[u, 1], y_peer) for u in range(units)]
    x_top = [over(u, 2, sums.at[1, top(u)], land.at[0, top(u)], x_peer) for u in range(units)]
    x_low = [over(u, 3, sums.at[1, low(u)], land.at[0, low(u)], x_peer) for u in range(units)]
    y_low = [over(u, 4, sums.at[2, low(u)], land.at[1, low(u)], y_peer) for u in range(units)]
    y_top = [over(u, 5, sums.at[2, top(u)], land.at[1, top(u)], y_peer) for u in range(units)]

    in_copy(0).start()
    passed_ref[...] = forward_ref[...]
    start, share, give_back, end = weight_sum(grads, *more[:3], sum_ref, *more[3:])
    at = 0
    for ref in (shared_gate_ref, shared_up_ref, shared_down_ref):
        grads[at : at + ref.shape[0]] = ref[...]
        at += ref.shape[0]
    grads[at:] = jnp.zeros((grads.shape[0] - at, grads.shape[1]), bf16)
    start()

    def step(t, carry):
        @pl.when(t < 7)
        def _():
            in_copy(t + 1).start()

        p, s = t // 2, sequence(t)
        probs = jnp.zeros((EXTRA, rows), f32)
        for e in range(local):
            mask = slot_ref[s, e : e + 1, :] == number
            pick[e * CAP : (e + 1) * CAP, :] = mask.astype(f32).astype(bf16)
            column = gsw_ref[e, pl.ds(pl.multiple_of(s * CAP, 8), CAP), :]
            line = jnp.sum(jnp.where(mask, column, 0.0), axis=0, keepdims=True)
            probs = jnp.where(row == me * local + e, line, probs)
        in_copy(t).wait()
        back = tn(pick[...], ybuf[t % 2].reshape(local * CAP, -1))

        @pl.when(t % 2 == 0)
        def _():
            stage[p, :rows] = back.astype(bf16)
            stage[p, rows:] = jnp.zeros((tall - rows, back.shape[1]), bf16)
            stage[p, rows:, :rows] = probs.astype(bf16)
            to_core(p).start()

        @pl.when(t % 2 == 1)
        def _():
            to_core(p).wait_recv()
            sums[p, :rows] = (back + given[p, :rows].astype(f32)).astype(bf16)
            sums[p, rows:] = given[p, rows:]
            sums[p, rows:, :rows] = (probs + given[p, rows:, :rows].astype(f32)).astype(bf16)

        @pl.when(t == 1)
        def _():
            far_top[0].start()
            far_low[0].start()

        @pl.when(t == 3)
        def _():
            x_top[0].start()

        @pl.when(t == 5)
        def _():
            y_low[0].start()
            far_top[1].start()
            far_low[1].start()

        return carry

    lax.fori_loop(0, 8, step, 0)
    def relayed(u):
        far_low[u].wait_recv()
        at = slice(u * unit + half, (u + 1) * unit)
        sums[1, at] = (sums[1, at].astype(f32) + relay[u, 1].astype(f32)).astype(bf16)
        x_low[u].start()
        far_top[u].wait_recv()
        at = slice(u * unit, u * unit + half)
        sums[2, at] = (sums[2, at].astype(f32) + relay[u, 0].astype(f32)).astype(bf16)
        y_top[u].start()

    def block_of(u, q):
        return pl.ds(pl.multiple_of(u * unit + q * part, 16), part)

    def z_sems(u, number):
        return zsend.at[u, number], zrecv.at[u, number]

    scatter = [
        [
            remote(
                total.at[block_of(u, (z + i) % 4)],
                zland.at[u, i - 1],
                *z_sems(u, i - 1),
                z_peers[i - 1],
            )
            for i in (1, 2, 3)
        ]
        for u in range(units)
    ]

    def back_copy(u, q, i):
        at = out_ref.at[block_of(u, q)]
        return remote(at, at, *z_sems(u, 2 + i), z_peers[i - 1])

    def landed(u):
        for copy in (x_top[u], y_top[u], x_low[u], y_low[u]):
            copy.wait_recv()
        at = slice(u * unit, (u + 1) * unit)
        added = sums[3, at].astype(f32) + land[0, at].astype(f32) + land[1, at].astype(f32)
        ours = min(rows, (u + 1) * unit) - u * unit
        if ours == unit:
            total[at] = (added + mine_ref[at].astype(f32)).astype(bf16)
        else:
            here = slice(u * unit, u * unit + ours)
            total[here] = (added[:ours] + mine_ref[here].astype(f32)).astype(bf16)
            total[u * unit + ours : (u + 1) * unit] = added[ours:].astype(bf16)
        for i in (1, 0, 2):
            scatter[u][i].start()

    def summed(u):
        done = total[block_of(u, z)].astype(f32)
        for i in range(3):
            scatter[u][i].wait_recv()
            done = done + zland[u, i].astype(f32)
        out_ref[block_of(u, z)] = done.astype(bf16)
        for i in (2, 1, 3):
            back_copy(u, z, i).start()

    relayed(0)
    x_top[1].start()
    y_low[1].start()
    far_top[2].start()
    far_low[2].start()
    relayed(1)
    x_top[2].start()
    y_low[2].start()
    landed(0)
    relayed(2)
    share()
    landed(1)
    summed(0)
    landed(2)
    summed(1)
    give_back()
    summed(2)
    end()
    for u in range(units):
        for i in (1, 2, 3):
            back_copy(u, (z + 4 - i) % 4, i).wait_recv()
    for u in range(units):
        for copy in (far_top[u], far_low[u], x_top[u], x_low[u], y_low[u], y_top[u], *scatter[u]):
            copy.wait_send()
        for i in (1, 2, 3):
            back_copy(u, z, i).wait_send()
    for p in range(4):
        to_core(p).wait_send()


def collect_sum(y, slot, gsw, mine, forward, *shared):
    s, local, cap, width = y.shape
    rows = slot.shape[2]
    tall = rows + EXTRA
    dma = pltpu.SemaphoreType.DMA
    weights = 128 * (-(-sum(a.shape[0] for a in shared) // 128))
    vmem = pl.BlockSpec(memory_space=pltpu.VMEM)
    return pl.pallas_call(
        collect_sum_kernel,
        in_specs=[pl.BlockSpec(memory_space=pl.ANY)] + [vmem] * 7,
        out_specs=[vmem, vmem, vmem],
        out_shape=[
            jax.ShapeDtypeStruct((tall, width), bf16),
            jax.ShapeDtypeStruct((weights, width), bf16),
            jax.ShapeDtypeStruct(forward.shape, bf16),
        ],
        scratch_shapes=[
            pltpu.VMEM((local * cap, rows), bf16),
            pltpu.VMEM((2, local, cap, width), bf16),
            pltpu.VMEM((4, tall, width), bf16),
            pltpu.VMEM((4, tall, width), bf16),
            pltpu.VMEM((4, tall, width), bf16),
            pltpu.VMEM((3, 2, tall // 6, width), bf16),
            pltpu.VMEM((2, tall, width), bf16),
            pltpu.VMEM((3, 3, tall // 12, width), bf16),
            pltpu.VMEM((tall, width), bf16),
            dma((2,)),
            dma((4,)),
            dma((4,)),
            dma((3, 6)),
            dma((3, 6)),
            dma((3, 6)),
            dma((3, 6)),
            *weight_sum_scratch(weights, width),
        ],
        compiler_params=pltpu.CompilerParams(
            vmem_limit_bytes=VMEM_LIMIT, collective_id=2, has_side_effects=True
        ),
        cost_estimate=takes(131),
        name="collect_sum",
    )(y, slot, gsw, mine, *shared, forward)


def back_kernel(
    sums_ref,
    residual_ref,
    normed2_ref,
    grad_ref,
    router_ref,
    ffn_gain_ref,
    out_ref,
    q_ref,
    k_ref,
    v_ref,
    probs_ref,
    cos_ref,
    sin_ref,
    wq_ref,
    wk_ref,
    wv_ref,
    normed_ref,
    attended_ref,
    x_ref,
    gain_ref,
    tokens_ref,
    early_ref,
    late_ref,
    dq_ref,
    dk_ref,
    dv_ref,
    back_t,
    low_t,
    part,
    low_part,
    zland,
    mine,
    theirs,
    zsend,
    zrecv,
    lsend,
    lrecv,
    *more,
):
    chip, core, z, cx, cy, cd = places()
    odd = z % 2
    c_peer = (chip, 1 - core, z)
    z_peers = [(chip, core, (z + i) % 4) for i in (1, 2, 3)]
    quarter, width = wq_ref.shape
    rows = x_ref.shape[1]
    early, late = more[0], more[8]
    experts = router_ref.shape[0]
    whole = HEAD_DIM * (quarter // HEAD_DIM)
    spare = quarter - whole
    heads = whole // HEAD_DIM
    greet([c_peer, *[(c, core, z) for c in (cx, cy, cd)], *z_peers])

    logits = nt(router_ref[...], normed2_ref[...])
    raised = jnp.exp(logits - jnp.max(logits, axis=0, keepdims=True))
    gates = raised / jnp.sum(raised, axis=0, keepdims=True)
    grad_probs = sums_ref[rows:, :rows].astype(f32)
    grad_logits = gates * (grad_probs - jnp.sum(grad_probs * gates, axis=0, keepdims=True))
    grad_logits = grad_logits.astype(bf16)
    grad_router = nn(grad_logits, normed2_ref[...])
    grad_normed2 = sums_ref[:rows].astype(f32) + tn(grad_logits, router_ref[...])
    residual = residual_ref[...]
    rms2 = lax.rsqrt(jnp.sum(residual * residual, axis=-1, keepdims=True) * (1.0 / width) + EPS)
    grad_ffn = jnp.sum(grad_normed2 * residual * rms2, axis=0, keepdims=True)
    u = grad_normed2 * ffn_gain_ref[...]
    mean2 = jnp.sum(u * residual, axis=-1, keepdims=True) * (1.0 / width)
    added = rms2 * u - residual * (rms2 * rms2 * rms2 * mean2)
    back_t[...] = added.T + grad_ref[...].astype(f32)
    low_t[...] = back_t[...].astype(bf16)
    own = block(z, quarter)
    early[:quarter] = nt(low_t[own], attended_ref[...]).astype(bf16)
    early[quarter:] = grad_router.astype(bf16)
    start, share, give_back, end = weight_sum(early, *more[1:4], early_ref, *more[4:8])
    start()

    cosine, sine = cos_ref[...], sin_ref[...]
    half_dim = HEAD_DIM // 2
    scale = 1.0 / math.sqrt(HEAD_DIM)

    def turn_back(v):
        a, b = v[:half_dim] * scale, v[half_dim:] * scale
        turned = [a * cosine + b * sine, b * cosine - a * sine]
        return jnp.concatenate(turned, axis=0).astype(bf16)

    first_lane = z * quarter + odd * spare
    shared_lane = z * quarter + (1 - odd) * whole - odd * spare
    for h in range(heads + 1):
        lane = first_lane + h * HEAD_DIM if h < heads else shared_lane
        lane = pl.ds(pl.multiple_of(lane, HEAD_DIM), HEAD_DIM)
        grad_attended = tn(out_ref[:, lane], low_t[...]).astype(bf16)
        probs = probs_ref[h]
        grad_p = tn(grad_attended, v_ref[h])
        grad_v = nn(grad_attended, probs.astype(bf16)).astype(bf16)
        delta = jnp.sum(probs * grad_p, axis=-1, keepdims=True)
        grad_s = (probs * (grad_p - delta)).astype(bf16)
        grad_q = turn_back(nt(k_ref[h], grad_s))
        grad_k = turn_back(nn(q_ref[h], grad_s))
        for ref, value in ((dq_ref, grad_q), (dk_ref, grad_k), (dv_ref, grad_v)):
            if h < heads:
                at = pl.ds(pl.multiple_of(odd * spare + h * HEAD_DIM, 16), HEAD_DIM)
                ref[at] = value
            else:
                at = pl.ds(pl.multiple_of((1 - odd) * whole, 16), spare)
                ref[at] = jnp.where(odd == 1, value[spare:], value[:spare])
        if h == 0:
            share()

    x_all = x_ref[...].astype(f32)
    rms1 = lax.rsqrt(jnp.sum(x_all * x_all, axis=0, keepdims=True) * (1.0 / width) + EPS)
    part[...] = tn(wq_ref[...], dq_ref[...])
    part[...] += tn(wk_ref[...], dk_ref[...])
    part[...] += tn(wv_ref[...], dv_ref[...])
    low_part[...] = part[...].astype(bf16)
    to_z = [
        remote(
            low_part.at[block((z + i) % 4, quarter)],
            zland.at[i - 1],
            zsend.at[i - 1],
            zrecv.at[i - 1],
            z_peers[i - 1],
        )
        for i in (1, 2, 3)
    ]
    few_to_z = [
        remote(mine, theirs.at[i], lsend.at[i], lrecv.at[i], peer) for i, peer in enumerate(z_peers)
    ]
    along = part[...] * x_ref[...].astype(f32)
    mine[...] = jnp.zeros(mine.shape, f32)
    mine[0:1, :rows] = jnp.sum(along * gain_ref[...], axis=0, keepdims=True)
    mine[:, rows:] = nt(jnp.ones((8, rows), bf16), (along * rms1).astype(bf16))
    for copy in few_to_z:
        copy.start()
    for i in (1, 0, 2):
        to_z[i].start()

    give_back()
    normed = normed_ref[...]
    for i, ref in enumerate((dq_ref, dk_ref, dv_ref)):
        late[i * quarter : (i + 1) * quarter] = nn(ref[...], normed).astype(bf16)
    at = 3 * quarter
    for copy in few_to_z:
        copy.wait_recv()
    few = mine[...] + theirs[0] + theirs[1] + theirs[2]
    late[at:] = jnp.zeros((late.shape[0] - at, width), bf16)
    line = lax.broadcasted_iota(jnp.int32, (16, width), 0)
    gains = jnp.where(line == 0, few[0:1, rows:], jnp.where(line == 1, grad_ffn, 0.0))
    late[at : at + 16] = gains.astype(bf16)

    start, share, give_back, end_late = weight_sum(late, *more[9:12], late_ref, *more[12:16])
    start()
    share()

    total = part[own]
    for i in range(3):
        to_z[i].wait_recv()
        total = total + zland[i].astype(f32)
    x = x_ref[own].astype(f32)
    mean = few[0:1, :rows] * (1.0 / width)
    tokens_ref[...] = back_t[own] + rms1 * gain_ref[own] * total - x * (rms1 * rms1 * rms1 * mean)

    give_back()
    end()
    end_late()
    for copy in (*to_z, *few_to_z):
        copy.wait_send()


def back(*args):
    quarter, width = args[13].shape
    rows = args[1].shape[0]
    early, late = quarter + args[4].shape[0], 128 * (3 * quarter // 128 + 1)
    vmem = pl.BlockSpec(memory_space=pltpu.VMEM)
    dma = pltpu.SemaphoreType.DMA
    return pl.pallas_call(
        back_kernel,
        in_specs=[vmem] * len(args),
        out_specs=[vmem] * 3,
        out_shape=[
            jax.ShapeDtypeStruct((quarter, rows), f32),
            jax.ShapeDtypeStruct((early, width), bf16),
            jax.ShapeDtypeStruct((late, width), bf16),
        ],
        scratch_shapes=[
            *[pltpu.VMEM((quarter, rows), bf16)] * 3,
            pltpu.VMEM((width, rows), f32),
            pltpu.VMEM((width, rows), bf16),
            pltpu.VMEM((width, rows), f32),
            pltpu.VMEM((width, rows), bf16),
            pltpu.VMEM((3, quarter, rows), bf16),
            pltpu.VMEM((8, rows + width), f32),
            pltpu.VMEM((3, 8, rows + width), f32),
            dma((3,)),
            dma((3,)),
            dma((3,)),
            dma((3,)),
            *weight_sum_scratch(early, width),
            *weight_sum_scratch(late, width),
        ],
        compiler_params=pltpu.CompilerParams(
            vmem_limit_bytes=VMEM_LIMIT, collective_id=3, has_side_effects=True
        ),
        cost_estimate=takes(90),
        name="back",
    )(*args)


def widen_kernel(early_ref, late_ref, shared_ref, *out_refs):
    quarter = out_refs[0].shape[0]
    for i in range(3):
        out_refs[i][...] = late_ref[i * quarter : (i + 1) * quarter].astype(f32)
    out_refs[3][...] = early_ref[:quarter].astype(f32)
    out_refs[4][...] = early_ref[quarter:].astype(f32)
    out_refs[5][...] = late_ref[3 * quarter : 3 * quarter + 8].astype(f32)
    size = out_refs[6].shape[0]
    for i in range(3):
        out_refs[6 + i][...] = shared_ref[i * size : (i + 1) * size].astype(f32)


def widen(early, late, shared, quarter, hidden_units):
    width = early.shape[1]
    step = width // 5
    tall = [quarter] * 4 + [early.shape[0] - quarter, 8] + [hidden_units] * 3
    blocks = lambda lines: pl.BlockSpec((lines, step), lambda i: (0, i))
    return pl.pallas_call(
        widen_kernel,
        grid=(width // step,),
        in_specs=[blocks(a.shape[0]) for a in (early, late, shared)],
        out_specs=[blocks(lines) for lines in tall],
        out_shape=[jax.ShapeDtypeStruct((lines, width), f32) for lines in tall],
        compiler_params=pltpu.CompilerParams(vmem_limit_bytes=VMEM_LIMIT),
        cost_estimate=takes(8),
        name="widen",
    )(early, late, shared)


def plain_front(
    tokens, attn_gain, query_t, key_t, value_t, attn_out, ffn_gain, documents, tables
):
    rows, width = tokens.shape
    quarter = query_t.shape[0]
    hs, hs_count = lax.axis_index("hs"), lax.axis_size("hs")
    odd = (hs % 2) == 1
    spare = -quarter % HEAD_DIM
    heads = (quarter + spare) // HEAD_DIM

    def outer(w):
        return jnp.where(odd, w[:spare], w[quarter - spare :])

    sent = jnp.concatenate([outer(query_t), outer(key_t), outer(value_t)], axis=0)
    got = lax.ppermute(sent, "hs", [(i, i ^ 1) for i in range(hs_count)])

    def widened(w, extra):
        return jnp.where(
            odd, jnp.concatenate([extra, w], axis=0), jnp.concatenate([w, extra], axis=0)
        )

    x = tokens.astype(f32)
    rms1 = lax.rsqrt(jnp.mean(x * x, axis=-1, keepdims=True) + EPS)
    normed1 = (x * rms1 * attn_gain).astype(bf16)
    shape3 = (heads, HEAD_DIM, rows)
    q, k, v = [
        ein("cd,td->ct", widened(w, got[i * spare : (i + 1) * spare]), normed1).reshape(shape3)
        for i, w in enumerate((query_t, key_t, value_t))
    ]
    q, k, v = rope(q, *tables).astype(bf16), rope(k, *tables).astype(bf16), v.astype(bf16)
    positions = jnp.arange(rows, dtype=jnp.int32)
    doc = documents[0]
    allowed = (positions[:, None] >= positions[None, :]) & (doc[:, None] == doc[None, :])
    scale = 1.0 / math.sqrt(HEAD_DIM)
    scores = jnp.where(allowed[None], ein("hdq,hdk->hqk", q, k) * scale, -1e30)
    raised = jnp.exp(scores - jnp.max(scores, axis=-1, keepdims=True))
    probs = raised / jnp.sum(raised, axis=-1, keepdims=True)
    attended = ein("hdk,hqk->hdq", v, probs.astype(bf16)).astype(bf16).reshape(-1, rows)
    attended = jnp.where(odd, attended[spare:], attended[:quarter])
    attended_t = lax.all_gather(attended, "hs", axis=0, tiled=True)
    out_t = lax.all_gather(attn_out.T, "hs", axis=0, tiled=True)
    residual = x + ein("ct,oc->to", attended_t, out_t)
    rms2 = lax.rsqrt(jnp.mean(residual * residual, axis=-1, keepdims=True) + EPS)
    normed2 = (residual * rms2 * ffn_gain).astype(bf16)
    return normed1, q, k, v, probs, attended_t, out_t, residual, normed2


def over_ep(a):
    return lax.psum(a.astype(bf16), EP).astype(f32)


def plain_back(
    sums,
    residual,
    normed2,
    grad_t,
    router_t,
    ffn_gain,
    out_t,
    q,
    k,
    v,
    probs,
    tables,
    query_t,
    key_t,
    value_t,
    normed1,
    attended_t,
    tokens,
    attn_gain,
):
    rows, width = tokens.shape
    quarter = query_t.shape[0]
    hs = lax.axis_index("hs")
    odd = (hs % 2) == 1
    spare = -quarter % HEAD_DIM
    held = quarter + spare
    col0 = hs * quarter

    def own(v):
        v = v.astype(bf16).reshape(held, rows)
        return jnp.where(odd, v[spare:], v[:quarter])

    gates = jax.nn.softmax(nt(normed2, router_t), axis=-1)
    grad_probs = sums[rows:, :rows].T.astype(f32)
    grad_logits = (
        gates * (grad_probs - jnp.sum(grad_probs * gates, axis=-1, keepdims=True))
    ).astype(bf16)
    grad_router = tn(grad_logits, normed2)
    grad_normed2 = sums[:rows].astype(f32) + dot(grad_logits, router_t)
    rms2 = lax.rsqrt(jnp.mean(residual * residual, axis=-1, keepdims=True) + EPS)
    grad_ffn_gain = jnp.sum(grad_normed2 * residual * rms2, axis=0)
    u = grad_normed2 * ffn_gain
    grad_residual = (
        grad_t.T.astype(f32)
        + rms2 * u
        - residual * rms2**3 * jnp.mean(u * residual, axis=-1, keepdims=True)
    )
    back_t = grad_residual.T
    low_t = back_t.astype(bf16)
    out_held = lax.dynamic_slice_in_dim(out_t, jnp.where(odd, col0 - spare, col0), held, 1)
    grad_attended = tn(out_held, low_t).astype(bf16).reshape(-1, HEAD_DIM, rows)
    grad_p = ein("hdq,hdk->hqk", grad_attended, v)
    grad_v = own(ein("hdq,hqk->hdk", grad_attended, probs.astype(bf16)))
    grad_s = (probs * (grad_p - jnp.sum(probs * grad_p, axis=-1, keepdims=True))).astype(bf16)
    scale = 1.0 / math.sqrt(HEAD_DIM)
    grad_q = own(rope_back(ein("hdk,hqk->hdq", k, grad_s) * scale, *tables))
    grad_k = own(rope_back(ein("hdq,hqk->hdk", q, grad_s) * scale, *tables))
    own_rows = lambda a: lax.dynamic_slice_in_dim(a, col0, quarter, 0)
    heads_sums = [
        over_ep(dot(grad_q, normed1)),
        over_ep(dot(grad_k, normed1)),
        over_ep(dot(grad_v, normed1)),
        over_ep(nt(own_rows(low_t), attended_t)),
    ]
    part = tn(query_t, grad_q) + tn(key_t, grad_k) + tn(value_t, grad_v)
    grad_n1 = lax.psum_scatter(part.astype(bf16), "hs", scatter_dimension=0, tiled=True)
    grad_n1 = grad_n1.astype(f32)
    x = tokens.T.astype(f32)
    x_own = own_rows(x)
    rms_t = lax.rsqrt(jnp.mean(x * x, axis=0, keepdims=True) + EPS)
    w1 = grad_n1 * own_rows(attn_gain)[:, None]
    mean1 = lax.psum(jnp.sum(w1 * x_own, axis=0, keepdims=True), "hs") / width
    grad_tokens = own_rows(back_t) + rms_t * w1 - x_own * rms_t**3 * mean1
    gain_own = jnp.sum(grad_n1 * x_own * rms_t, axis=1)
    gain_part = lax.dynamic_update_slice_in_dim(jnp.zeros((width,), f32), gain_own, col0, 0)
    grad_attn_gain = lax.psum(gain_part, (*EP, "hs"))
    return (
        grad_tokens,
        heads_sums,
        over_ep(grad_router),
        grad_attn_gain,
        lax.psum(grad_ffn_gain, EP),
    )


def shards(
    tokens,
    attn_gain,
    attn_query,
    attn_key,
    attn_value,
    attn_out,
    ffn_gain,
    router,
    shared_gate,
    shared_up,
    shared_down,
    expert_gate,
    expert_up,
    expert_down,
    routes,
    documents,
    out_grad,
):
    rows, width = tokens.shape
    quarter = out_grad.shape[1]
    hs = lax.axis_index("hs")
    ep_count = lax.axis_size("xy") * lax.axis_size("core")
    ep = lax.axis_index("xy") * lax.axis_size("core") + lax.axis_index("core")
    local = expert_gate.shape[0]
    experts = router.shape[1]
    small = ep_count == 8 and lax.axis_size("hs") == 4

    query_t, key_t, value_t, router_t = attn_query.T, attn_key.T, attn_value.T, router.T
    grad_all_t = lax.all_gather(out_grad.T, (*EP, "hs"), axis=0, tiled=True)
    grad_all_t = grad_all_t.reshape(ep_count, width, rows)
    grad_t = lax.dynamic_index_in_dim(grad_all_t, ep, 0, keepdims=False)
    positions = jnp.arange(rows, dtype=jnp.int32)
    below = (positions[:, None] > positions[None, :]).astype(bf16)
    chosen = jnp.any(
        routes[:, :, None] == jnp.arange(experts, dtype=jnp.int32)[None, None, :], axis=1
    )
    own_slots = jnp.where(chosen, dot(below, chosen.astype(bf16)), -1.0).T.astype(bf16)
    tables = rope_tables(rows)

    if small:
        ahead = front(
            tokens, attn_gain, query_t, key_t, value_t, attn_out.T, ffn_gain, documents, tables
        )
    else:
        ahead = plain_front(
            tokens, attn_gain, query_t, key_t, value_t, attn_out, ffn_gain, documents, tables
        )
    normed1, q, k, v, probs, attended_t, out_t, residual, normed2 = ahead
    out_t = out_t.reshape(width, width)

    sh_gate = dot(normed2, shared_gate)
    sh_up = dot(normed2, shared_up)
    sh_sig = jax.nn.sigmoid(sh_gate)
    sh_act = sh_gate * sh_sig
    sh_hidden = (sh_act * sh_up).astype(bf16)
    shared_part = dot(sh_hidden, shared_down)
    grad_sh = ein("dt,fd->tf", grad_t, shared_down)
    grad_sh_gate = (grad_sh * sh_up * sh_sig * (1 + sh_gate * (1 - sh_sig))).astype(bf16)
    grad_sh_up = (grad_sh * sh_act).astype(bf16)
    shared_grads = [
        ein("tf,td->fd", grad_sh_gate, normed2).astype(bf16),
        ein("tf,td->fd", grad_sh_up, normed2).astype(bf16),
        ein("tf,dt->fd", sh_hidden, grad_t).astype(bf16),
    ]
    shared_back = ein("tf,df->td", grad_sh_gate, shared_gate) + ein(
        "tf,df->td", grad_sh_up, shared_up
    )

    first = ep * local
    rolled = jnp.roll(router_t, -first, axis=0)
    if small:
        ex_in, slot_weight, slot = gather_spread(normed2, own_slots, rolled, local, ep_count)
    else:
        slot = lax.dynamic_slice_in_dim(
            lax.all_gather(own_slots, EP, axis=0), first, local, 1
        ).astype(jnp.int32)
        normed_all = lax.all_gather(normed2, EP, axis=0, tiled=True)
        ex_in, slot_weight = spread(normed_all, slot, rolled)
    gate_t, up_t = expert_gate.swapaxes(1, 2), expert_up.swapaxes(1, 2)
    ex_grad = spread(grad_all_t, slot)
    ex_out, ex_gate, ex_up = experts_forward(ex_in, slot_weight, gate_t, up_t, expert_down)
    out_part = collect(ex_out, slot).reshape(ep_count * rows, width)
    ex_back, grad_gate_t, grad_up_t, grad_expert_down, grad_slot_weight = experts_backward(
        ex_in, ex_grad, ex_gate, ex_up, slot_weight, gate_t, up_t, expert_down
    )

    if small:
        back_sums, shared_sums, shared_part = collect_sum(
            ex_back, slot, grad_slot_weight, shared_back.astype(bf16), shared_part.astype(bf16), *shared_grads
        )
        grad_tokens, early, late = back(
            back_sums,
            residual,
            normed2,
            grad_t,
            router_t,
            ffn_gain[None, :],
            out_t,
            q,
            k,
            v,
            probs,
            *tables,
            query_t,
            key_t,
            value_t,
            normed1,
            attended_t,
            tokens.T,
            attn_gain[:, None],
        )
        *heads_sums, grad_router, gains, sum_gate, sum_up, sum_down = widen(
            early, late, shared_sums, quarter, shared_down.shape[0]
        )
        shared_sums = sum_gate, sum_up, sum_down
        grad_attn_gain, grad_ffn_gain = gains[0], gains[1]
    else:
        back_part = collect(ex_back, slot, grad_slot_weight, first, experts).reshape(-1, width)
        back_rows = lax.psum_scatter(back_part, EP, scatter_dimension=0, tiled=True).astype(f32)
        back_rows = jnp.concatenate([back_rows[:rows] + shared_back, back_rows[rows:]], axis=0)
        back_sums = lax.psum(back_rows.astype(bf16), "hs")
        shared_sums = [over_ep(a) for a in shared_grads]
        grad_tokens, heads_sums, grad_router, grad_attn_gain, grad_ffn_gain = plain_back(
            back_sums,
            residual,
            normed2,
            grad_t,
            router_t,
            ffn_gain,
            out_t,
            q,
            k,
            v,
            probs,
            tables,
            query_t,
            key_t,
            value_t,
            normed1,
            attended_t,
            tokens,
            attn_gain,
        )

    rows_major = Layout(major_to_minor=(0, 1))
    out_part = with_layout_constraint(out_part, rows_major)
    out_rows = lax.psum_scatter(out_part, EP, scatter_dimension=0, tiled=True)
    out_rows = with_layout_constraint(out_rows, rows_major)
    out_rows = (out_rows.astype(f32) + shared_part.astype(f32)).astype(bf16)
    out_quarter = lax.psum_scatter(out_rows, "hs", scatter_dimension=1, tiled=True)
    residual_quarter = lax.dynamic_slice_in_dim(residual, hs * quarter, quarter, 1)
    output = (residual_quarter + out_quarter.astype(f32)).astype(bf16)

    return (
        output,
        grad_tokens.T,
        grad_attn_gain,
        *[a.T for a in heads_sums],
        grad_ffn_gain,
        grad_router.T,
        shared_sums[0].T,
        shared_sums[1].T,
        shared_sums[2],
        grad_gate_t.swapaxes(1, 2),
        grad_up_t.swapaxes(1, 2),
        grad_expert_down,
    )


def solution(mesh):
    ep_count, hs_count = mesh.devices.shape
    cut = Mesh(mesh.devices.reshape(ep_count // 2, 2, hs_count), ("xy", "core", "hs"))
    return jax.shard_map(
        shards,
        mesh=cut,
        in_specs=(
            P(EP, None),
            P(),
            P(None, "hs"),
            P(None, "hs"),
            P(None, "hs"),
            P(None, "hs"),
            P(),
            P(),
            P(None, "hs"),
            P(None, "hs"),
            P("hs", None),
            P(EP, None, "hs"),
            P(EP, None, "hs"),
            P(EP, "hs", None),
            P(EP, None),
            P(EP, None),
            P(EP, "hs"),
        ),
        out_specs=(
            P(EP, "hs"),
            P(EP, "hs"),
            P(),
            P(None, "hs"),
            P(None, "hs"),
            P(None, "hs"),
            P(None, "hs"),
            P(),
            P(),
            P(None, "hs"),
            P(None, "hs"),
            P("hs", None),
            P(EP, None, "hs"),
            P(EP, None, "hs"),
            P(EP, "hs", None),
        ),
        check_vma=False,
    )
```

profile of v0, /device:TPU:9, one launch (start us, length us, event | category | flops | bytes accessed | tf_op | source)
XLA Modules:
  0.0 532.8 jit_solution(15582706002430264744)
XLA Ops:
  8.8 1.3 broadcast_in_dim.19.ffn_gain_ref
  10.1 1.3 broadcast_in_dim.18.gain_ref
  11.4 1.5 copy.47.doc_column_ref
  13.0 77.2 %front.1 = (bf16[512,1280]{1,0:T(8,128)(2,1)}, bf16[3,128,512]{2,1,0:T(8,128)(2,1)}, bf16[3,128,512]{2,1,0:T(8,128)(2,1)}, bf16[3,128,512]{2,1,0:T(8,128)(2,1)},...) custom-call(bf16[512,1280]{1,0:T(8,128)(2,1)} %x_ref.1, ...), custom_call_target="tpu_custom_call" | custom-call | bytes 150000000 | tf_op jit(solution)/shard_map/front/pallas_call | solution.py:741
  92.0 70.9 %gather_spread.1 = (bf16[8,8,112,1280]{3,2,1,0:T(8,128)(2,1)}, f32[8,896,1]{2,1,0:T(8,128)}, s32[8,8,512]{2,1,0:T(8,128)}) custom-call(bf16[512,1280]{1,0:T(8,128)(2,1)} %get-tuple-element.51.own_ref.normed2_ref, bf16[64,512]{1,0:T(8,128)(2,1)} %fusion.1.slots_ref, bf16[64,1280]{1,0:T(8,128)(2,1)} %fusion.4.router_ref), custom_call_target="tpu_custom_call" | custom-call | bytes 186000000 | tf_op jit(solution)/shard_map/gather_spread/pallas_call | solution.py:528
  162.9 30.6 %experts_forward.1 = (bf16[8,8,112,1280]{3,2,1,0:T(8,128)(2,1)}, f32[8,896,256]{2,1,0:T(8,128)}, f32[8,896,256]{2,1,0:T(8,128)}) custom-call(bf16[8,8,112,1280]{3,2,1,0:T(8,128)(2,1)} %get-tuple-element.52.x_ref, f32[8,896,1]{2,1,0:T(8,128)} %get-tuple-element.53.sw_ref, bf16[8,224,1280]{2,1,0:T(8,128)(2,1)} %bitcast.49, bf16[8,224,1280]{2,1,0:T(8,128)(2,1)} %bitcast.51, ...), custom_call_target="tpu_custom_call" | custom-call | bytes 93000000 | tf_op jit(solution)/shard_map/experts_forward/pallas_call | solution.py:229
  193.5 17.4 %collect.1 = bf16[8,512,1280]{2,1,0:T(8,128)(2,1)} custom-call(bf16[8,8,112,1280]{3,2,1,0:T(8,128)(2,1)} %get-tuple-element.54.y_ref, s32[8,8,512]{2,1,0:T(8,128)} %get-tuple-element.55.slot_ref.refs_1_), custom_call_target="tpu_custom_call" | custom-call | bytes 51000000 | tf_op jit(solution)/shard_map/collect/pallas_call | solution.py:304
  212.2 2.0 fusion.5
  214.2 17.1 %spread.1.gx_ref = bf16[8,8,112,1280]{3,2,1,0:T(8,128)(2,1)} custom-call(bf16[8,1280,512]{2,1,0:T(8,128)(2,1)} %bitcast.53, s32[8,8,512]{2,1,0:T(8,128)} %get-tuple-element.55.slot_ref.refs_1_), custom_call_target="tpu_custom_call" | custom-call | bytes 51000000 | tf_op jit(solution)/shard_map/spread/pallas_call | solution.py:119
  231.3 49.0 %experts_backward.1 = (bf16[8,8,112,1280]{3,2,1,0:T(8,128)(2,1)}, f32[8,224,1280]{2,1,0:T(8,128)}, f32[8,224,1280]{2,1,0:T(8,128)}, f32[8,224,1280]{2,1,0:T(8,128)}, f32[8,896,1]{2,1,0:T(8,128)}) custom-call(bf16[8,8,112,1280]{3,2,1,0:T(8,128)(2,1)} %get-tuple-element.52.x_ref, bf16[8,8,112,1280]{3,2,1,0:T(8,128)(2,1)} %spread.1.gx_ref, ...), custom_call_target="tpu_custom_call" | custom-call | bytes 141000000 | tf_op jit(solution)/shard_map/experts_backward/pallas_call | solution.py:247
  280.3 1.6 dynamic-slice_bitcast_fusion.grad_ref
  284.0 1.8 convolution_convert_fusion.1.shared_down_ref
  285.8 1.9 convolution_convert_fusion.forward_ref
  287.7 1.8 convolution_convert_fusion.3.shared_gate_ref
  289.5 1.8 convolution_convert_fusion.2.shared_up_ref
  292.1 2.0 fusion.mine_ref
  294.1 123.8 %collect_sum.1 = (bf16[576,1280]{1,0:T(8,128)(2,1)}, bf16[1408,1280]{1,0:T(8,128)(2,1)}, bf16[512,1280]{1,0:T(8,128)(2,1)}) custom-call(bf16[8,8,112,1280]{3,2,1,0:T(8,128)(2,1)} %get-tuple-element.58.y_ref, s32[8,8,512]{2,1,0:T(8,128)} %get-tuple-element.55.slot_ref.refs_1_, f32[8,896,1]{2,1,0:T(8,128)} %get-tuple-element.59.gsw_ref, ...), custom_call_target="tpu_custom_call" | custom-call | bytes 393000000 | tf_op jit(solution)/shard_map/collect_sum/pallas_call | solution.py:1002
  417.9 2.0 add_convert_fusion
  419.9 1.5 copy.51
  423.0 1.5 copy.48
  424.5 86.0 %back.1 = (f32[320,512]{1,0:T(8,128)}, bf16[384,1280]{1,0:T(8,128)(2,1)}, bf16[1024,1280]{1,0:T(8,128)(2,1)}) custom-call(bf16[576,1280]{1,0:T(8,128)(2,1)} %get-tuple-element.61.sums_ref, f32[512,1280]{1,0:T(8,128)} %get-tuple-element.50.residual_ref, bf16[512,1280]{1,0:T(8,128)(2,1)} %get-tuple-element.51.own_ref.normed2_ref, bf16[1280,512]{1,0:T(8,128)(2,1)} %copy-done.2, ...), custom_call_target="tpu_custom_call" | custom-call | bytes 270000000 | tf_op jit(solution)/shard_map/back/pallas_call | solution.py:1211
  510.5 8.7 %widen.1 = (f32[320,1280]{1,0:T(8,128)}, f32[320,1280]{1,0:T(8,128)}, f32[320,1280]{1,0:T(8,128)}, f32[320,1280]{1,0:T(8,128)}, f32[64,1280]{1,0:T(8,128)}, /*in...) custom-call(bf16[384,1280]{1,0:T(8,128)(2,1)} %get-tuple-element.70.early_ref, ...), custom_call_target="tpu_custom_call" | custom-call | bytes 24000000 | tf_op jit(solution)/shard_map/widen/pallas_call | solution.py:1261
  519.2 1.5 slice_reduce_fusion
  521.9 1.6 add_convert_fusion.1
  (39 shorter events, 11.3 us)
Async XLA Ops:
  8.0 274.8 %copy-start = (bf16[1280,448]{0,1:T(8,128)(2,1)S(1)}, bf16[1280,448]{0,1:T(8,128)(2,1)}, u32[]{:S(2)}) copy-start(bf16[1280,448]{0,1:T(8,128)(2,1)} %param.28) | copy-start | bytes 3440644
  8.0 206.2 %all-gather.2.cloned.1.call-start = ((), (), s32[]{:S(2)}) async-start(), calls=%async_computation.3 | async-start | bytes 10813440 | tf_op jit(solution)/shard_map/all_gather | solution.py:1439
  8.8 409.1 %reduce-scatter.5.cloned.1.call-start = ((), (), s32[]{:S(2)}) async-start(), calls=%async_computation.2 | async-start | bytes 11796480 | tf_op jit(solution)/shard_map/reduce_scatter | solution.py:1557
  13.0 77.2 %copy-start.8 = (s32[512,7]{0,1:T(8,128)S(1)}, s32[512,7]{0,1:T(8,128)}, u32[]{:S(2)}) copy-start(s32[512,7]{0,1:T(8,128)} %param.33) | copy-start | bytes 43012
  13.0 78.3 %copy-start.5 = (bf16[1280,64]{0,1:T(8,128)(2,1)S(1)}, bf16[1280,64]{0,1:T(8,128)(2,1)}, u32[]{:S(2)}) copy-start(bf16[1280,64]{0,1:T(8,128)(2,1)} %param.26) | copy-start | bytes 491524
  210.8 1.3 copy-start.1
  210.9 309.8 %reduce-scatter.7.cloned.1.call-start = ((), (), s32[]{:S(2)}) async-start(), calls=%async_computation.4 | async-start | bytes 1638400
  280.3 1.8 copy-start.9
  282.1 1.9 copy-start.2
  289.5 1.8 copy-start.4
  419.9 1.6 copy-start.7
  421.5 1.6 copy-start.3
  521.8 2.5 copy-start.6
Sparse Core Ops, SparseCore 0:
  11.7 121.4 all-gather.1
Sparse Core Ops, SparseCore 1:
  210.9 80.7 reduce-scatter.4
  421.6 32.5 reduce-scatter.6
where the time goes:
time: 537 us; the launch traced here: 533 us
  Pallas kernels  481 us (90%)
  between operations  15.9 us (3%)
  local copies, waits for them, and re-layouts  15.8 us (3%)
  matrix products  14.9 us (3%)
    pallas_call x1, Pallas kernels, collect_sum(): pl.pallas_call(collect_sum_kernel, in_specs=[pl.BlockSpec(memory_space=pl...  124 us
    pallas_call x1, Pallas kernels, back(): pl.pallas_call(back_kernel, in_specs=[vmem] * len(args), out_specs=[vmem]...  86 us
    pallas_call x1, Pallas kernels, front(): pl.pallas_call(front_kernel, in_specs=[vmem] * 11, out_specs=[vmem] * 9,...  77.2 us
    pallas_call x1, Pallas kernels, gather_spread(): pl.pallas_call(gather_spread_kernel, in_specs=[vmem, vmem, vmem], out_spe...  70.9 us
    pallas_call x1, Pallas kernels, experts_backward(): pl.pallas_call(functools.partial(experts_backward_kernel, groups), grid=(...  49 us
    pallas_call x1, Pallas kernels, experts_forward(): pl.pallas_call(experts_forward_kernel, grid=(local, groups), in_specs=[sl...  30.6 us
    pallas_call x1, Pallas kernels, collect(): pl.pallas_call(kernel, grid=(s,), in_specs=in_specs, out_specs=pl.BlockSp...  17.4 us
    pallas_call x1, Pallas kernels, spread(): pl.pallas_call(functools.partial(spread_kernel, weighted), grid=(s,), in_...  17.1 us
  transfers between devices with their start and end apart: 3, of which 0 were waited for; matrix products, arithmetic and copies ran while one was open for 5% of the time, Pallas kernels for 90%

commit v1 on v0

--- a/solution.py
+++ b/solution.py
@@ -212,6 +212,14 @@
     dx_ref[...] = (nn(gg, wg[...]) + nn(gu, wu[...])).astype(bf16).reshape(dx_ref.shape)
 
 
+def sending(remote_too, collective_id):
+    if not remote_too:
+        return pltpu.CompilerParams(vmem_limit_bytes=VMEM_LIMIT)
+    return pltpu.CompilerParams(
+        vmem_limit_bytes=VMEM_LIMIT, collective_id=collective_id, has_side_effects=True
+    )
+
+
 def expert_specs(s, width):
     group = min(s, 8)
     slots = pl.BlockSpec((group, 1, CAP, width), lambda i, j: (j, i, 0, 0))
@@ -220,23 +228,75 @@
     return s // group, slots, lines, per
 
 
-def experts_forward(x, sw, wg, wu, wd):
+def experts_forward_sending_kernel(
+    x_ref,
+    sw_ref,
+    wg_ref,
+    wu_ref,
+    wd_ref,
+    grad_ref,
+    y_ref,
+    gate_ref,
+    up_ref,
+    near_ref,
+    wg,
+    wu,
+    wd,
+    send,
+    recv,
+):
+    chip, core, z, cx, cy, cd = places()
+    peers = [(cx, core, z), (cy, core, z)]
+    copies = [
+        remote(grad_ref, near_ref.at[i], send.at[i], recv.at[i], peer) for i, peer in enumerate(peers)
+    ]
+
+    @pl.when(pl.program_id(0) == 0)
+    def _():
+        greet(peers)
+        for copy in copies:
+            copy.start()
+
+    experts_forward_kernel(
+        x_ref, sw_ref, wg_ref, wu_ref, wd_ref, y_ref, gate_ref, up_ref, wg, wu, wd
+    )
+
+    @pl.when(pl.program_id(0) == pl.num_programs(0) - 1)
+    def _():
+        for copy in copies:
+            copy.wait()
+
+
+def experts_forward(x, sw, wg, wu, wd, grad=None):
     s, local, cap, width = x.shape
     ff = wg.shape[1]
     rows = s * cap
     groups, slots, lines, per = expert_specs(s, width)
     middle = jax.ShapeDtypeStruct((local, rows, PAD), f32)
+    kernel = experts_forward_kernel
+    in_specs = [slots, lines(1)] + [per(ff, width)] * 3
+    out_specs = [slots, lines(PAD), lines(PAD)]
+    out_shape = [jax.ShapeDtypeStruct(x.shape, bf16), middle, middle]
+    scratch = [pltpu.VMEM((PAD, width), bf16)] * 3
+    args = [x, sw, wg, wu, wd]
+    if grad is not None:
+        kernel = experts_forward_sending_kernel
+        in_specs.append(pl.BlockSpec(memory_space=pl.ANY))
+        out_specs.append(pl.BlockSpec(memory_space=pl.ANY))
+        out_shape.append(jax.ShapeDtypeStruct((2, *grad.shape), bf16))
+        scratch += [pltpu.SemaphoreType.DMA((2,))] * 2
+        args.append(grad)
     return pl.pallas_call(
-        experts_forward_kernel,
+        kernel,
         grid=(local, groups),
-        in_specs=[slots, lines(1)] + [per(ff, width)] * 3,
-        out_specs=[slots, lines(PAD), lines(PAD)],
-        out_shape=[jax.ShapeDtypeStruct(x.shape, bf16), middle, middle],
-        scratch_shapes=[pltpu.VMEM((PAD, width), bf16)] * 3,
-        compiler_params=pltpu.CompilerParams(vmem_limit_bytes=VMEM_LIMIT),
+        in_specs=in_specs,
+        out_specs=out_specs,
+        out_shape=out_shape,
+        scratch_shapes=scratch,
+        compiler_params=sending(grad is not None, 4),
         cost_estimate=takes(31),
         name="experts_forward",
-    )(x, sw, wg, wu, wd)
+    )(*args)
 
 
 def experts_backward(x, gx, gate, up, sw, wg, wu, wd):
@@ -268,6 +328,41 @@
     out_ref[0] = tn(pick[...], y_ref[...].reshape(pick.shape[0], -1)).astype(bf16)
 
 
+def collect_sending_kernel(
+    y_ref, slot_ref, grad_ref, near_ref, out_ref, far_ref, given_ref, pick, send, recv, csend, crecv
+):
+    chip, core, z, cx, cy, cd = places()
+    x_peer, y_peer, c_peer = (cx, core, z), (cy, core, z), (chip, 1 - core, z)
+    half = grad_ref.shape[0] // 2
+    top, low = pl.ds(0, half), pl.ds(half, half)
+    relays = [
+        remote(near_ref.at[0, top], far_ref.at[top], send.at[0], recv.at[0], y_peer),
+        remote(near_ref.at[1, low], far_ref.at[low], send.at[1], recv.at[1], x_peer),
+    ]
+    passes = [
+        remote(ref, given_ref.at[i], csend.at[i], crecv.at[i], c_peer)
+        for i, ref in enumerate((grad_ref, near_ref.at[0], near_ref.at[1], far_ref))
+    ]
+
+    @pl.when(pl.program_id(0) == 0)
+    def _():
+        greet([x_peer, y_peer, c_peer])
+        for copy in (*relays, *passes[:3]):
+            copy.start()
+
+    collect_kernel(y_ref, slot_ref, out_ref, pick)
+
+    @pl.when(pl.program_id(0) == pl.num_programs(0) - 1)
+    def _():
+        for copy in relays:
+            copy.wait_recv()
+        passes[3].start()
+        for copy in passes:
+            copy.wait()
+        for copy in relays:
+            copy.wait_send()
+
+
 def collect_back_kernel(experts, y_ref, slot_ref, gsw_ref, first_ref, out_ref, pick):
     local, rows = slot_ref.shape[1:]
     first = first_ref[0]
@@ -281,6 +376,94 @@
     out_ref[0, :rows] = tn(pick[...], y_ref[...].reshape(pick.shape[0], -1)).astype(bf16)
     out_ref[0, rows:] = jnp.zeros((experts, out_ref.shape[2]), bf16)
     out_ref[0, rows:, :rows] = probs.astype(bf16)
+
+
+def collect_sending(y, slot, grad, near):
+    s, local, cap, width = y.shape
+    rows = slot.shape[2]
+    dma = pltpu.SemaphoreType.DMA
+    whole = pl.BlockSpec(memory_space=pl.ANY)
+    return pl.pallas_call(
+        collect_sending_kernel,
+        grid=(s,),
+        in_specs=[
+            pl.BlockSpec((1, local, cap, width), lambda i: (i, 0, 0, 0)),
+            pl.BlockSpec((1, local, rows), lambda i: (i, 0, 0)),
+            whole,
+            whole,
+        ],
+        out_specs=[pl.BlockSpec((1, rows, width), lambda i: (i, 0, 0)), whole, whole],
+        out_shape=[
+            jax.ShapeDtypeStruct((s, rows, width), bf16),
+            jax.ShapeDtypeStruct(grad.shape, bf16),
+            jax.ShapeDtypeStruct((4, *grad.shape), bf16),
+        ],
+        scratch_shapes=[
+            pltpu.VMEM((local * cap, rows), bf16),
+            dma((2,)),
+            dma((2,)),
+            dma((4,)),
+            dma((4,)),
+        ],
+        compiler_params=sending(True, 5),
+        cost_estimate=takes(20),
+        name="collect_sending",
+    )(y, slot, grad, near)
+
+
+def spread_grad_kernel(grad_ref, near_ref, far_ref, given_ref, slot_ref, x_ref, pick, gbuf, xbuf, come, gone):
+    chip, core = lax.axis_index("xy"), lax.axis_index("core")
+    local, rows = slot_ref.shape[1:]
+    here = [grad_ref, near_ref.at[0], near_ref.at[1], far_ref]
+    sources = [(here[t // 2], given_ref.at[t // 2])[t % 2] for t in range(8)]
+
+    def in_copy(t):
+        return pltpu.make_async_copy(sources[t], gbuf.at[t % 2], come.at[t % 2])
+
+    def out_copy(t, src):
+        return pltpu.make_async_copy(xbuf.at[t % 2], x_ref.at[src], gone.at[t % 2])
+
+    number = lax.broadcasted_iota(jnp.int32, (CAP, rows), 0)
+    in_copy(0).start()
+    for t in range(8):
+        if t < 7:
+            in_copy(t + 1).start()
+        x, y = (chip % 2 + (t // 2) % 2) % 2, (chip // 2 + t // 4) % 2
+        src = (y * 2 + x) * 2 + (core + t % 2) % 2
+        slots = slot_ref[src]
+        for e in range(local):
+            mask = slots[e : e + 1, :] == number
+            pick[e * CAP : (e + 1) * CAP, :] = mask.astype(f32).astype(bf16)
+        in_copy(t).wait()
+        if t >= 2:
+            out_copy(t, src).wait()
+        xbuf[t % 2] = nt(pick[...], gbuf[t % 2]).astype(bf16).reshape(xbuf.shape[1:])
+        out_copy(t, src).start()
+    out_copy(0, 0).wait()
+    out_copy(1, 0).wait()
+
+
+def spread_grad(grad, near, far, given, slot):
+    s, local, rows = slot.shape
+    width = grad.shape[0]
+    whole = pl.BlockSpec(memory_space=pl.ANY)
+    dma = pltpu.SemaphoreType.DMA
+    return pl.pallas_call(
+        spread_grad_kernel,
+        in_specs=[whole] * 4 + [pl.BlockSpec(memory_space=pltpu.VMEM)],
+        out_specs=whole,
+        out_shape=jax.ShapeDtypeStruct((s, local, CAP, width), bf16),
+        scratch_shapes=[
+            pltpu.VMEM((local * CAP, rows), bf16),
+            pltpu.VMEM((2, width, rows), bf16),
+            pltpu.VMEM((2, local, CAP, width), bf16),
+            dma((2,)),
+            dma((2,)),
+        ],
+        compiler_params=sending(False, 0),
+        cost_estimate=takes(16),
+        name="spread_grad",
+    )(grad, near, far, given, slot)
 
 
 def collect(y, slot, gsw=None, first=None, experts=0):
@@ -413,7 +596,22 @@
 
 
 def gather_spread_kernel(
-    own_ref, slots_ref, router_ref, x_ref, sw_ref, slot_ref, held, pick, xbuf, send, recv, copied
+    own_ref,
+    slots_ref,
+    router_ref,
+    grad_ref,
+    x_ref,
+    sw_ref,
+    slot_ref,
+    grad_all_ref,
+    held,
+    pick,
+    xbuf,
+    send,
+    recv,
+    copied,
+    zsend,
+    zrecv,
 ):
     chip, core, z, cx, cy, cd = places()
     other = 1 - core
@@ -433,7 +631,15 @@
         )
 
     whole = pl.ds(0, tall)
-    greet([x_peer, y_peer, c_peer])
+    z_peers = [(chip, core, (z + i) % 4) for i in (1, 2, 3)]
+    greet([x_peer, y_peer, c_peer, *z_peers])
+    quarter = grad_ref.shape[0]
+
+    def grad_copy(i, q):
+        return remote(
+            grad_ref, grad_all_ref.at[block(q, quarter)], zsend.at[i], zrecv.at[i], z_peers[i]
+        )
+
     held[me, :rows] = own_ref[...]
     held[me, rows:] = jnp.zeros((EXTRA, own_ref.shape[1]), bf16)
     held[me, rows:, :rows] = slots_ref[...]
@@ -443,8 +649,9 @@
     relay_top, relay_low = move(5, at(cx, core), top, y_peer), move(6, at(cy, core), low, x_peer)
     pass_x, pass_y = move(7, at(cx, core), whole, c_peer), move(8, at(cy, core), whole, c_peer)
     pass_d = move(9, at(cd, core), whole, c_peer)
-    for copy in (x_top, y_low, x_low, y_top, to_core):
+    for copy in (x_top, y_low, x_low, y_top, to_core, *[grad_copy(i, z) for i in (1, 0, 2)]):
         copy.start()
+    grad_all_ref[block(z, quarter)] = grad_ref[...]
 
     def arrived(number, slot, part):
         move(number, slot, part, c_peer).wait_recv()
@@ -517,22 +724,26 @@
     lax.fori_loop(0, 8, step, 0)
     out_copy(0, me).wait()
     out_copy(1, me).wait()
+    for i in range(3):
+        grad_copy(i, (z + 3 - i) % 4).wait_recv()
+        grad_copy(i, z).wait_send()
     for copy in (x_top, x_low, y_low, y_top, to_core, relay_top, relay_low, pass_x, pass_y, pass_d):
         copy.wait_send()
 
 
-def gather_spread(own, slots, router_t, local, ep_count):
+def gather_spread(own, slots, router_t, grad_quarter, local, ep_count):
     rows, width = own.shape
     tall = rows + EXTRA
     vmem = pl.BlockSpec(memory_space=pltpu.VMEM)
     return pl.pallas_call(
         gather_spread_kernel,
-        in_specs=[vmem, vmem, vmem],
-        out_specs=[pl.BlockSpec(memory_space=pl.ANY), vmem, vmem],
+        in_specs=[vmem] * 4,
+        out_specs=[pl.BlockSpec(memory_space=pl.ANY), vmem, vmem, vmem],
         out_shape=[
             jax.ShapeDtypeStruct((ep_count, local, CAP, width), bf16),
             jax.ShapeDtypeStruct((local, ep_count * CAP, 1), f32),
             jax.ShapeDtypeStruct((ep_count, local, rows), jnp.int32),
+            jax.ShapeDtypeStruct((width, rows), bf16),
         ],
         scratch_shapes=[
             pltpu.VMEM((ep_count, tall, width), bf16),
@@ -541,13 +752,15 @@
             pltpu.SemaphoreType.DMA((10,)),
             pltpu.SemaphoreType.DMA((10,)),
             pltpu.SemaphoreType.DMA((2,)),
+            pltpu.SemaphoreType.DMA((3,)),
+            pltpu.SemaphoreType.DMA((3,)),
         ],
         compiler_params=pltpu.CompilerParams(
             vmem_limit_bytes=VMEM_LIMIT, collective_id=0, has_side_effects=True
         ),
         cost_estimate=takes(62),
         name="gather_spread",
-    )(own, slots, router_t)
+    )(own, slots, router_t, grad_quarter)
 
 
 def front_kernel(
@@ -1436,9 +1649,6 @@
     small = ep_count == 8 and lax.axis_size("hs") == 4
 
     query_t, key_t, value_t, router_t = attn_query.T, attn_key.T, attn_value.T, router.T
-    grad_all_t = lax.all_gather(out_grad.T, (*EP, "hs"), axis=0, tiled=True)
-    grad_all_t = grad_all_t.reshape(ep_count, width, rows)
-    grad_t = lax.dynamic_index_in_dim(grad_all_t, ep, 0, keepdims=False)
     positions = jnp.arange(rows, dtype=jnp.int32)
     below = (positions[:, None] > positions[None, :]).astype(bf16)
     chosen = jnp.any(
@@ -1457,6 +1667,34 @@
         )
     normed1, q, k, v, probs, attended_t, out_t, residual, normed2 = ahead
     out_t = out_t.reshape(width, width)
+
+    first = ep * local
+    rolled = jnp.roll(router_t, -first, axis=0)
+    gate_t, up_t = expert_gate.swapaxes(1, 2), expert_up.swapaxes(1, 2)
+    weights = gate_t, up_t, expert_down
+    if small:
+        ex_in, slot_weight, slot, grad_t = gather_spread(
+            normed2, own_slots, rolled, out_grad.T, local, ep_count
+        )
+        ex_out, ex_gate, ex_up, near = experts_forward(ex_in, slot_weight, *weights, grad_t)
+        out_part, far, given = collect_sending(ex_out, slot, grad_t, near)
+        ex_grad = spread_grad(grad_t, near, far, given, slot)
+    else:
+        grad_all_t = lax.all_gather(out_grad.T, (*EP, "hs"), axis=0, tiled=True)
+        grad_all_t = grad_all_t.reshape(ep_count, width, rows)
+        grad_t = lax.dynamic_index_in_dim(grad_all_t, ep, 0, keepdims=False)
+        slot = lax.dynamic_slice_in_dim(
+            lax.all_gather(own_slots, EP, axis=0), first, local, 1
+        ).astype(jnp.int32)
+        normed_all = lax.all_gather(normed2, EP, axis=0, tiled=True)
+        ex_in, slot_weight = spread(normed_all, slot, rolled)
+        ex_out, ex_gate, ex_up = experts_forward(ex_in, slot_weight, *weights)
+        out_part = collect(ex_out, slot)
+        ex_grad = spread(grad_all_t, slot)
+    out_part = out_part.reshape(ep_count * rows, width)
+    ex_back, grad_gate_t, grad_up_t, grad_expert_down, grad_slot_weight = experts_backward(
+        ex_in, ex_grad, ex_gate, ex_up, slot_weight, *weights
+    )
 
     sh_gate = dot(normed2, shared_gate)
     sh_up = dot(normed2, shared_up)
@@ -1474,24 +1712,6 @@
     ]
     shared_back = ein("tf,df->td", grad_sh_gate, shared_gate) + ein(
         "tf,df->td", grad_sh_up, shared_up
-    )
-
-    first = ep * local
-    rolled = jnp.roll(router_t, -first, axis=0)
-    if small:
-        ex_in, slot_weight, slot = gather_spread(normed2, own_slots, rolled, local, ep_count)
-    else:
-        slot = lax.dynamic_slice_in_dim(
-            lax.all_gather(own_slots, EP, axis=0), first, local, 1
-        ).astype(jnp.int32)
-        normed_all = lax.all_gather(normed2, EP, axis=0, tiled=True)
-        ex_in, slot_weight = spread(normed_all, slot, rolled)
-    gate_t, up_t = expert_gate.swapaxes(1, 2), expert_up.swapaxes(1, 2)
-    ex_grad = spread(grad_all_t, slot)
-    ex_out, ex_gate, ex_up = experts_forward(ex_in, slot_weight, gate_t, up_t, expert_down)
-    out_part = collect(ex_out, slot).reshape(ep_count * rows, width)
-    ex_back, grad_gate_t, grad_up_t, grad_expert_down, grad_slot_weight = experts_backward(
-        ex_in, ex_grad, ex_gate, ex_up, slot_weight, gate_t, up_t, expert_down
     )
 
     if small:

time: 537 us -> 506 us (0.942)
  Pallas kernels: 481 us -> 451 us
    pallas_call x1, Pallas kernels: 77.2 us -> 55.2 us  [front(): pl.pallas_call(front_kernel, in_specs=[vmem] * 11, out_specs=[vmem] * 9,...]
    pallas_call x1, Pallas kernels: 124 us -> 115 us  [collect_sum(): pl.pallas_call(collect_sum_kernel, in_specs=[pl.BlockSpec(memory_space=pl...]
  transfers between devices with their start and end apart: 3 -> 2, of which waited for: 0 -> 0; matrix products, arithmetic and copies ran while one was open for 5% -> 3% of each run, Pallas kernels for 90% -> 55%
where the time goes in v1:
time: 506 us; the launch traced here: 499 us
  Pallas kernels  451 us (89%)
  between operations  14.5 us (3%)
  local copies, waits for them, and re-layouts  14 us (3%)
  matrix products  13.6 us (3%)
  other arithmetic  6.06 us (1%)
    pallas_call x1, Pallas kernels, collect_sum(): pl.pallas_call(collect_sum_kernel, in_specs=[pl.BlockSpec(memory_space=pl...  115 us
    pallas_call x1, Pallas kernels, back(): pl.pallas_call(back_kernel, in_specs=[vmem] * len(args), out_specs=[vmem]...  86.3 us
    pallas_call x1, Pallas kernels, gather_spread(): pl.pallas_call(gather_spread_kernel, in_specs=[vmem] * 4, out_specs=[pl.B...  61.5 us
    pallas_call x1, Pallas kernels, front(): pl.pallas_call(front_kernel, in_specs=[vmem] * 11, out_specs=[vmem] * 9,...  55.2 us
    pallas_call x1, Pallas kernels, experts_backward(): pl.pallas_call(functools.partial(experts_backward_kernel, groups), grid=(...  47.4 us
    pallas_call x1, Pallas kernels, experts_forward(): pl.pallas_call(kernel, grid=(local, groups), in_specs=in_specs, out_specs...  35.4 us
    pallas_call x1, Pallas kernels, collect_sending(): pl.pallas_call(collect_sending_kernel, grid=(s,), in_specs=[pl.BlockSpec(...  23.2 us
    pallas_call x1, Pallas kernels, spread_grad(): pl.pallas_call(spread_grad_kernel, in_specs=[whole] * 4 + [pl.BlockSpec(m...  18.3 us
  transfers between devices with their start and end apart: 2, of which 0 were waited for; matrix products, arithmetic and copies ran while one was open for 3% of the time, Pallas kernels for 55%

profile of v1, /device:TPU:9, one launch (start us, length us, event | category | flops | bytes accessed | tf_op | source)
XLA Modules:
  0.0 499.3 jit_solution(12516200307904407625)
XLA Ops:
  7.3 1.4 broadcast_in_dim.19.ffn_gain_ref
  8.6 1.3 broadcast_in_dim.18.gain_ref
  11.7 1.5 copy.47.doc_column_ref
  13.2 1.6 fusion.4.router_ref
  14.9 55.2 %front.1 = (bf16[512,1280]{1,0:T(8,128)(2,1)}, bf16[3,128,512]{2,1,0:T(8,128)(2,1)}, bf16[3,128,512]{2,1,0:T(8,128)(2,1)}, bf16[3,128,512]{2,1,0:T(8,128)(2,1)},...) custom-call(bf16[512,1280]{1,0:T(8,128)(2,1)} %x_ref.1, ...), custom_call_target="tpu_custom_call" | custom-call | bytes 150000000 | tf_op jit(solution)/shard_map/front/pallas_call | solution.py:954
  70.1 61.5 %gather_spread.1 = (bf16[8,8,112,1280]{3,2,1,0:T(8,128)(2,1)}, f32[8,896,1]{2,1,0:T(8,128)}, s32[8,8,512]{2,1,0:T(8,128)}, bf16[1280,512]{1,0:T(8,128)(2,1)}) custom-call(bf16[512,1280]{1,0:T(8,128)(2,1)} %get-tuple-element.56.own_ref.normed2_ref, bf16[64,512]{1,0:T(8,128)(2,1)} %fusion.1.slots_ref, bf16[64,1280]{1,0:T(8,128)(2,1)} %fusion.4.router_ref, ...), custom_call_target="tpu_custom_call" | custom-call | bytes 186000000 | tf_op jit(solution)/shard_map/gather_spread/pallas_call | solution.py:738
  131.6 35.4 %experts_forward.1 = (bf16[8,8,112,1280]{3,2,1,0:T(8,128)(2,1)}, f32[8,896,256]{2,1,0:T(8,128)}, f32[8,896,256]{2,1,0:T(8,128)}, bf16[2,1280,512]{2,1,0:T(8,128)(2,1)}) custom-call(bf16[8,8,112,1280]{3,2,1,0:T(8,128)(2,1)} %get-tuple-element.57.x_ref, f32[8,896,1]{2,1,0:T(8,128)} %get-tuple-element.58.sw_ref, bf16[8,224,1280]{2,1,0:T(8,128)(2,1)} %bitcast.45, ...), custom_call_target="tpu_custom_call" | custom-call | bytes 93000000 | tf_op jit(solution)/shard_map/experts_forward/pallas_call | solution.py:289
  167.0 23.2 %collect_sending.1 = (bf16[8,512,1280]{2,1,0:T(8,128)(2,1)}, bf16[1280,512]{1,0:T(8,128)(2,1)}, bf16[4,1280,512]{2,1,0:T(8,128)(2,1)}) custom-call(bf16[8,8,112,1280]{3,2,1,0:T(8,128)(2,1)} %get-tuple-element.60.y_ref, s32[8,8,512]{2,1,0:T(8,128)} %get-tuple-element.61.slot_ref, bf16[1280,512]{1,0:T(8,128)(2,1)} %get-tuple-element.59.grad_ref, ...), custom_call_target="tpu_custom_call" | custom-call | bytes 60000000 | tf_op jit(solution)/shard_map/collect_sending/pallas_call | solution.py:386
  190.4 18.3 %spread_grad.1.gx_ref = bf16[8,8,112,1280]{3,2,1,0:T(8,128)(2,1)} custom-call(bf16[1280,512]{1,0:T(8,128)(2,1)} %get-tuple-element.59.grad_ref, bf16[2,1280,512]{2,1,0:T(8,128)(2,1)} %get-tuple-element.62.near_ref, bf16[1280,512]{1,0:T(8,128)(2,1)} %get-tuple-element.64.far_ref, bf16[4,1280,512]{2,1,0:T(8,128)(2,1)} %get-tuple-element.65.given_ref, ...), custom_call_target="tpu_custom_call" | custom-call | bytes 48000000 | tf_op jit(solution)/shard_map/spread_grad/pallas_call | solution.py:451
  208.7 47.4 %experts_backward.1 = (bf16[8,8,112,1280]{3,2,1,0:T(8,128)(2,1)}, f32[8,224,1280]{2,1,0:T(8,128)}, f32[8,224,1280]{2,1,0:T(8,128)}, f32[8,224,1280]{2,1,0:T(8,128)}, f32[8,896,1]{2,1,0:T(8,128)}) custom-call(bf16[8,8,112,1280]{3,2,1,0:T(8,128)(2,1)} %get-tuple-element.57.x_ref, bf16[8,8,112,1280]{3,2,1,0:T(8,128)(2,1)} %spread_grad.1.gx_ref, ...), custom_call_target="tpu_custom_call" | custom-call | bytes 141000000 | tf_op jit(solution)/shard_map/experts_backward/pallas_call | solution.py:307
  259.7 1.8 convolution_convert_fusion.1.shared_down_ref
  261.5 1.9 convolution_convert_fusion.forward_ref
  263.4 1.8 convolution_convert_fusion.3.shared_gate_ref
  265.2 1.8 convolution_convert_fusion.2.shared_up_ref
  267.8 2.0 fusion.mine_ref
  269.8 115.0 %collect_sum.1 = (bf16[576,1280]{1,0:T(8,128)(2,1)}, bf16[1408,1280]{1,0:T(8,128)(2,1)}, bf16[512,1280]{1,0:T(8,128)(2,1)}) custom-call(bf16[8,8,112,1280]{3,2,1,0:T(8,128)(2,1)} %get-tuple-element.68.y_ref, s32[8,8,512]{2,1,0:T(8,128)} %get-tuple-element.61.slot_ref, f32[8,896,1]{2,1,0:T(8,128)} %get-tuple-element.69.gsw_ref, ...), custom_call_target="tpu_custom_call" | custom-call | bytes 393000000 | tf_op jit(solution)/shard_map/collect_sum/pallas_call | solution.py:1215
  384.8 2.0 add_convert_fusion
  386.8 1.5 copy.51
  389.9 1.5 copy.48
  391.3 86.3 %back.1 = (f32[320,512]{1,0:T(8,128)}, bf16[384,1280]{1,0:T(8,128)(2,1)}, bf16[1024,1280]{1,0:T(8,128)(2,1)}) custom-call(bf16[576,1280]{1,0:T(8,128)(2,1)} %get-tuple-element.71.sums_ref, f32[512,1280]{1,0:T(8,128)} %get-tuple-element.55.residual_ref, bf16[512,1280]{1,0:T(8,128)(2,1)} %get-tuple-element.56.own_ref.normed2_ref, ...), custom_call_target="tpu_custom_call" | custom-call | bytes 270000000 | tf_op jit(solution)/shard_map/back/pallas_call | solution.py:1424
  477.6 8.7 %widen.1 = (f32[320,1280]{1,0:T(8,128)}, f32[320,1280]{1,0:T(8,128)}, f32[320,1280]{1,0:T(8,128)}, f32[320,1280]{1,0:T(8,128)}, f32[64,1280]{1,0:T(8,128)}, /*in...) custom-call(bf16[384,1280]{1,0:T(8,128)(2,1)} %get-tuple-element.80.early_ref, ...), custom_call_target="tpu_custom_call" | custom-call | bytes 24000000 | tf_op jit(solution)/shard_map/widen/pallas_call | solution.py:1474
  486.3 1.5 slice_reduce_fusion
  487.8 1.2 copy.52
  489.0 1.6 add_convert_fusion.1
  (31 shorter events, 9.7 us)
Async XLA Ops:
  7.2 251.4 %copy-start = (bf16[1280,448]{0,1:T(8,128)(2,1)S(1)}, bf16[1280,448]{0,1:T(8,128)(2,1)}, u32[]{:S(2)}) copy-start(bf16[1280,448]{0,1:T(8,128)(2,1)} %param.28) | copy-start | bytes 3440644
  7.2 377.6 %reduce-scatter.5.cloned.1.call-start = ((), (), s32[]{:S(2)}) async-start(), calls=%async_computation.2 | async-start | bytes 11796480 | tf_op jit(solution)/shard_map/reduce_scatter | solution.py:1777
  190.2 297.6 %reduce-scatter.7.cloned.1.call-start = ((), (), s32[]{:S(2)}) async-start(), calls=%async_computation.3 | async-start | bytes 1638400
  208.7 47.4 %copy-start.2 = (bf16[512,1280]{1,0:T(8,128)(2,1)S(1)}, bf16[512,1280]{1,0:T(8,128)(2,1)}, u32[]{:S(2)}) copy-start(bf16[512,1280]{1,0:T(8,128)(2,1)} %get-tuple-element.56.own_ref.normed2_ref) | copy-start | bytes 3932164
  208.7 47.4 %copy-start.4 = (bf16[1280,448]{0,1:T(8,128)(2,1)S(1)}, bf16[1280,448]{0,1:T(8,128)(2,1)}, u32[]{:S(2)}) copy-start(bf16[1280,448]{0,1:T(8,128)(2,1)} %param.27) | copy-start | bytes 3440644
  256.1 1.3 copy-start.1
  256.2 1.6 copy-start.7
  386.8 1.5 copy-start.6
  388.3 1.6 copy-start.3
  489.0 2.5 copy-start.5
Sparse Core Ops, SparseCore 0:
  190.3 80.0 reduce-scatter.4
  388.4 32.9 reduce-scatter.6

commit v2 on v1

--- a/solution.py
+++ b/solution.py
@@ -770,9 +770,7 @@
     wk_ref,
     wv_ref,
     wo_ref,
-    ffn_gain_ref,
     doc_ref,
-    doc_column_ref,
     cos_ref,
     sin_ref,
     normed1_ref,
@@ -848,7 +846,7 @@
 
     x = x_ref[...].astype(f32)
     rms1 = lax.rsqrt(jnp.sum(x * x, axis=-1, keepdims=True) * (1.0 / width) + EPS)
-    normed1_ref[...] = (x * rms1 * gain_ref[...]).astype(bf16)
+    normed1_ref[...] = (x * rms1 * gain_ref[0:1]).astype(bf16)
     out_ref[z] = wo_ref[...]
 
     cosine, sine = cos_ref[...], sin_ref[...]
@@ -856,7 +854,8 @@
     scale = 1.0 / math.sqrt(HEAD_DIM)
     row = lax.broadcasted_iota(jnp.int32, (rows, rows), 0)
     column = lax.broadcasted_iota(jnp.int32, (rows, rows), 1)
-    allowed = (row >= column) & (doc_column_ref[...] == doc_ref[...])
+    doc = jnp.broadcast_to(doc_ref[...].astype(f32), (rows, rows))
+    allowed = (row >= column) & (doc == doc.T)
 
     def turn(pre):
         a, b = pre[:half_dim], pre[half_dim:]
@@ -934,7 +933,7 @@
     residual = x_ref[...].astype(f32) + nt(attended, out_ref[...].reshape(width, width))
     residual_ref[...] = residual
     rms2 = lax.rsqrt(jnp.sum(residual * residual, axis=-1, keepdims=True) * (1.0 / width) + EPS)
-    normed2_ref[...] = (residual * rms2 * ffn_gain_ref[...]).astype(bf16)
+    normed2_ref[...] = (residual * rms2 * gain_ref[1:2]).astype(bf16)
     for one in (trade, *out_z, *copies):
         one.wait_send()
     for i in range(3):
@@ -943,7 +942,7 @@
         out_core(i, core).wait_send()
 
 
-def front(x, gain, wq, wk, wv, wo, ffn_gain, doc, tables):
+def front(x, gains, wq, wk, wv, wo, doc, tables):
     rows, width = x.shape
     quarter = wq.shape[0]
     heads = -(-quarter // HEAD_DIM)
@@ -953,7 +952,7 @@
     low = lambda *shape: jax.ShapeDtypeStruct(shape, bf16)
     return pl.pallas_call(
         front_kernel,
-        in_specs=[vmem] * 11,
+        in_specs=[vmem] * 9,
         out_specs=[vmem] * 9,
         out_shape=[
             low(rows, width),
@@ -983,21 +982,22 @@
         ),
         cost_estimate=takes(50),
         name="front",
-    )(x, gain[None, :], wq, wk, wv, wo, ffn_gain[None, :], doc, doc.T, *tables)
+    )(x, gains, wq, wk, wv, wo, doc, *tables)
 
 
 def collect_sum_kernel(
     y_ref,
     slot_ref,
     gsw_ref,
-    mine_ref,
-    shared_gate_ref,
-    shared_up_ref,
-    shared_down_ref,
-    forward_ref,
+    normed_ref,
+    grad_ref,
+    gate_ref,
+    up_ref,
+    down_ref,
     out_ref,
     sum_ref,
-    passed_ref,
+    forward_ref,
+    mine,
     pick,
     ybuf,
     stage,
@@ -1006,7 +1006,6 @@
     relay,
     land,
     zland,
-    total,
     copied,
     core_send,
     core_recv,
@@ -1038,7 +1037,7 @@
         return pltpu.make_async_copy(y_ref.at[sequence(t)], ybuf.at[t % 2], copied.at[t % 2])
 
     def to_core(p):
-        return remote(stage.at[p], given.at[p], core_send.at[p], core_recv.at[p], c_peer)
+        return remote(stage.at[p % 2], given.at[p], core_send.at[p], core_recv.at[p], c_peer)
 
     units = 3
     unit = tall // units
@@ -1061,14 +1060,25 @@
     y_top = [over(u, 5, sums.at[2, top(u)], land.at[1, top(u)], y_peer) for u in range(units)]
 
     in_copy(0).start()
-    passed_ref[...] = forward_ref[...]
     start, share, give_back, end = weight_sum(grads, *more[:3], sum_ref, *more[3:])
-    at = 0
-    for ref in (shared_gate_ref, shared_up_ref, shared_down_ref):
-        grads[at : at + ref.shape[0]] = ref[...]
-        at += ref.shape[0]
-    grads[at:] = jnp.zeros((grads.shape[0] - at, grads.shape[1]), bf16)
-    start()
+
+    def shared_expert():
+        normed, grad_t = normed_ref[...], grad_ref[...]
+        size = gate_ref.shape[0]
+        gate, up = nt(gate_ref[...], normed), nt(up_ref[...], normed)
+        sig = 1.0 / (1.0 + jnp.exp(-gate))
+        act = gate * sig
+        hidden = (act * up).astype(bf16)
+        forward_ref[...] = tn(hidden, down_ref[...]).astype(bf16)
+        grad_hidden = nn(down_ref[...], grad_t)
+        grad_gate = (grad_hidden * up * sig * (1.0 + gate * (1.0 - sig))).astype(bf16)
+        grad_up = (grad_hidden * act).astype(bf16)
+        grads[:size] = nn(grad_gate, normed).astype(bf16)
+        grads[size : 2 * size] = nn(grad_up, normed).astype(bf16)
+        grads[2 * size : 3 * size] = nt(hidden, grad_t).astype(bf16)
+        grads[3 * size :] = jnp.zeros((grads.shape[0] - 3 * size, grads.shape[1]), bf16)
+        start()
+        mine[...] = (tn(grad_gate, gate_ref[...]) + tn(grad_up, up_ref[...])).astype(bf16)
 
     def step(t, carry):
         @pl.when(t < 7)
@@ -1088,9 +1098,13 @@
 
         @pl.when(t % 2 == 0)
         def _():
-            stage[p, :rows] = back.astype(bf16)
-            stage[p, rows:] = jnp.zeros((tall - rows, back.shape[1]), bf16)
-            stage[p, rows:, :rows] = probs.astype(bf16)
+            @pl.when(p >= 2)
+            def _():
+                to_core(p - 2).wait_send()
+
+            stage[p % 2, :rows] = back.astype(bf16)
+            stage[p % 2, rows:] = jnp.zeros((tall - rows, back.shape[1]), bf16)
+            stage[p % 2, rows:, :rows] = probs.astype(bf16)
             to_core(p).start()
 
         @pl.when(t % 2 == 1)
@@ -1137,7 +1151,7 @@
     scatter = [
         [
             remote(
-                total.at[block_of(u, (z + i) % 4)],
+                sums.at[3, block_of(u, (z + i) % 4)],
                 zland.at[u, i - 1],
                 *z_sems(u, i - 1),
                 z_peers[i - 1],
@@ -1158,16 +1172,16 @@
         added = sums[3, at].astype(f32) + land[0, at].astype(f32) + land[1, at].astype(f32)
         ours = min(rows, (u + 1) * unit) - u * unit
         if ours == unit:
-            total[at] = (added + mine_ref[at].astype(f32)).astype(bf16)
+            sums[3, at] = (added + mine[at].astype(f32)).astype(bf16)
         else:
             here = slice(u * unit, u * unit + ours)
-            total[here] = (added[:ours] + mine_ref[here].astype(f32)).astype(bf16)
-            total[u * unit + ours : (u + 1) * unit] = added[ours:].astype(bf16)
+            sums[3, here] = (added[:ours] + mine[here].astype(f32)).astype(bf16)
+            sums[3, u * unit + ours : (u + 1) * unit] = added[ours:].astype(bf16)
         for i in (1, 0, 2):
             scatter[u][i].start()
 
     def summed(u):
-        done = total[block_of(u, z)].astype(f32)
+        done = sums[3, block_of(u, z)].astype(f32)
         for i in range(3):
             scatter[u][i].wait_recv()
             done = done + zland[u, i].astype(f32)
@@ -1180,6 +1194,7 @@
     y_low[1].start()
     far_top[2].start()
     far_low[2].start()
+    shared_expert()
     relayed(1)
     x_top[2].start()
     y_low[2].start()
@@ -1201,11 +1216,11 @@
             copy.wait_send()
         for i in (1, 2, 3):
             back_copy(u, z, i).wait_send()
-    for p in range(4):
+    for p in (2, 3):
         to_core(p).wait_send()
 
 
-def collect_sum(y, slot, gsw, mine, forward, *shared):
+def collect_sum(y, slot, gsw, normed, grad_t, *shared):
     s, local, cap, width = y.shape
     rows = slot.shape[2]
     tall = rows + EXTRA
@@ -1219,18 +1234,18 @@
         out_shape=[
             jax.ShapeDtypeStruct((tall, width), bf16),
             jax.ShapeDtypeStruct((weights, width), bf16),
-            jax.ShapeDtypeStruct(forward.shape, bf16),
+            jax.ShapeDtypeStruct((rows, width), bf16),
         ],
         scratch_shapes=[
+            pltpu.VMEM((rows, width), bf16),
             pltpu.VMEM((local * cap, rows), bf16),
             pltpu.VMEM((2, local, cap, width), bf16),
-            pltpu.VMEM((4, tall, width), bf16),
+            pltpu.VMEM((2, tall, width), bf16),
             pltpu.VMEM((4, tall, width), bf16),
             pltpu.VMEM((4, tall, width), bf16),
             pltpu.VMEM((3, 2, tall // 6, width), bf16),
             pltpu.VMEM((2, tall, width), bf16),
             pltpu.VMEM((3, 3, tall // 12, width), bf16),
-            pltpu.VMEM((tall, width), bf16),
             dma((2,)),
             dma((4,)),
             dma((4,)),
@@ -1245,7 +1260,7 @@
         ),
         cost_estimate=takes(131),
         name="collect_sum",
-    )(y, slot, gsw, mine, *shared, forward)
+    )(y, slot, gsw, normed, grad_t, *shared)
 
 
 def back_kernel(
@@ -1271,10 +1286,14 @@
     gain_ref,
     tokens_ref,
     early_ref,
-    late_ref,
+    first_ref,
+    second_ref,
+    shared_ref,
     dq_ref,
     dk_ref,
     dv_ref,
+    x_t,
+    gain_column,
     back_t,
     low_t,
     part,
@@ -1293,8 +1312,13 @@
     c_peer = (chip, 1 - core, z)
     z_peers = [(chip, core, (z + i) % 4) for i in (1, 2, 3)]
     quarter, width = wq_ref.shape
-    rows = x_ref.shape[1]
-    early, late = more[0], more[8]
+    rows = x_ref.shape[0]
+    groups = [
+        weight_sum(*more[8 * i : 8 * i + 4], ref, *more[8 * i + 4 : 8 * i + 8])
+        for i, ref in enumerate((early_ref, first_ref, second_ref, shared_ref))
+    ]
+    early, *by_head = [more[8 * i] for i in range(4)]
+    START, SHARE, GIVE_BACK, END = range(4)
     experts = router_ref.shape[0]
     whole = HEAD_DIM * (quarter // HEAD_DIM)
     spare = quarter - whole
@@ -1312,7 +1336,7 @@
     residual = residual_ref[...]
     rms2 = lax.rsqrt(jnp.sum(residual * residual, axis=-1, keepdims=True) * (1.0 / width) + EPS)
     grad_ffn = jnp.sum(grad_normed2 * residual * rms2, axis=0, keepdims=True)
-    u = grad_normed2 * ffn_gain_ref[...]
+    u = grad_normed2 * ffn_gain_ref[1:2]
     mean2 = jnp.sum(u * residual, axis=-1, keepdims=True) * (1.0 / width)
     added = rms2 * u - residual * (rms2 * rms2 * rms2 * mean2)
     back_t[...] = added.T + grad_ref[...].astype(f32)
@@ -1320,8 +1344,8 @@
     own = block(z, quarter)
     early[:quarter] = nt(low_t[own], attended_ref[...]).astype(bf16)
     early[quarter:] = grad_router.astype(bf16)
-    start, share, give_back, end = weight_sum(early, *more[1:4], early_ref, *more[4:8])
-    start()
+    groups[0][START]()
+    normed = normed_ref[...]
 
     cosine, sine = cos_ref[...], sin_ref[...]
     half_dim = HEAD_DIM // 2
@@ -1345,17 +1369,23 @@
         grad_s = (probs * (grad_p - delta)).astype(bf16)
         grad_q = turn_back(nt(k_ref[h], grad_s))
         grad_k = turn_back(nn(q_ref[h], grad_s))
-        for ref, value in ((dq_ref, grad_q), (dk_ref, grad_k), (dv_ref, grad_v)):
+        for i, (ref, value) in enumerate(((dq_ref, grad_q), (dk_ref, grad_k), (dv_ref, grad_v))):
             if h < heads:
-                at = pl.ds(pl.multiple_of(odd * spare + h * HEAD_DIM, 16), HEAD_DIM)
-                ref[at] = value
+                size = HEAD_DIM
+                at = pl.ds(pl.multiple_of(odd * spare + h * HEAD_DIM, 16), size)
             else:
-                at = pl.ds(pl.multiple_of((1 - odd) * whole, 16), spare)
-                ref[at] = jnp.where(odd == 1, value[spare:], value[:spare])
-        if h == 0:
-            share()
-
-    x_all = x_ref[...].astype(f32)
+                size = spare
+                at = pl.ds(pl.multiple_of((1 - odd) * whole, 16), size)
+                value = jnp.where(odd == 1, value[spare:], value[:spare])
+            ref[at] = value
+            by_head[h][i * size : (i + 1) * size] = nn(value, normed).astype(bf16)
+        if h < heads:
+            groups[1 + h][START]()
+            groups[h][SHARE]()
+
+    x_t[...] = x_ref[...].T
+    gain_column[...] = jnp.broadcast_to(gain_ref[0:1], (8, width)).T
+    x_all = x_t[...].astype(f32)
     rms1 = lax.rsqrt(jnp.sum(x_all * x_all, axis=0, keepdims=True) * (1.0 / width) + EPS)
     part[...] = tn(wq_ref[...], dq_ref[...])
     part[...] += tn(wk_ref[...], dk_ref[...])
@@ -1374,20 +1404,17 @@
     few_to_z = [
         remote(mine, theirs.at[i], lsend.at[i], lrecv.at[i], peer) for i, peer in enumerate(z_peers)
     ]
-    along = part[...] * x_ref[...].astype(f32)
+    along = part[...] * x_t[...].astype(f32)
     mine[...] = jnp.zeros(mine.shape, f32)
-    mine[0:1, :rows] = jnp.sum(along * gain_ref[...], axis=0, keepdims=True)
+    mine[0:1, :rows] = jnp.sum(along * gain_column[:, 0:1], axis=0, keepdims=True)
     mine[:, rows:] = nt(jnp.ones((8, rows), bf16), (along * rms1).astype(bf16))
     for copy in few_to_z:
         copy.start()
     for i in (1, 0, 2):
         to_z[i].start()
 
-    give_back()
-    normed = normed_ref[...]
-    for i, ref in enumerate((dq_ref, dk_ref, dv_ref)):
-        late[i * quarter : (i + 1) * quarter] = nn(ref[...], normed).astype(bf16)
-    at = 3 * quarter
+    at = 3 * spare
+    late = by_head[heads]
     for copy in few_to_z:
         copy.wait_recv()
     few = mine[...] + theirs[0] + theirs[1] + theirs[2]
@@ -1395,22 +1422,24 @@
     line = lax.broadcasted_iota(jnp.int32, (16, width), 0)
     gains = jnp.where(line == 0, few[0:1, rows:], jnp.where(line == 1, grad_ffn, 0.0))
     late[at : at + 16] = gains.astype(bf16)
-
-    start, share, give_back, end_late = weight_sum(late, *more[9:12], late_ref, *more[12:16])
-    start()
-    share()
+    groups[3][START]()
+    groups[2][SHARE]()
+    groups[0][GIVE_BACK]()
+    groups[3][SHARE]()
+    groups[1][GIVE_BACK]()
 
     total = part[own]
     for i in range(3):
         to_z[i].wait_recv()
         total = total + zland[i].astype(f32)
-    x = x_ref[own].astype(f32)
+    x = x_t[own].astype(f32)
     mean = few[0:1, :rows] * (1.0 / width)
-    tokens_ref[...] = back_t[own] + rms1 * gain_ref[own] * total - x * (rms1 * rms1 * rms1 * mean)
-
-    give_back()
-    end()
-    end_late()
+    tokens_ref[...] = back_t[own] + rms1 * gain_column[own, 0:1] * total - x * (rms1 * rms1 * rms1 * mean)
+
+    groups[2][GIVE_BACK]()
+    groups[3][GIVE_BACK]()
+    for group in groups:
+        group[END]()
     for copy in (*to_z, *few_to_z):
         copy.wait_send()
 
@@ -1418,20 +1447,22 @@
 def back(*args):
     quarter, width = args[13].shape
     rows = args[1].shape[0]
-    early, late = quarter + args[4].shape[0], 128 * (3 * quarter // 128 + 1)
+    spare = quarter % HEAD_DIM
+    tall = [quarter + args[4].shape[0], 3 * HEAD_DIM, 3 * HEAD_DIM, 3 * spare + 64]
     vmem = pl.BlockSpec(memory_space=pltpu.VMEM)
     dma = pltpu.SemaphoreType.DMA
     return pl.pallas_call(
         back_kernel,
         in_specs=[vmem] * len(args),
-        out_specs=[vmem] * 3,
+        out_specs=[vmem] * 5,
         out_shape=[
             jax.ShapeDtypeStruct((quarter, rows), f32),
-            jax.ShapeDtypeStruct((early, width), bf16),
-            jax.ShapeDtypeStruct((late, width), bf16),
+            *[jax.ShapeDtypeStruct((lines, width), bf16) for lines in tall],
         ],
         scratch_shapes=[
             *[pltpu.VMEM((quarter, rows), bf16)] * 3,
+            pltpu.VMEM((width, rows), bf16),
+            pltpu.VMEM((width, 8), f32),
             pltpu.VMEM((width, rows), f32),
             pltpu.VMEM((width, rows), bf16),
             pltpu.VMEM((width, rows), f32),
@@ -1443,8 +1474,7 @@
             dma((3,)),
             dma((3,)),
             dma((3,)),
-            *weight_sum_scratch(early, width),
-            *weight_sum_scratch(late, width),
+            *[one for lines in tall for one in weight_sum_scratch(lines, width)],
         ],
         compiler_params=pltpu.CompilerParams(
             vmem_limit_bytes=VMEM_LIMIT, collective_id=3, has_side_effects=True
@@ -1454,33 +1484,40 @@
     )(*args)
 
 
-def widen_kernel(early_ref, late_ref, shared_ref, *out_refs):
+def widen_kernel(early_ref, first_ref, second_ref, last_ref, shared_ref, *out_refs):
     quarter = out_refs[0].shape[0]
+    odd = lax.axis_index("hs") % 2
+    whole = HEAD_DIM * (quarter // HEAD_DIM)
+    spare = quarter - whole
     for i in range(3):
-        out_refs[i][...] = late_ref[i * quarter : (i + 1) * quarter].astype(f32)
+        for h, ref in enumerate((first_ref, second_ref)):
+            at = pl.ds(pl.multiple_of(odd * spare + h * HEAD_DIM, 8), HEAD_DIM)
+            out_refs[i][at] = ref[i * HEAD_DIM : (i + 1) * HEAD_DIM].astype(f32)
+        at = pl.ds(pl.multiple_of((1 - odd) * whole, 8), spare)
+        out_refs[i][at] = last_ref[i * spare : (i + 1) * spare].astype(f32)
     out_refs[3][...] = early_ref[:quarter].astype(f32)
     out_refs[4][...] = early_ref[quarter:].astype(f32)
-    out_refs[5][...] = late_ref[3 * quarter : 3 * quarter + 8].astype(f32)
+    out_refs[5][...] = last_ref[3 * spare : 3 * spare + 16].astype(f32)
     size = out_refs[6].shape[0]
     for i in range(3):
         out_refs[6 + i][...] = shared_ref[i * size : (i + 1) * size].astype(f32)
 
 
-def widen(early, late, shared, quarter, hidden_units):
-    width = early.shape[1]
+def widen(sums, quarter, hidden_units):
+    width = sums[0].shape[1]
     step = width // 5
-    tall = [quarter] * 4 + [early.shape[0] - quarter, 8] + [hidden_units] * 3
+    tall = [quarter] * 4 + [sums[0].shape[0] - quarter, 16] + [hidden_units] * 3
     blocks = lambda lines: pl.BlockSpec((lines, step), lambda i: (0, i))
     return pl.pallas_call(
         widen_kernel,
         grid=(width // step,),
-        in_specs=[blocks(a.shape[0]) for a in (early, late, shared)],
+        in_specs=[blocks(a.shape[0]) for a in sums],
         out_specs=[blocks(lines) for lines in tall],
         out_shape=[jax.ShapeDtypeStruct((lines, width), f32) for lines in tall],
         compiler_params=pltpu.CompilerParams(vmem_limit_bytes=VMEM_LIMIT),
         cost_estimate=takes(8),
         name="widen",
-    )(early, late, shared)
+    )(*sums)
 
 
 def plain_front(
@@ -1658,8 +1695,9 @@
     tables = rope_tables(rows)
 
     if small:
+        both_gains = jnp.stack([attn_gain, ffn_gain])
         ahead = front(
-            tokens, attn_gain, query_t, key_t, value_t, attn_out.T, ffn_gain, documents, tables
+            tokens, both_gains, query_t, key_t, value_t, attn_out.T, documents, tables
         )
     else:
         ahead = plain_front(
@@ -1696,35 +1734,17 @@
         ex_in, ex_grad, ex_gate, ex_up, slot_weight, *weights
     )
 
-    sh_gate = dot(normed2, shared_gate)
-    sh_up = dot(normed2, shared_up)
-    sh_sig = jax.nn.sigmoid(sh_gate)
-    sh_act = sh_gate * sh_sig
-    sh_hidden = (sh_act * sh_up).astype(bf16)
-    shared_part = dot(sh_hidden, shared_down)
-    grad_sh = ein("dt,fd->tf", grad_t, shared_down)
-    grad_sh_gate = (grad_sh * sh_up * sh_sig * (1 + sh_gate * (1 - sh_sig))).astype(bf16)
-    grad_sh_up = (grad_sh * sh_act).astype(bf16)
-    shared_grads = [
-        ein("tf,td->fd", grad_sh_gate, normed2).astype(bf16),
-        ein("tf,td->fd", grad_sh_up, normed2).astype(bf16),
-        ein("tf,dt->fd", sh_hidden, grad_t).astype(bf16),
-    ]
-    shared_back = ein("tf,df->td", grad_sh_gate, shared_gate) + ein(
-        "tf,df->td", grad_sh_up, shared_up
-    )
-
     if small:
         back_sums, shared_sums, shared_part = collect_sum(
-            ex_back, slot, grad_slot_weight, shared_back.astype(bf16), shared_part.astype(bf16), *shared_grads
+            ex_back, slot, grad_slot_weight, normed2, grad_t, shared_gate.T, shared_up.T, shared_down
         )
-        grad_tokens, early, late = back(
+        grad_tokens, *sums = back(
             back_sums,
             residual,
             normed2,
             grad_t,
             router_t,
-            ffn_gain[None, :],
+            both_gains,
             out_t,
             q,
             k,
@@ -1736,15 +1756,32 @@
             value_t,
             normed1,
             attended_t,
-            tokens.T,
-            attn_gain[:, None],
+            tokens,
+            both_gains,
         )
         *heads_sums, grad_router, gains, sum_gate, sum_up, sum_down = widen(
-            early, late, shared_sums, quarter, shared_down.shape[0]
+            [*sums, shared_sums], quarter, shared_down.shape[0]
         )
         shared_sums = sum_gate, sum_up, sum_down
         grad_attn_gain, grad_ffn_gain = gains[0], gains[1]
     else:
+        sh_gate = dot(normed2, shared_gate)
+        sh_up = dot(normed2, shared_up)
+        sh_sig = jax.nn.sigmoid(sh_gate)
+        sh_act = sh_gate * sh_sig
+        sh_hidden = (sh_act * sh_up).astype(bf16)
+        shared_part = dot(sh_hidden, shared_down)
+        grad_sh = ein("dt,fd->tf", grad_t, shared_down)
+        grad_sh_gate = (grad_sh * sh_up * sh_sig * (1 + sh_gate * (1 - sh_sig))).astype(bf16)
+        grad_sh_up = (grad_sh * sh_act).astype(bf16)
+        shared_grads = [
+            ein("tf,td->fd", grad_sh_gate, normed2).astype(bf16),
+            ein("tf,td->fd", grad_sh_up, normed2).astype(bf16),
+            ein("tf,dt->fd", sh_hidden, grad_t).astype(bf16),
+        ]
+        shared_back = ein("tf,df->td", grad_sh_gate, shared_gate) + ein(
+            "tf,df->td", grad_sh_up, shared_up
+        )
         back_part = collect(ex_back, slot, grad_slot_weight, first, experts).reshape(-1, width)
         back_rows = lax.psum_scatter(back_part, EP, scatter_dimension=0, tiled=True).astype(f32)
         back_rows = jnp.concatenate([back_rows[:rows] + shared_back, back_rows[rows:]], axis=0)

time: 506 us -> 483 us (0.955)
  matrix products: 13.6 us -> 0.91 us
  Pallas kernels: 451 us -> 444 us
  local copies, waits for them, and re-layouts: 14 us -> 7.45 us
    dot_general x6 -> x0, matrix products: 8.92 us -> none  [ein(): return jnp.einsum(spec, a, b, preferred_element_type=f32)]
    pallas_call x1, Pallas kernels: 86.3 us -> 78.9 us  [back(): pl.pallas_call(back_kernel, in_specs=[vmem] * len(args), out_specs=[vmem]...]
  transfers between devices with their start and end apart: 2 -> 2, of which waited for: 0 -> 0; matrix products, arithmetic and copies ran while one was open for 3% -> 0% of each run, Pallas kernels for 55% -> 57%
where the time goes in v2:
time: 483 us; the launch traced here: 474 us
  Pallas kernels  444 us (92%)
  between operations  14.4 us (3%)
  local copies, waits for them, and re-layouts  7.45 us (2%)
  other arithmetic  6.6 us (1%)
    pallas_call x1, Pallas kernels, collect_sum(): pl.pallas_call(collect_sum_kernel, in_specs=[pl.BlockSpec(memory_space=pl...  116 us
    pallas_call x1, Pallas kernels, back(): pl.pallas_call(back_kernel, in_specs=[vmem] * len(args), out_specs=[vmem]...  78.9 us
    pallas_call x1, Pallas kernels, gather_spread(): pl.pallas_call(gather_spread_kernel, in_specs=[vmem] * 4, out_specs=[pl.B...  61.5 us
    pallas_call x1, Pallas kernels, front(): pl.pallas_call(front_kernel, in_specs=[vmem] * 9, out_specs=[vmem] * 9, o...  55.1 us
    pallas_call x1, Pallas kernels, experts_backward(): pl.pallas_call(functools.partial(experts_backward_kernel, groups), grid=(...  47.3 us
    pallas_call x1, Pallas kernels, experts_forward(): pl.pallas_call(kernel, grid=(local, groups), in_specs=in_specs, out_specs...  35.4 us
    pallas_call x1, Pallas kernels, collect_sending(): pl.pallas_call(collect_sending_kernel, grid=(s,), in_specs=[pl.BlockSpec(...  23.2 us
    pallas_call x1, Pallas kernels, spread_grad(): pl.pallas_call(spread_grad_kernel, in_specs=[whole] * 4 + [pl.BlockSpec(m...  18.1 us
  transfers between devices with their start and end apart: 2, of which 0 were waited for; matrix products, arithmetic and copies ran while one was open for 0% of the time, Pallas kernels for 57%

profile of v2, /device:TPU:9, one launch (start us, length us, event | category | flops | bytes accessed | tf_op | source)
XLA Modules:
  0.0 474.1 jit_solution(10797225870548046056)
XLA Ops:
  7.2 0.0 reduce-scatter.5.cloned.1.call-start
  7.3 0.7 stack.9
  8.0 0.7 stack.10
  8.7 0.8 fusion.1
  9.5 0.9 fusion.slots_ref
  10.4 0.6 pad_maximum_fusion.gain_ref.ffn_gain_ref
  11.0 1.6 fusion.2.router_ref
  12.7 55.1 %front.1 = (bf16[512,1280]{1,0:T(8,128)(2,1)}, bf16[3,128,512]{2,1,0:T(8,128)(2,1)}, bf16[3,128,512]{2,1,0:T(8,128)(2,1)}, bf16[3,128,512]{2,1,0:T(8,128)(2,1)},...) custom-call(bf16[512,1280]{1,0:T(8,128)(2,1)} %x_ref.3, ...), custom_call_target="tpu_custom_call" | custom-call | bytes 150000000 | tf_op jit(solution)/shard_map/front/pallas_call | solution.py:953
  67.8 61.5 %gather_spread.1 = (bf16[8,8,112,1280]{3,2,1,0:T(8,128)(2,1)}, f32[8,896,1]{2,1,0:T(8,128)}, s32[8,8,512]{2,1,0:T(8,128)}, bf16[1280,512]{1,0:T(8,128)(2,1)}) custom-call(bf16[512,1280]{1,0:T(8,128)(2,1)} %get-tuple-element.58.own_ref.normed_ref.normed2_ref, bf16[64,512]{1,0:T(8,128)(2,1)} %fusion.slots_ref, bf16[64,1280]{1,0:T(8,128)(2,1)} %fusion.2.router_ref, ...), custom_call_target="tpu_custom_call" | custom-call | bytes 186000000 | tf_op jit(solution)/shard_map/gather_spread/pallas_call | solution.py:738
  129.3 35.4 %experts_forward.1 = (bf16[8,8,112,1280]{3,2,1,0:T(8,128)(2,1)}, f32[8,896,256]{2,1,0:T(8,128)}, f32[8,896,256]{2,1,0:T(8,128)}, bf16[2,1280,512]{2,1,0:T(8,128)(2,1)}) custom-call(bf16[8,8,112,1280]{3,2,1,0:T(8,128)(2,1)} %get-tuple-element.59.x_ref, f32[8,896,1]{2,1,0:T(8,128)} %get-tuple-element.60.sw_ref, bf16[8,224,1280]{2,1,0:T(8,128)(2,1)} %bitcast.27, ...), custom_call_target="tpu_custom_call" | custom-call | bytes 93000000 | tf_op jit(solution)/shard_map/experts_forward/pallas_call | solution.py:289
  164.6 23.2 %collect_sending.1 = (bf16[8,512,1280]{2,1,0:T(8,128)(2,1)}, bf16[1280,512]{1,0:T(8,128)(2,1)}, bf16[4,1280,512]{2,1,0:T(8,128)(2,1)}) custom-call(bf16[8,8,112,1280]{3,2,1,0:T(8,128)(2,1)} %get-tuple-element.62.y_ref, s32[8,8,512]{2,1,0:T(8,128)} %get-tuple-element.63.slot_ref, bf16[1280,512]{1,0:T(8,128)(2,1)} %get-tuple-element.61.grad_ref, ...), custom_call_target="tpu_custom_call" | custom-call | bytes 60000000 | tf_op jit(solution)/shard_map/collect_sending/pallas_call | solution.py:386
  187.9 0.2 reduce-scatter.7.cloned.1.call-start
  188.1 18.1 %spread_grad.1.gx_ref = bf16[8,8,112,1280]{3,2,1,0:T(8,128)(2,1)} custom-call(bf16[1280,512]{1,0:T(8,128)(2,1)} %get-tuple-element.61.grad_ref, bf16[2,1280,512]{2,1,0:T(8,128)(2,1)} %get-tuple-element.64.near_ref, bf16[1280,512]{1,0:T(8,128)(2,1)} %get-tuple-element.66.far_ref, bf16[4,1280,512]{2,1,0:T(8,128)(2,1)} %get-tuple-element.67.given_ref, ...), custom_call_target="tpu_custom_call" | custom-call | bytes 48000000 | tf_op jit(solution)/shard_map/spread_grad/pallas_call | solution.py:451
  206.2 47.3 %experts_backward.1 = (bf16[8,8,112,1280]{3,2,1,0:T(8,128)(2,1)}, f32[8,224,1280]{2,1,0:T(8,128)}, f32[8,224,1280]{2,1,0:T(8,128)}, f32[8,224,1280]{2,1,0:T(8,128)}, f32[8,896,1]{2,1,0:T(8,128)}) custom-call(bf16[8,8,112,1280]{3,2,1,0:T(8,128)(2,1)} %get-tuple-element.59.x_ref, bf16[8,8,112,1280]{3,2,1,0:T(8,128)(2,1)} %spread_grad.1.gx_ref, ...), custom_call_target="tpu_custom_call" | custom-call | bytes 141000000 | tf_op jit(solution)/shard_map/experts_backward/pallas_call | solution.py:307
  253.5 116.1 %collect_sum.1 = (bf16[576,1280]{1,0:T(8,128)(2,1)}, bf16[1408,1280]{1,0:T(8,128)(2,1)}, bf16[512,1280]{1,0:T(8,128)(2,1)}) custom-call(bf16[8,8,112,1280]{3,2,1,0:T(8,128)(2,1)} %get-tuple-element.70.y_ref, s32[8,8,512]{2,1,0:T(8,128)} %get-tuple-element.63.slot_ref, f32[8,896,1]{2,1,0:T(8,128)} %get-tuple-element.71.gsw_ref, ...), custom_call_target="tpu_custom_call" | custom-call | bytes 393000000 | tf_op jit(solution)/shard_map/collect_sum/pallas_call | solution.py:1230
  369.6 2.0 add_convert_fusion
  371.6 1.6 copy.39
  373.3 78.9 %back.1 = (f32[320,512]{1,0:T(8,128)}, bf16[384,1280]{1,0:T(8,128)(2,1)}, bf16[384,1280]{1,0:T(8,128)(2,1)}, bf16[384,1280]{1,0:T(8,128)(2,1)}, bf16[256,1280]{1,0:T(8,128)(2,1)}) custom-call(bf16[576,1280]{1,0:T(8,128)(2,1)} %get-tuple-element.73.sums_ref, f32[512,1280]{1,0:T(8,128)} %get-tuple-element.57.residual_ref, ...), custom_call_target="tpu_custom_call" | custom-call | bytes 270000000 | tf_op jit(solution)/shard_map/back/pallas_call | solution.py:1454
  452.3 8.9 %widen.1 = (f32[320,1280]{1,0:T(8,128)}, f32[320,1280]{1,0:T(8,128)}, f32[320,1280]{1,0:T(8,128)}, f32[320,1280]{1,0:T(8,128)}, f32[64,1280]{1,0:T(8,128)}, /*in...) custom-call(bf16[384,1280]{1,0:T(8,128)(2,1)} %get-tuple-element.82.early_ref, ...), custom_call_target="tpu_custom_call" | custom-call | bytes 24000000 | tf_op jit(solution)/shard_map/widen/pallas_call | solution.py:1511
  461.2 1.5 slice_reduce_fusion
  462.7 1.2 copy.40
  463.8 1.5 add_convert_fusion.1
  465.4 0.9 copy.38
  466.3 0.8 copy.42
  (6 shorter events, 0.1 us)
Async XLA Ops:
  7.2 362.4 %reduce-scatter.5.cloned.1.call-start = ((), (), s32[]{:S(2)}) async-start(), calls=%async_computation.2 | async-start | bytes 11796480 | tf_op jit(solution)/shard_map/reduce_scatter | solution.py:1814
  187.9 274.8 %reduce-scatter.7.cloned.1.call-start = ((), (), s32[]{:S(2)}) async-start(), calls=%async_computation.3 | async-start | bytes 1638400
  461.1 5.1 %copy-start = (f32[320,512]{1,0:T(8,128)S(1)}, f32[320,512]{1,0:T(8,128)}, u32[]{:S(2)}) copy-start(f32[320,512]{1,0:T(8,128)} %get-tuple-element.81) | copy-start | bytes 1966084
Sparse Core Ops, SparseCore 0:
  188.0 80.0 reduce-scatter.4
  373.4 38.6 reduce-scatter.6

commit v3 on v2

--- a/solution.py
+++ b/solution.py
@@ -641,8 +641,10 @@
         )
 
     held[me, :rows] = own_ref[...]
-    held[me, rows:] = jnp.zeros((EXTRA, own_ref.shape[1]), bf16)
-    held[me, rows:, :rows] = slots_ref[...]
+    packed = tall - rows
+    held[me, rows:, 2 * rows :] = jnp.zeros((packed, own_ref.shape[1] - 2 * rows), bf16)
+    held[me, rows:, :rows] = slots_ref[:packed]
+    held[me, rows:, rows : 2 * rows] = slots_ref[packed:]
     x_top, x_low = move(0, me, top, x_peer), move(1, me, low, x_peer)
     y_low, y_top = move(2, me, low, y_peer), move(3, me, top, y_peer)
     to_core = move(4, me, whole, c_peer)
@@ -701,7 +703,9 @@
 
         x, y = (chip % 2 + (t // 2) % 2) % 2, (chip // 2 + t // 4) % 2
         src = (y * 2 + x) * 2 + (core + t % 2) % 2
-        slots = nn(chosen, held[src, rows:, :rows]).astype(jnp.int32)
+        slots = nn(chosen[:, :packed], held[src, rows:, :rows])
+        slots += nn(chosen[:, packed:], held[src, rows:, rows : 2 * rows])
+        slots = slots.astype(jnp.int32)
         slot_ref[src] = slots
         logits = nt(router_ref[...], held[src, :rows])
         raised = jnp.exp(logits - jnp.max(logits, axis=0, keepdims=True))
@@ -733,7 +737,7 @@
 
 def gather_spread(own, slots, router_t, grad_quarter, local, ep_count):
     rows, width = own.shape
-    tall = rows + EXTRA
+    tall = rows + EXTRA // 2
     vmem = pl.BlockSpec(memory_space=pltpu.VMEM)
     return pl.pallas_call(
         gather_spread_kernel,
@@ -773,6 +777,15 @@
     doc_ref,
     cos_ref,
     sin_ref,
+    normed1_out,
+    q_out,
+    k_out,
+    v_out,
+    probs_out,
+    attended_out,
+    out_out,
+    residual_ref,
+    normed2_ref,
     normed1_ref,
     q_ref,
     k_ref,
@@ -780,8 +793,7 @@
     probs_ref,
     attended_ref,
     out_ref,
-    residual_ref,
-    normed2_ref,
+    gone,
     shared,
     beside,
     esend,
@@ -857,6 +869,11 @@
     doc = jnp.broadcast_to(doc_ref[...].astype(f32), (rows, rows))
     allowed = (row >= column) & (doc == doc.T)
 
+    kept = (normed1_ref, q_ref, k_ref, v_ref, probs_ref, attended_ref, out_ref)
+    outs = (normed1_out, q_out, k_out, v_out, probs_out, attended_out, out_out)
+    writes = [pltpu.make_async_copy(a, b, gone.at[i]) for i, (a, b) in enumerate(zip(kept, outs))]
+    writes[0].start()
+
     def turn(pre):
         a, b = pre[:half_dim], pre[half_dim:]
         return (
@@ -910,6 +927,8 @@
         both = jnp.concatenate([first, second], axis=0)
         to[heads] = both.astype(bf16) if to is v_ref else turn(both)
     last = attend(heads)
+    for i in (1, 2, 3, 4):
+        writes[i].start()
     last = jnp.where(odd == 1, last[spare:], last[:spare])
     start = mine + (1 - odd) * whole
     attended_ref[pl.ds(pl.multiple_of(start, 16), spare)] = last
@@ -929,11 +948,15 @@
             attended_copy(h, from_z * quarter + from_odd * spare + h * HEAD_DIM, HEAD_DIM)(i).wait_recv()
         attended_copy(heads, from_z * quarter + (1 - from_odd) * whole, spare)(i).wait_recv()
         out_core(i, other).wait_recv()
+    writes[5].start()
+    writes[6].start()
     attended = attended_ref[...].T
     residual = x_ref[...].astype(f32) + nt(attended, out_ref[...].reshape(width, width))
     residual_ref[...] = residual
     rms2 = lax.rsqrt(jnp.sum(residual * residual, axis=-1, keepdims=True) * (1.0 / width) + EPS)
     normed2_ref[...] = (residual * rms2 * gain_ref[1:2]).astype(bf16)
+    for write in writes:
+        write.wait()
     for one in (trade, *out_z, *copies):
         one.wait_send()
     for i in range(3):
@@ -950,20 +973,21 @@
     vmem = pl.BlockSpec(memory_space=pltpu.VMEM)
     dma = pltpu.SemaphoreType.DMA
     low = lambda *shape: jax.ShapeDtypeStruct(shape, bf16)
+    early = [
+        low(rows, width),
+        *[low(heads, HEAD_DIM, rows)] * 3,
+        jax.ShapeDtypeStruct((heads, rows, rows), f32),
+        low(width, rows),
+        low(4, quarter, width),
+    ]
     return pl.pallas_call(
         front_kernel,
         in_specs=[vmem] * 9,
-        out_specs=[vmem] * 9,
-        out_shape=[
-            low(rows, width),
-            *[low(heads, HEAD_DIM, rows)] * 3,
-            jax.ShapeDtypeStruct((heads, rows, rows), f32),
-            low(width, rows),
-            low(4, quarter, width),
-            jax.ShapeDtypeStruct((rows, width), f32),
-            low(rows, width),
-        ],
+        out_specs=[pl.BlockSpec(memory_space=pl.ANY)] * len(early) + [vmem] * 2,
+        out_shape=[*early, jax.ShapeDtypeStruct((rows, width), f32), low(rows, width)],
         scratch_shapes=[
+            *[pltpu.VMEM(a.shape, a.dtype) for a in early],
+            dma((len(early),)),
             pltpu.VMEM((3 * spare, width), bf16),
             pltpu.VMEM((3 * spare, width), bf16),
             dma,
@@ -1269,21 +1293,53 @@
     normed2_ref,
     grad_ref,
     router_ref,
-    ffn_gain_ref,
+    gain_ref,
+    cos_ref,
+    sin_ref,
+    *refs,
+):
+    late, outs, rest = refs[:11], refs[11:16], refs[16:]
+    held, sems, rest = rest[:11], rest[11], rest[12:]
+    loads = [pltpu.make_async_copy(a, b, sems.at[i]) for i, (a, b) in enumerate(zip(late, held))]
+    for load in loads:
+        load.start()
+    back_steps(
+        loads,
+        sums_ref,
+        residual_ref,
+        normed2_ref,
+        grad_ref,
+        router_ref,
+        gain_ref,
+        cos_ref,
+        sin_ref,
+        *held,
+        *outs,
+        *rest,
+    )
+
+
+def back_steps(
+    loads,
+    sums_ref,
+    residual_ref,
+    normed2_ref,
+    grad_ref,
+    router_ref,
+    gain_ref,
+    cos_ref,
+    sin_ref,
     out_ref,
     q_ref,
     k_ref,
     v_ref,
     probs_ref,
-    cos_ref,
-    sin_ref,
     wq_ref,
     wk_ref,
     wv_ref,
-    normed_ref,
     attended_ref,
     x_ref,
-    gain_ref,
+    normed_ref,
     tokens_ref,
     early_ref,
     first_ref,
@@ -1336,16 +1392,12 @@
     residual = residual_ref[...]
     rms2 = lax.rsqrt(jnp.sum(residual * residual, axis=-1, keepdims=True) * (1.0 / width) + EPS)
     grad_ffn = jnp.sum(grad_normed2 * residual * rms2, axis=0, keepdims=True)
-    u = grad_normed2 * ffn_gain_ref[1:2]
+    u = grad_normed2 * gain_ref[1:2]
     mean2 = jnp.sum(u * residual, axis=-1, keepdims=True) * (1.0 / width)
     added = rms2 * u - residual * (rms2 * rms2 * rms2 * mean2)
     back_t[...] = added.T + grad_ref[...].astype(f32)
     low_t[...] = back_t[...].astype(bf16)
     own = block(z, quarter)
-    early[:quarter] = nt(low_t[own], attended_ref[...]).astype(bf16)
-    early[quarter:] = grad_router.astype(bf16)
-    groups[0][START]()
-    normed = normed_ref[...]
 
     cosine, sine = cos_ref[...], sin_ref[...]
     half_dim = HEAD_DIM // 2
@@ -1356,6 +1408,8 @@
         turned = [a * cosine + b * sine, b * cosine - a * sine]
         return jnp.concatenate(turned, axis=0).astype(bf16)
 
+    for i in range(5):
+        loads[i].wait()
     first_lane = z * quarter + odd * spare
     shared_lane = z * quarter + (1 - odd) * whole - odd * spare
     for h in range(heads + 1):
@@ -1369,24 +1423,16 @@
         grad_s = (probs * (grad_p - delta)).astype(bf16)
         grad_q = turn_back(nt(k_ref[h], grad_s))
         grad_k = turn_back(nn(q_ref[h], grad_s))
-        for i, (ref, value) in enumerate(((dq_ref, grad_q), (dk_ref, grad_k), (dv_ref, grad_v))):
+        for ref, value in ((dq_ref, grad_q), (dk_ref, grad_k), (dv_ref, grad_v)):
             if h < heads:
-                size = HEAD_DIM
-                at = pl.ds(pl.multiple_of(odd * spare + h * HEAD_DIM, 16), size)
+                at = pl.ds(pl.multiple_of(odd * spare + h * HEAD_DIM, 16), HEAD_DIM)
+                ref[at] = value
             else:
-                size = spare
-                at = pl.ds(pl.multiple_of((1 - odd) * whole, 16), size)
-                value = jnp.where(odd == 1, value[spare:], value[:spare])
-            ref[at] = value
-            by_head[h][i * size : (i + 1) * size] = nn(value, normed).astype(bf16)
-        if h < heads:
-            groups[1 + h][START]()
-            groups[h][SHARE]()
-
-    x_t[...] = x_ref[...].T
-    gain_column[...] = jnp.broadcast_to(gain_ref[0:1], (8, width)).T
-    x_all = x_t[...].astype(f32)
-    rms1 = lax.rsqrt(jnp.sum(x_all * x_all, axis=0, keepdims=True) * (1.0 / width) + EPS)
+                at = pl.ds(pl.multiple_of((1 - odd) * whole, 16), spare)
+                ref[at] = jnp.where(odd == 1, value[spare:], value[:spare])
+
+    for i in (5, 6, 7):
+        loads[i].wait()
     part[...] = tn(wq_ref[...], dq_ref[...])
     part[...] += tn(wk_ref[...], dk_ref[...])
     part[...] += tn(wv_ref[...], dv_ref[...])
@@ -1404,15 +1450,37 @@
     few_to_z = [
         remote(mine, theirs.at[i], lsend.at[i], lrecv.at[i], peer) for i, peer in enumerate(z_peers)
     ]
-    along = part[...] * x_t[...].astype(f32)
+    for i in (1, 0, 2):
+        to_z[i].start()
+    loads[8].wait()
+    loads[9].wait()
+    loads[10].wait()
+    early[:quarter] = nt(low_t[own], attended_ref[...]).astype(bf16)
+    early[quarter:] = grad_router.astype(bf16)
+    groups[0][START]()
+    x_t[...] = x_ref[...].T
+    gain_column[...] = jnp.broadcast_to(gain_ref[0:1], (8, width)).T
+    x_all = x_t[...].astype(f32)
+    rms1 = lax.rsqrt(jnp.sum(x_all * x_all, axis=0, keepdims=True) * (1.0 / width) + EPS)
+    along = part[...] * x_all
     mine[...] = jnp.zeros(mine.shape, f32)
     mine[0:1, :rows] = jnp.sum(along * gain_column[:, 0:1], axis=0, keepdims=True)
     mine[:, rows:] = nt(jnp.ones((8, rows), bf16), (along * rms1).astype(bf16))
     for copy in few_to_z:
         copy.start()
-    for i in (1, 0, 2):
-        to_z[i].start()
-
+
+    normed = normed_ref[...]
+    for h in range(heads + 1):
+        if h < heads:
+            size, at = HEAD_DIM, odd * spare + h * HEAD_DIM
+        else:
+            size, at = spare, (1 - odd) * whole
+        at = pl.ds(pl.multiple_of(at, 16), size)
+        for i, ref in enumerate((dq_ref, dk_ref, dv_ref)):
+            by_head[h][i * size : (i + 1) * size] = nn(ref[at], normed).astype(bf16)
+        if h < heads:
+            groups[1 + h][START]()
+            groups[h][SHARE]()
     at = 3 * spare
     late = by_head[heads]
     for copy in few_to_z:
@@ -1444,22 +1512,24 @@
         copy.wait_send()
 
 
-def back(*args):
-    quarter, width = args[13].shape
-    rows = args[1].shape[0]
+def back(now, late):
+    quarter, width = late[5].shape
+    rows = now[1].shape[0]
     spare = quarter % HEAD_DIM
-    tall = [quarter + args[4].shape[0], 3 * HEAD_DIM, 3 * HEAD_DIM, 3 * spare + 64]
+    tall = [quarter + now[4].shape[0], 3 * HEAD_DIM, 3 * HEAD_DIM, 3 * spare + 64]
     vmem = pl.BlockSpec(memory_space=pltpu.VMEM)
     dma = pltpu.SemaphoreType.DMA
     return pl.pallas_call(
         back_kernel,
-        in_specs=[vmem] * len(args),
+        in_specs=[vmem] * len(now) + [pl.BlockSpec(memory_space=pl.ANY)] * len(late),
         out_specs=[vmem] * 5,
         out_shape=[
             jax.ShapeDtypeStruct((quarter, rows), f32),
             *[jax.ShapeDtypeStruct((lines, width), bf16) for lines in tall],
         ],
         scratch_shapes=[
+            *[pltpu.VMEM(a.shape, a.dtype) for a in late],
+            dma((len(late),)),
             *[pltpu.VMEM((quarter, rows), bf16)] * 3,
             pltpu.VMEM((width, rows), bf16),
             pltpu.VMEM((width, 8), f32),
@@ -1481,7 +1551,7 @@
         ),
         cost_estimate=takes(90),
         name="back",
-    )(*args)
+    )(*now, *late)
 
 
 def widen_kernel(early_ref, first_ref, second_ref, last_ref, shared_ref, *out_refs):
@@ -1739,25 +1809,8 @@
             ex_back, slot, grad_slot_weight, normed2, grad_t, shared_gate.T, shared_up.T, shared_down
         )
         grad_tokens, *sums = back(
-            back_sums,
-            residual,
-            normed2,
-            grad_t,
-            router_t,
-            both_gains,
-            out_t,
-            q,
-            k,
-            v,
-            probs,
-            *tables,
-            query_t,
-            key_t,
-            value_t,
-            normed1,
-            attended_t,
-            tokens,
-            both_gains,
+            (back_sums, residual, normed2, grad_t, router_t, both_gains, *tables),
+            (out_t, q, k, v, probs, query_t, key_t, value_t, attended_t, tokens, normed1),
         )
         *heads_sums, grad_router, gains, sum_gate, sum_up, sum_down = widen(
             [*sums, shared_sums], quarter, shared_down.shape[0]

time: 483 us -> 493 us (1.021)
  Pallas kernels: 444 us -> 456 us
    pallas_call x2, Pallas kernels: 134 us -> 148 us  [the longest x1 96.4 us: back(): pl.pallas_call(back_kernel, in_specs=[vmem] * len(now) + [pl.BlockSpec(me...]
  transfers between devices with their start and end apart: 2 -> 2, of which waited for: 0 -> 0; matrix products, arithmetic and copies ran while one was open for 0% -> 0% of each run, Pallas kernels for 57% -> 59%
where the time goes in v3:
time: 493 us; the launch traced here: 486 us
  Pallas kernels  456 us (92%)
  between operations  14.4 us (3%)
  local copies, waits for them, and re-layouts  7.45 us (2%)
  other arithmetic  6.6 us (1%)
    pallas_call x1, Pallas kernels, collect_sum(): pl.pallas_call(collect_sum_kernel, in_specs=[pl.BlockSpec(memory_space=pl...  116 us
    pallas_call x1, Pallas kernels, back(): pl.pallas_call(back_kernel, in_specs=[vmem] * len(now) + [pl.BlockSpec(me...  96.4 us
    pallas_call x1, Pallas kernels, gather_spread(): pl.pallas_call(gather_spread_kernel, in_specs=[vmem] * 4, out_specs=[pl.B...  58.8 us
    pallas_call x1, Pallas kernels, front(): pl.pallas_call(front_kernel, in_specs=[vmem] * 9, out_specs=[pl.BlockSpec...  52.1 us
    pallas_call x1, Pallas kernels, experts_backward(): pl.pallas_call(functools.partial(experts_backward_kernel, groups), grid=(...  47.2 us
    pallas_call x1, Pallas kernels, experts_forward(): pl.pallas_call(kernel, grid=(local, groups), in_specs=in_specs, out_specs...  35.2 us
    pallas_call x1, Pallas kernels, collect_sending(): pl.pallas_call(collect_sending_kernel, grid=(s,), in_specs=[pl.BlockSpec(...  23.3 us
    pallas_call x1, Pallas kernels, spread_grad(): pl.pallas_call(spread_grad_kernel, in_specs=[whole] * 4 + [pl.BlockSpec(m...  18.1 us
  transfers between devices with their start and end apart: 2, of which 0 were waited for; matrix products, arithmetic and copies ran while one was open for 0% of the time, Pallas kernels for 59%

profile of v3, /device:TPU:9, one launch (start us, length us, event | category | flops | bytes accessed | tf_op | source)
XLA Modules:
  0.0 485.8 jit_solution(17763390725963327568)
XLA Ops:
  7.2 0.0 reduce-scatter.5.cloned.1.call-start
  7.3 0.7 stack.9
  8.0 0.7 stack.10
  8.7 0.8 fusion.1
  9.5 0.9 fusion.slots_ref
  10.4 0.6 pad_maximum_fusion.gain_ref
  11.0 1.6 fusion.2.router_ref
  12.7 52.1 %front.1 = (bf16[512,1280]{1,0:T(8,128)(2,1)}, bf16[3,128,512]{2,1,0:T(8,128)(2,1)}, bf16[3,128,512]{2,1,0:T(8,128)(2,1)}, bf16[3,128,512]{2,1,0:T(8,128)(2,1)},...) custom-call(bf16[512,1280]{1,0:T(8,128)(2,1)} %refs_9_.1, ...), custom_call_target="tpu_custom_call" | custom-call | bytes 150000000 | tf_op jit(solution)/shard_map/front/pallas_call | solution.py:983
  64.8 58.8 %gather_spread.1 = (bf16[8,8,112,1280]{3,2,1,0:T(8,128)(2,1)}, f32[8,896,1]{2,1,0:T(8,128)}, s32[8,8,512]{2,1,0:T(8,128)}, bf16[1280,512]{1,0:T(8,128)(2,1)}) custom-call(bf16[512,1280]{1,0:T(8,128)(2,1)} %get-tuple-element.58.own_ref.normed_ref.normed2_ref, bf16[64,512]{1,0:T(8,128)(2,1)} %fusion.slots_ref, bf16[64,1280]{1,0:T(8,128)(2,1)} %fusion.2.router_ref, ...), custom_call_target="tpu_custom_call" | custom-call | bytes 186000000 | tf_op jit(solution)/shard_map/gather_spread/pallas_call | solution.py:742
  123.6 35.2 %experts_forward.1 = (bf16[8,8,112,1280]{3,2,1,0:T(8,128)(2,1)}, f32[8,896,256]{2,1,0:T(8,128)}, f32[8,896,256]{2,1,0:T(8,128)}, bf16[2,1280,512]{2,1,0:T(8,128)(2,1)}) custom-call(bf16[8,8,112,1280]{3,2,1,0:T(8,128)(2,1)} %get-tuple-element.59.x_ref, f32[8,896,1]{2,1,0:T(8,128)} %get-tuple-element.60.sw_ref, bf16[8,224,1280]{2,1,0:T(8,128)(2,1)} %bitcast.27, ...), custom_call_target="tpu_custom_call" | custom-call | bytes 93000000 | tf_op jit(solution)/shard_map/experts_forward/pallas_call | solution.py:289
  158.8 23.3 %collect_sending.1 = (bf16[8,512,1280]{2,1,0:T(8,128)(2,1)}, bf16[1280,512]{1,0:T(8,128)(2,1)}, bf16[4,1280,512]{2,1,0:T(8,128)(2,1)}) custom-call(bf16[8,8,112,1280]{3,2,1,0:T(8,128)(2,1)} %get-tuple-element.62.y_ref, s32[8,8,512]{2,1,0:T(8,128)} %get-tuple-element.63.slot_ref, bf16[1280,512]{1,0:T(8,128)(2,1)} %get-tuple-element.61.grad_ref, ...), custom_call_target="tpu_custom_call" | custom-call | bytes 60000000 | tf_op jit(solution)/shard_map/collect_sending/pallas_call | solution.py:386
  182.2 0.2 reduce-scatter.7.cloned.1.call-start
  182.4 18.1 %spread_grad.1.gx_ref = bf16[8,8,112,1280]{3,2,1,0:T(8,128)(2,1)} custom-call(bf16[1280,512]{1,0:T(8,128)(2,1)} %get-tuple-element.61.grad_ref, bf16[2,1280,512]{2,1,0:T(8,128)(2,1)} %get-tuple-element.64.near_ref, bf16[1280,512]{1,0:T(8,128)(2,1)} %get-tuple-element.66.far_ref, bf16[4,1280,512]{2,1,0:T(8,128)(2,1)} %get-tuple-element.67.given_ref, ...), custom_call_target="tpu_custom_call" | custom-call | bytes 48000000 | tf_op jit(solution)/shard_map/spread_grad/pallas_call | solution.py:451
  200.5 47.2 %experts_backward.1 = (bf16[8,8,112,1280]{3,2,1,0:T(8,128)(2,1)}, f32[8,224,1280]{2,1,0:T(8,128)}, f32[8,224,1280]{2,1,0:T(8,128)}, f32[8,224,1280]{2,1,0:T(8,128)}, f32[8,896,1]{2,1,0:T(8,128)}) custom-call(bf16[8,8,112,1280]{3,2,1,0:T(8,128)(2,1)} %get-tuple-element.59.x_ref, bf16[8,8,112,1280]{3,2,1,0:T(8,128)(2,1)} %spread_grad.1.gx_ref, ...), custom_call_target="tpu_custom_call" | custom-call | bytes 141000000 | tf_op jit(solution)/shard_map/experts_backward/pallas_call | solution.py:307
  247.7 116.2 %collect_sum.1 = (bf16[576,1280]{1,0:T(8,128)(2,1)}, bf16[1408,1280]{1,0:T(8,128)(2,1)}, bf16[512,1280]{1,0:T(8,128)(2,1)}) custom-call(bf16[8,8,112,1280]{3,2,1,0:T(8,128)(2,1)} %get-tuple-element.70.y_ref, s32[8,8,512]{2,1,0:T(8,128)} %get-tuple-element.63.slot_ref, f32[8,896,1]{2,1,0:T(8,128)} %get-tuple-element.71.gsw_ref, ...), custom_call_target="tpu_custom_call" | custom-call | bytes 393000000 | tf_op jit(solution)/shard_map/collect_sum/pallas_call | solution.py:1254
  363.9 2.0 add_convert_fusion
  366.0 1.6 copy.39
  367.6 96.4 %back.1 = (f32[320,512]{1,0:T(8,128)}, bf16[384,1280]{1,0:T(8,128)(2,1)}, bf16[384,1280]{1,0:T(8,128)(2,1)}, bf16[384,1280]{1,0:T(8,128)(2,1)}, bf16[256,1280]{1,0:T(8,128)(2,1)}) custom-call(bf16[576,1280]{1,0:T(8,128)(2,1)} %get-tuple-element.73.sums_ref, f32[512,1280]{1,0:T(8,128)} %get-tuple-element.57.residual_ref, ...), custom_call_target="tpu_custom_call" | custom-call | bytes 270000000 | tf_op jit(solution)/shard_map/back/pallas_call | solution.py:1522
  464.0 8.9 %widen.1 = (f32[320,1280]{1,0:T(8,128)}, f32[320,1280]{1,0:T(8,128)}, f32[320,1280]{1,0:T(8,128)}, f32[320,1280]{1,0:T(8,128)}, f32[64,1280]{1,0:T(8,128)}, /*in...) custom-call(bf16[384,1280]{1,0:T(8,128)(2,1)} %get-tuple-element.82.early_ref, ...), custom_call_target="tpu_custom_call" | custom-call | bytes 24000000 | tf_op jit(solution)/shard_map/widen/pallas_call | solution.py:1581
  472.9 1.5 slice_reduce_fusion
  474.4 1.2 copy.40
  475.6 1.5 add_convert_fusion.1
  477.1 0.9 copy.38
  478.0 0.8 copy.42
  (6 shorter events, 0.1 us)
Async XLA Ops:
  7.2 356.7 %reduce-scatter.5.cloned.1.call-start = ((), (), s32[]{:S(2)}) async-start(), calls=%async_computation.2 | async-start | bytes 11796480 | tf_op jit(solution)/shard_map/reduce_scatter | solution.py:1867
  182.2 292.2 %reduce-scatter.7.cloned.1.call-start = ((), (), s32[]{:S(2)}) async-start(), calls=%async_computation.3 | async-start | bytes 1638400
  472.9 5.1 %copy-start = (f32[320,512]{1,0:T(8,128)S(1)}, f32[320,512]{1,0:T(8,128)}, u32[]{:S(2)}) copy-start(f32[320,512]{1,0:T(8,128)} %get-tuple-element.81) | copy-start | bytes 1966084
Sparse Core Ops, SparseCore 0:
  182.3 80.0 reduce-scatter.4
  367.7 49.3 reduce-scatter.6

commit v4 on v3

--- a/solution.py
+++ b/solution.py
@@ -499,6 +499,7 @@
 
 MESH = pl.DeviceIdType.MESH
 EXTRA = 64
+SUM_STARTS = (0, 192, 384)
 
 
 def places():
@@ -522,6 +523,47 @@
 
 def block(q, size):
     return pl.ds(pl.multiple_of(q * size, 16), size)
+
+
+def weight_gather(out_ref, csend, crecv, send, recv):
+    chip, core, z, cx, cy, cd = places()
+    other = 1 - core
+    c_peer = (chip, other, z)
+    chips = (cx, cy, cd)
+    count = out_ref.shape[0] // 2
+    piece = count // 4
+
+    def place(c, k):
+        return pl.ds(pl.multiple_of(k * count + c * piece, 16), piece)
+
+    def give(number, c, k, sems, peer):
+        return remote(out_ref.at[place(c, k)], out_ref.at[place(c, k)], *sems(number), peer)
+
+    def chip_sems(i):
+        return send.at[3 + i], recv.at[3 + i]
+
+    def core_sems(i):
+        return csend.at[1 + i], crecv.at[1 + i]
+
+    gather = [give(i, chip, core, chip_sems, (c, core, z)) for i, c in enumerate(chips)]
+    over = [give(i, c, core, core_sems, c_peer) for i, c in enumerate((*chips, chip))]
+
+    def put(done):
+        out_ref[place(chip, core)] = done.astype(bf16)
+        for i in (2, 0, 1):
+            gather[i].start()
+        over[3].start()
+
+    def end():
+        for i, c in enumerate(chips):
+            give(i, c, core, chip_sems, (c, core, z)).wait_recv()
+            over[i].start()
+        for i, c in enumerate((*chips, chip)):
+            give(i, c, other, core_sems, c_peer).wait_recv()
+        for copy in (*gather, *over):
+            copy.wait_send()
+
+    return put, end
 
 
 def weight_sum(grads, given, half, land, out_ref, csend, crecv, send, recv):
@@ -537,6 +579,8 @@
         remote(half.at[block(c, piece)], land.at[i], send.at[i], recv.at[i], (c, core, z))
         for i, c in enumerate(chips)
     ]
+    if out_ref is not None:
+        put, gathered = weight_gather(out_ref, csend, crecv, send, recv)
 
     def share():
         to_core.wait_recv()
@@ -544,41 +588,23 @@
         for i in (2, 0, 1):
             scatter[i].start()
 
-    def place(c, k):
-        return pl.ds(pl.multiple_of(k * count + c * piece, 16), piece)
-
-    def give(number, c, k, sems, peer):
-        return remote(out_ref.at[place(c, k)], out_ref.at[place(c, k)], *sems(number), peer)
-
-    def chip_sems(i):
-        return send.at[3 + i], recv.at[3 + i]
-
-    def core_sems(i):
-        return csend.at[1 + i], crecv.at[1 + i]
-
-    gather = [give(i, chip, core, chip_sems, (c, core, z)) for i, c in enumerate(chips)]
-    over = [give(i, c, core, core_sems, c_peer) for i, c in enumerate((*chips, chip))]
-
-    def give_back():
+    def total():
         done = half[block(chip, piece)].astype(f32)
         for i in range(3):
             scatter[i].wait_recv()
             done = done + land[i].astype(f32)
-        out_ref[place(chip, core)] = done.astype(bf16)
-        for i in (2, 0, 1):
-            gather[i].start()
-        over[3].start()
+        return done
+
+    def give_back():
+        put(total())
 
     def end():
-        for i, c in enumerate(chips):
-            give(i, c, core, chip_sems, (c, core, z)).wait_recv()
-            over[i].start()
-        for i, c in enumerate((*chips, chip)):
-            give(i, c, other, core_sems, c_peer).wait_recv()
-        for copy in (to_core, *scatter, *gather, *over):
+        if out_ref is not None:
+            gathered()
+        for copy in (to_core, *scatter):
             copy.wait_send()
 
-    return to_core.start, share, give_back, end
+    return to_core.start, share, give_back, end, total
 
 
 def weight_sum_scratch(tall, width):
@@ -1063,28 +1089,31 @@
     def to_core(p):
         return remote(stage.at[p % 2], given.at[p], core_send.at[p], core_recv.at[p], c_peer)
 
-    units = 3
-    unit = tall // units
-    half, part = unit // 2, unit // 4
+    starts = (*SUM_STARTS, tall)
+    units = len(starts) - 1
+    sizes = [starts[u + 1] - starts[u] for u in range(units)]
 
     def top(u):
-        return pl.ds(u * unit, half)
+        return pl.ds(starts[u], sizes[u] // 2)
 
     def low(u):
-        return pl.ds(u * unit + half, half)
+        return pl.ds(starts[u] + sizes[u] // 2, sizes[u] // 2)
+
+    def first(u, of):
+        return pl.ds(0, sizes[u] // of)
 
     def over(u, number, src, dst, peer):
         return remote(src, dst, send.at[u, number], recv.at[u, number], peer)
 
-    far_top = [over(u, 0, sums.at[0, top(u)], relay.at[u, 0], x_peer) for u in range(units)]
-    far_low = [over(u, 1, sums.at[0, low(u)], relay.at[u, 1], y_peer) for u in range(units)]
+    far_top = [over(u, 0, sums.at[0, top(u)], relay.at[u, 0, first(u, 2)], x_peer) for u in range(units)]
+    far_low = [over(u, 1, sums.at[0, low(u)], relay.at[u, 1, first(u, 2)], y_peer) for u in range(units)]
     x_top = [over(u, 2, sums.at[1, top(u)], land.at[0, top(u)], x_peer) for u in range(units)]
     x_low = [over(u, 3, sums.at[1, low(u)], land.at[0, low(u)], x_peer) for u in range(units)]
     y_low = [over(u, 4, sums.at[2, low(u)], land.at[1, low(u)], y_peer) for u in range(units)]
     y_top = [over(u, 5, sums.at[2, top(u)], land.at[1, top(u)], y_peer) for u in range(units)]
 
     in_copy(0).start()
-    start, share, give_back, end = weight_sum(grads, *more[:3], sum_ref, *more[3:])
+    start, share, _, end, total = weight_sum(grads, *more[:3], None, *more[3:])
 
     def shared_expert():
         normed, grad_t = normed_ref[...], grad_ref[...]
@@ -1158,16 +1187,17 @@
     lax.fori_loop(0, 8, step, 0)
     def relayed(u):
         far_low[u].wait_recv()
-        at = slice(u * unit + half, (u + 1) * unit)
-        sums[1, at] = (sums[1, at].astype(f32) + relay[u, 1].astype(f32)).astype(bf16)
+        at = low(u)
+        sums[1, at] = (sums[1, at].astype(f32) + relay[u, 1, first(u, 2)].astype(f32)).astype(bf16)
         x_low[u].start()
         far_top[u].wait_recv()
-        at = slice(u * unit, u * unit + half)
-        sums[2, at] = (sums[2, at].astype(f32) + relay[u, 0].astype(f32)).astype(bf16)
+        at = top(u)
+        sums[2, at] = (sums[2, at].astype(f32) + relay[u, 0, first(u, 2)].astype(f32)).astype(bf16)
         y_top[u].start()
 
     def block_of(u, q):
-        return pl.ds(pl.multiple_of(u * unit + q * part, 16), part)
+        part = sizes[u] // 4
+        return pl.ds(pl.multiple_of(starts[u] + q * part, 16), part)
 
     def z_sems(u, number):
         return zsend.at[u, number], zrecv.at[u, number]
@@ -1176,7 +1206,7 @@
         [
             remote(
                 sums.at[3, block_of(u, (z + i) % 4)],
-                zland.at[u, i - 1],
+                zland.at[u, i - 1, first(u, 4)],
                 *z_sems(u, i - 1),
                 z_peers[i - 1],
             )
@@ -1192,15 +1222,15 @@
     def landed(u):
         for copy in (x_top[u], y_top[u], x_low[u], y_low[u]):
             copy.wait_recv()
-        at = slice(u * unit, (u + 1) * unit)
+        at = slice(starts[u], starts[u + 1])
         added = sums[3, at].astype(f32) + land[0, at].astype(f32) + land[1, at].astype(f32)
-        ours = min(rows, (u + 1) * unit) - u * unit
-        if ours == unit:
+        ours = min(rows, starts[u + 1]) - starts[u]
+        if ours == sizes[u]:
             sums[3, at] = (added + mine[at].astype(f32)).astype(bf16)
         else:
-            here = slice(u * unit, u * unit + ours)
+            here = slice(starts[u], starts[u] + ours)
             sums[3, here] = (added[:ours] + mine[here].astype(f32)).astype(bf16)
-            sums[3, u * unit + ours : (u + 1) * unit] = added[ours:].astype(bf16)
+            sums[3, starts[u] + ours : starts[u + 1]] = added[ours:].astype(bf16)
         for i in (1, 0, 2):
             scatter[u][i].start()
 
@@ -1208,30 +1238,31 @@
         done = sums[3, block_of(u, z)].astype(f32)
         for i in range(3):
             scatter[u][i].wait_recv()
-            done = done + zland[u, i].astype(f32)
+            done = done + zland[u, i, first(u, 4)].astype(f32)
         out_ref[block_of(u, z)] = done.astype(bf16)
         for i in (2, 1, 3):
             back_copy(u, z, i).start()
 
     relayed(0)
-    x_top[1].start()
-    y_low[1].start()
-    far_top[2].start()
-    far_low[2].start()
-    shared_expert()
-    relayed(1)
-    x_top[2].start()
-    y_low[2].start()
-    landed(0)
-    relayed(2)
-    share()
-    landed(1)
-    summed(0)
-    landed(2)
-    summed(1)
-    give_back()
-    summed(2)
+    for u in range(1, units):
+        x_top[u].start()
+        y_low[u].start()
+        if u < units - 1:
+            far_top[u + 1].start()
+            far_low[u + 1].start()
+        if u == 1:
+            shared_expert()
+        relayed(u)
+        if u == units - 1:
+            share()
+        landed(u - 1)
+        if u >= 2:
+            summed(u - 2)
+    landed(units - 1)
+    summed(units - 2)
+    sum_ref[...] = total().astype(bf16)
     end()
+    summed(units - 1)
     for u in range(units):
         for i in (1, 2, 3):
             back_copy(u, (z + 4 - i) % 4, i).wait_recv()
@@ -1249,6 +1280,8 @@
     rows = slot.shape[2]
     tall = rows + EXTRA
     dma = pltpu.SemaphoreType.DMA
+    units = len(SUM_STARTS)
+    most = max(b - a for a, b in zip(SUM_STARTS, (*SUM_STARTS[1:], tall)))
     weights = 128 * (-(-sum(a.shape[0] for a in shared) // 128))
     vmem = pl.BlockSpec(memory_space=pltpu.VMEM)
     return pl.pallas_call(
@@ -1257,7 +1290,7 @@
         out_specs=[vmem, vmem, vmem],
         out_shape=[
             jax.ShapeDtypeStruct((tall, width), bf16),
-            jax.ShapeDtypeStruct((weights, width), bf16),
+            jax.ShapeDtypeStruct((weights // 8, width), bf16),
             jax.ShapeDtypeStruct((rows, width), bf16),
         ],
         scratch_shapes=[
@@ -1267,16 +1300,16 @@
             pltpu.VMEM((2, tall, width), bf16),
             pltpu.VMEM((4, tall, width), bf16),
             pltpu.VMEM((4, tall, width), bf16),
-            pltpu.VMEM((3, 2, tall // 6, width), bf16),
+            pltpu.VMEM((units, 2, most // 2, width), bf16),
             pltpu.VMEM((2, tall, width), bf16),
-            pltpu.VMEM((3, 3, tall // 12, width), bf16),
+            pltpu.VMEM((units, 3, most // 4, width), bf16),
             dma((2,)),
             dma((4,)),
             dma((4,)),
-            dma((3, 6)),
-            dma((3, 6)),
-            dma((3, 6)),
-            dma((3, 6)),
+            dma((units, 6)),
+            dma((units, 6)),
+            dma((units, 6)),
+            dma((units, 6)),
             *weight_sum_scratch(weights, width),
         ],
         compiler_params=pltpu.CompilerParams(
@@ -1296,9 +1329,10 @@
     gain_ref,
     cos_ref,
     sin_ref,
+    piece_ref,
     *refs,
 ):
-    late, outs, rest = refs[:11], refs[11:16], refs[16:]
+    late, outs, rest = refs[:11], refs[11:17], refs[17:]
     held, sems, rest = rest[:11], rest[11], rest[12:]
     loads = [pltpu.make_async_copy(a, b, sems.at[i]) for i, (a, b) in enumerate(zip(late, held))]
     for load in loads:
@@ -1313,6 +1347,7 @@
         gain_ref,
         cos_ref,
         sin_ref,
+        piece_ref,
         *held,
         *outs,
         *rest,
@@ -1329,6 +1364,7 @@
     gain_ref,
     cos_ref,
     sin_ref,
+    piece_ref,
     out_ref,
     q_ref,
     k_ref,
@@ -1345,6 +1381,7 @@
     first_ref,
     second_ref,
     shared_ref,
+    shared_sum_ref,
     dq_ref,
     dk_ref,
     dv_ref,
@@ -1380,6 +1417,8 @@
     spare = quarter - whole
     heads = whole // HEAD_DIM
     greet([c_peer, *[(c, core, z) for c in (cx, cy, cd)], *z_peers])
+    put, gathered = weight_gather(shared_sum_ref, *more[32:])
+    put(piece_ref[...])
 
     logits = nt(router_ref[...], normed2_ref[...])
     raised = jnp.exp(logits - jnp.max(logits, axis=0, keepdims=True))
@@ -1450,14 +1489,7 @@
     few_to_z = [
         remote(mine, theirs.at[i], lsend.at[i], lrecv.at[i], peer) for i, peer in enumerate(z_peers)
     ]
-    for i in (1, 0, 2):
-        to_z[i].start()
-    loads[8].wait()
     loads[9].wait()
-    loads[10].wait()
-    early[:quarter] = nt(low_t[own], attended_ref[...]).astype(bf16)
-    early[quarter:] = grad_router.astype(bf16)
-    groups[0][START]()
     x_t[...] = x_ref[...].T
     gain_column[...] = jnp.broadcast_to(gain_ref[0:1], (8, width)).T
     x_all = x_t[...].astype(f32)
@@ -1468,7 +1500,14 @@
     mine[:, rows:] = nt(jnp.ones((8, rows), bf16), (along * rms1).astype(bf16))
     for copy in few_to_z:
         copy.start()
-
+    for i in (1, 0, 2):
+        to_z[i].start()
+
+    loads[8].wait()
+    loads[10].wait()
+    early[:quarter] = nt(low_t[own], attended_ref[...]).astype(bf16)
+    early[quarter:] = grad_router.astype(bf16)
+    groups[0][START]()
     normed = normed_ref[...]
     for h in range(heads + 1):
         if h < heads:
@@ -1506,6 +1545,7 @@
 
     groups[2][GIVE_BACK]()
     groups[3][GIVE_BACK]()
+    gathered()
     for group in groups:
         group[END]()
     for copy in (*to_z, *few_to_z):
@@ -1517,15 +1557,16 @@
     rows = now[1].shape[0]
     spare = quarter % HEAD_DIM
     tall = [quarter + now[4].shape[0], 3 * HEAD_DIM, 3 * HEAD_DIM, 3 * spare + 64]
+    shared = 8 * now[8].shape[0]
     vmem = pl.BlockSpec(memory_space=pltpu.VMEM)
     dma = pltpu.SemaphoreType.DMA
     return pl.pallas_call(
         back_kernel,
         in_specs=[vmem] * len(now) + [pl.BlockSpec(memory_space=pl.ANY)] * len(late),
-        out_specs=[vmem] * 5,
+        out_specs=[vmem] * 6,
         out_shape=[
             jax.ShapeDtypeStruct((quarter, rows), f32),
-            *[jax.ShapeDtypeStruct((lines, width), bf16) for lines in tall],
+            *[jax.ShapeDtypeStruct((lines, width), bf16) for lines in (*tall, shared)],
         ],
         scratch_shapes=[
             *[pltpu.VMEM(a.shape, a.dtype) for a in late],
@@ -1545,6 +1586,10 @@
             dma((3,)),
             dma((3,)),
             *[one for lines in tall for one in weight_sum_scratch(lines, width)],
+            dma((5,)),
+            dma((5,)),
+            dma((6,)),
+            dma((6,)),
         ],
         compiler_params=pltpu.CompilerParams(
             vmem_limit_bytes=VMEM_LIMIT, collective_id=3, has_side_effects=True
@@ -1805,15 +1850,15 @@
     )
 
     if small:
-        back_sums, shared_sums, shared_part = collect_sum(
+        back_sums, shared_piece, shared_part = collect_sum(
             ex_back, slot, grad_slot_weight, normed2, grad_t, shared_gate.T, shared_up.T, shared_down
         )
         grad_tokens, *sums = back(
-            (back_sums, residual, normed2, grad_t, router_t, both_gains, *tables),
+            (back_sums, residual, normed2, grad_t, router_t, both_gains, *tables, shared_piece),
             (out_t, q, k, v, probs, query_t, key_t, value_t, attended_t, tokens, normed1),
         )
         *heads_sums, grad_router, gains, sum_gate, sum_up, sum_down = widen(
-            [*sums, shared_sums], quarter, shared_down.shape[0]
+            sums, quarter, shared_down.shape[0]
         )
         shared_sums = sum_gate, sum_up, sum_down
         grad_attn_gain, grad_ffn_gain = gains[0], gains[1]

time: 493 us -> 473 us (0.959)
  Pallas kernels: 456 us -> 437 us
    pallas_call x1, Pallas kernels: 96.4 us -> 78.7 us  [back(): pl.pallas_call(back_kernel, in_specs=[vmem] * len(now) + [pl.BlockSpec(me...]
  transfers between devices with their start and end apart: 2 -> 2, of which waited for: 0 -> 0; matrix products, arithmetic and copies ran while one was open for 0% -> 0% of each run, Pallas kernels for 59% -> 57%
where the time goes in v4:
time: 473 us; the launch traced here: 467 us
  Pallas kernels  437 us (92%)
  between operations  14.4 us (3%)
  local copies, waits for them, and re-layouts  7.45 us (2%)
  other arithmetic  6.6 us (1%)
    pallas_call x1, Pallas kernels, collect_sum(): pl.pallas_call(collect_sum_kernel, in_specs=[pl.BlockSpec(memory_space=pl...  115 us
    pallas_call x1, Pallas kernels, back(): pl.pallas_call(back_kernel, in_specs=[vmem] * len(now) + [pl.BlockSpec(me...  78.7 us
    pallas_call x1, Pallas kernels, gather_spread(): pl.pallas_call(gather_spread_kernel, in_specs=[vmem] * 4, out_specs=[pl.B...  58.8 us
    pallas_call x1, Pallas kernels, front(): pl.pallas_call(front_kernel, in_specs=[vmem] * 9, out_specs=[pl.BlockSpec...  52.1 us
    pallas_call x1, Pallas kernels, experts_backward(): pl.pallas_call(functools.partial(experts_backward_kernel, groups), grid=(...  47.2 us
    pallas_call x1, Pallas kernels, experts_forward(): pl.pallas_call(kernel, grid=(local, groups), in_specs=in_specs, out_specs...  35.2 us
    pallas_call x1, Pallas kernels, collect_sending(): pl.pallas_call(collect_sending_kernel, grid=(s,), in_specs=[pl.BlockSpec(...  23.3 us
    pallas_call x1, Pallas kernels, spread_grad(): pl.pallas_call(spread_grad_kernel, in_specs=[whole] * 4 + [pl.BlockSpec(m...  18.1 us
  transfers between devices with their start and end apart: 2, of which 0 were waited for; matrix products, arithmetic and copies ran while one was open for 0% of the time, Pallas kernels for 57%

profile of v4, /device:TPU:9, one launch (start us, length us, event | category | flops | bytes accessed | tf_op | source)
XLA Modules:
  0.0 466.8 jit_solution(4577393898267998282)
XLA Ops:
  7.2 0.0 reduce-scatter.5.cloned.1.call-start
  7.3 0.7 stack.9
  8.0 0.7 stack.10
  8.7 0.8 fusion.1
  9.5 0.9 fusion.slots_ref
  10.4 0.6 pad_maximum_fusion.gain_ref
  11.0 1.6 fusion.2.router_ref
  12.7 52.1 %front.1 = (bf16[512,1280]{1,0:T(8,128)(2,1)}, bf16[3,128,512]{2,1,0:T(8,128)(2,1)}, bf16[3,128,512]{2,1,0:T(8,128)(2,1)}, bf16[3,128,512]{2,1,0:T(8,128)(2,1)},...) custom-call(bf16[512,1280]{1,0:T(8,128)(2,1)} %refs_9_.1, ...), custom_call_target="tpu_custom_call" | custom-call | bytes 150000000 | tf_op jit(solution)/shard_map/front/pallas_call | solution.py:1009
  64.8 58.8 %gather_spread.1 = (bf16[8,8,112,1280]{3,2,1,0:T(8,128)(2,1)}, f32[8,896,1]{2,1,0:T(8,128)}, s32[8,8,512]{2,1,0:T(8,128)}, bf16[1280,512]{1,0:T(8,128)(2,1)}) custom-call(bf16[512,1280]{1,0:T(8,128)(2,1)} %get-tuple-element.59.own_ref.normed_ref.normed2_ref, bf16[64,512]{1,0:T(8,128)(2,1)} %fusion.slots_ref, bf16[64,1280]{1,0:T(8,128)(2,1)} %fusion.2.router_ref, ...), custom_call_target="tpu_custom_call" | custom-call | bytes 186000000 | tf_op jit(solution)/shard_map/gather_spread/pallas_call | solution.py:768
  123.6 35.2 %experts_forward.1 = (bf16[8,8,112,1280]{3,2,1,0:T(8,128)(2,1)}, f32[8,896,256]{2,1,0:T(8,128)}, f32[8,896,256]{2,1,0:T(8,128)}, bf16[2,1280,512]{2,1,0:T(8,128)(2,1)}) custom-call(bf16[8,8,112,1280]{3,2,1,0:T(8,128)(2,1)} %get-tuple-element.60.x_ref, f32[8,896,1]{2,1,0:T(8,128)} %get-tuple-element.61.sw_ref, bf16[8,224,1280]{2,1,0:T(8,128)(2,1)} %bitcast.27, ...), custom_call_target="tpu_custom_call" | custom-call | bytes 93000000 | tf_op jit(solution)/shard_map/experts_forward/pallas_call | solution.py:289
  158.8 23.3 %collect_sending.1 = (bf16[8,512,1280]{2,1,0:T(8,128)(2,1)}, bf16[1280,512]{1,0:T(8,128)(2,1)}, bf16[4,1280,512]{2,1,0:T(8,128)(2,1)}) custom-call(bf16[8,8,112,1280]{3,2,1,0:T(8,128)(2,1)} %get-tuple-element.63.y_ref, s32[8,8,512]{2,1,0:T(8,128)} %get-tuple-element.64.slot_ref, bf16[1280,512]{1,0:T(8,128)(2,1)} %get-tuple-element.62.grad_ref, ...), custom_call_target="tpu_custom_call" | custom-call | bytes 60000000 | tf_op jit(solution)/shard_map/collect_sending/pallas_call | solution.py:386
  182.2 0.2 reduce-scatter.7.cloned.1.call-start
  182.4 18.1 %spread_grad.1.gx_ref = bf16[8,8,112,1280]{3,2,1,0:T(8,128)(2,1)} custom-call(bf16[1280,512]{1,0:T(8,128)(2,1)} %get-tuple-element.62.grad_ref, bf16[2,1280,512]{2,1,0:T(8,128)(2,1)} %get-tuple-element.65.near_ref, bf16[1280,512]{1,0:T(8,128)(2,1)} %get-tuple-element.67.far_ref, bf16[4,1280,512]{2,1,0:T(8,128)(2,1)} %get-tuple-element.68.given_ref, ...), custom_call_target="tpu_custom_call" | custom-call | bytes 48000000 | tf_op jit(solution)/shard_map/spread_grad/pallas_call | solution.py:451
  200.5 47.2 %experts_backward.1 = (bf16[8,8,112,1280]{3,2,1,0:T(8,128)(2,1)}, f32[8,224,1280]{2,1,0:T(8,128)}, f32[8,224,1280]{2,1,0:T(8,128)}, f32[8,224,1280]{2,1,0:T(8,128)}, f32[8,896,1]{2,1,0:T(8,128)}) custom-call(bf16[8,8,112,1280]{3,2,1,0:T(8,128)(2,1)} %get-tuple-element.60.x_ref, bf16[8,8,112,1280]{3,2,1,0:T(8,128)(2,1)} %spread_grad.1.gx_ref, ...), custom_call_target="tpu_custom_call" | custom-call | bytes 141000000 | tf_op jit(solution)/shard_map/experts_backward/pallas_call | solution.py:307
  247.7 114.7 %collect_sum.1 = (bf16[576,1280]{1,0:T(8,128)(2,1)}, bf16[176,1280]{1,0:T(8,128)(2,1)}, bf16[512,1280]{1,0:T(8,128)(2,1)}) custom-call(bf16[8,8,112,1280]{3,2,1,0:T(8,128)(2,1)} %get-tuple-element.71.y_ref, s32[8,8,512]{2,1,0:T(8,128)} %get-tuple-element.64.slot_ref, f32[8,896,1]{2,1,0:T(8,128)} %get-tuple-element.72.gsw_ref, ...), custom_call_target="tpu_custom_call" | custom-call | bytes 393000000 | tf_op jit(solution)/shard_map/collect_sum/pallas_call | solution.py:1287
  362.5 2.0 add_convert_fusion
  364.5 1.6 copy.39
  366.2 78.7 %back.1 = (f32[320,512]{1,0:T(8,128)}, bf16[384,1280]{1,0:T(8,128)(2,1)}, bf16[384,1280]{1,0:T(8,128)(2,1)}, bf16[384,1280]{1,0:T(8,128)(2,1)}, bf16[256,1280]{1,0:T(8,128)(2,1)}, /*index=5*/bf16[1408,1280]{1,0:T(8,128)(2,1)}) custom-call(bf16[576,1280]{1,0:T(8,128)(2,1)} %get-tuple-element.74.sums_ref, f32[512,1280]{1,0:T(8,128)} %get-tuple-element.58.residual_ref, ...), custom_call_target="tpu_custom_call" | custom-call | bytes 270000000 | tf_op jit(solution)/shard_map/back/pallas_call | solution.py:1563
  444.9 8.9 %widen.1 = (f32[320,1280]{1,0:T(8,128)}, f32[320,1280]{1,0:T(8,128)}, f32[320,1280]{1,0:T(8,128)}, f32[320,1280]{1,0:T(8,128)}, f32[64,1280]{1,0:T(8,128)}, /*in...) custom-call(bf16[384,1280]{1,0:T(8,128)(2,1)} %get-tuple-element.84.early_ref, ...), custom_call_target="tpu_custom_call" | custom-call | bytes 24000000 | tf_op jit(solution)/shard_map/widen/pallas_call | solution.py:1626
  453.8 1.5 slice_reduce_fusion
  455.3 1.2 copy.40
  456.5 1.5 add_convert_fusion.1
  458.0 0.9 copy.38
  458.9 0.8 copy.42
  (6 shorter events, 0.1 us)
Async XLA Ops:
  7.2 355.3 %reduce-scatter.5.cloned.1.call-start = ((), (), s32[]{:S(2)}) async-start(), calls=%async_computation.2 | async-start | bytes 11796480 | tf_op jit(solution)/shard_map/reduce_scatter | solution.py:1912
  182.2 273.2 %reduce-scatter.7.cloned.1.call-start = ((), (), s32[]{:S(2)}) async-start(), calls=%async_computation.3 | async-start | bytes 1638400
  453.8 5.1 %copy-start = (f32[320,512]{1,0:T(8,128)S(1)}, f32[320,512]{1,0:T(8,128)}, u32[]{:S(2)}) copy-start(f32[320,512]{1,0:T(8,128)} %get-tuple-element.83) | copy-start | bytes 1966084
Sparse Core Ops, SparseCore 0:
  182.3 80.0 reduce-scatter.4
  366.3 51.3 reduce-scatter.6

commit v5 on v4

--- a/solution.py
+++ b/solution.py
@@ -499,7 +499,7 @@
 
 MESH = pl.DeviceIdType.MESH
 EXTRA = 64
-SUM_STARTS = (0, 192, 384)
+SUM_STARTS = (0, 192, 320, 448)
 
 
 def places():
@@ -1078,10 +1078,14 @@
 
     greet([x_peer, y_peer, c_peer, (cd, core, z), *z_peers])
 
+    def turn(t):
+        theirs = (t % 2) * (1 - t // 7) + (7 - t) // 7
+        return theirs * ((t + 1) // 2) + (1 - theirs) * (t // 2 - 1 + t // 7), theirs
+
     def sequence(t):
-        p = t // 2
+        p, theirs = turn(t)
         x, y = (chip % 2 + 1 + p // 2) % 2, (chip // 2 + 1 + p % 2) % 2
-        return (y * 2 + x) * 2 + (core + 1 + t % 2) % 2
+        return (y * 2 + x) * 2 + (core + theirs) % 2
 
     def in_copy(t):
         return pltpu.make_async_copy(y_ref.at[sequence(t)], ybuf.at[t % 2], copied.at[t % 2])
@@ -1138,7 +1142,7 @@
         def _():
             in_copy(t + 1).start()
 
-        p, s = t // 2, sequence(t)
+        (p, theirs), s = turn(t), sequence(t)
         probs = jnp.zeros((EXTRA, rows), f32)
         for e in range(local):
             mask = slot_ref[s, e : e + 1, :] == number
@@ -1149,7 +1153,7 @@
         in_copy(t).wait()
         back = tn(pick[...], ybuf[t % 2].reshape(local * CAP, -1))
 
-        @pl.when(t % 2 == 0)
+        @pl.when(theirs == 1)
         def _():
             @pl.when(p >= 2)
             def _():
@@ -1160,23 +1164,23 @@
             stage[p % 2, rows:, :rows] = probs.astype(bf16)
             to_core(p).start()
 
-        @pl.when(t % 2 == 1)
+        @pl.when(theirs == 0)
         def _():
             to_core(p).wait_recv()
             sums[p, :rows] = (back + given[p, :rows].astype(f32)).astype(bf16)
             sums[p, rows:] = given[p, rows:]
             sums[p, rows:, :rows] = (probs + given[p, rows:, :rows].astype(f32)).astype(bf16)
 
-        @pl.when(t == 1)
+        @pl.when(t == 2)
         def _():
             far_top[0].start()
             far_low[0].start()
 
-        @pl.when(t == 3)
+        @pl.when(t == 4)
         def _():
             x_top[0].start()
 
-        @pl.when(t == 5)
+        @pl.when(t == 6)
         def _():
             y_low[0].start()
             far_top[1].start()
@@ -1243,21 +1247,22 @@
         for i in (2, 1, 3):
             back_copy(u, z, i).start()
 
-    relayed(0)
-    for u in range(1, units):
-        x_top[u].start()
-        y_low[u].start()
+    for u in range(units):
+        relayed(u)
         if u < units - 1:
-            far_top[u + 1].start()
-            far_low[u + 1].start()
-        if u == 1:
+            x_top[u + 1].start()
+            y_low[u + 1].start()
+        if u < units - 2:
+            far_top[u + 2].start()
+            far_low[u + 2].start()
+        if u == 0:
             shared_expert()
-        relayed(u)
         if u == units - 1:
             share()
-        landed(u - 1)
-        if u >= 2:
-            summed(u - 2)
+        if u < units - 1:
+            landed(u)
+        if 1 <= u < units - 1:
+            summed(u - 1)
     landed(units - 1)
     summed(units - 2)
     sum_ref[...] = total().astype(bf16)

time: 473 us -> 466 us (0.985)
  Pallas kernels: 437 us -> 430 us
    pallas_call x1, Pallas kernels: 115 us -> 106 us  [collect_sum(): pl.pallas_call(collect_sum_kernel, in_specs=[pl.BlockSpec(memory_space=pl...]
where the time goes in v5:
time: 466 us; the launch traced here: 459 us
  Pallas kernels  430 us (92%)
  between operations  14.4 us (3%)
  local copies, waits for them, and re-layouts  7.45 us (2%)
  other arithmetic  6.6 us (1%)
    pallas_call x1, Pallas kernels, collect_sum(): pl.pallas_call(collect_sum_kernel, in_specs=[pl.BlockSpec(memory_space=pl...  106 us
    pallas_call x1, Pallas kernels, back(): pl.pallas_call(back_kernel, in_specs=[vmem] * len(now) + [pl.BlockSpec(me...  80.1 us
    pallas_call x1, Pallas kernels, gather_spread(): pl.pallas_call(gather_spread_kernel, in_specs=[vmem] * 4, out_specs=[pl.B...  58.8 us
    pallas_call x1, Pallas kernels, front(): pl.pallas_call(front_kernel, in_specs=[vmem] * 9, out_specs=[pl.BlockSpec...  52.1 us
    pallas_call x1, Pallas kernels, experts_backward(): pl.pallas_call(functools.partial(experts_backward_kernel, groups), grid=(...  47.2 us
    pallas_call x1, Pallas kernels, experts_forward(): pl.pallas_call(kernel, grid=(local, groups), in_specs=in_specs, out_specs...  35.2 us
    pallas_call x1, Pallas kernels, collect_sending(): pl.pallas_call(collect_sending_kernel, grid=(s,), in_specs=[pl.BlockSpec(...  23.3 us
    pallas_call x1, Pallas kernels, spread_grad(): pl.pallas_call(spread_grad_kernel, in_specs=[whole] * 4 + [pl.BlockSpec(m...  18.1 us
  transfers between devices with their start and end apart: 2, of which 0 were waited for; matrix products, arithmetic and copies ran while one was open for 0% of the time, Pallas kernels for 57%

profile of v5, /device:TPU:9, one launch (start us, length us, event | category | flops | bytes accessed | tf_op | source)
XLA Modules:
  0.0 459.4 jit_solution(366808780719935275)
XLA Ops:
  7.2 0.0 reduce-scatter.5.cloned.1.call-start
  7.3 0.7 stack.9
  8.0 0.7 stack.10
  8.7 0.8 fusion.1
  9.5 0.9 fusion.slots_ref
  10.4 0.6 pad_maximum_fusion.gain_ref
  11.0 1.6 fusion.2.router_ref
  12.7 52.1 %front.1 = (bf16[512,1280]{1,0:T(8,128)(2,1)}, bf16[3,128,512]{2,1,0:T(8,128)(2,1)}, bf16[3,128,512]{2,1,0:T(8,128)(2,1)}, bf16[3,128,512]{2,1,0:T(8,128)(2,1)},...) custom-call(bf16[512,1280]{1,0:T(8,128)(2,1)} %refs_9_.1, ...), custom_call_target="tpu_custom_call" | custom-call | bytes 150000000 | tf_op jit(solution)/shard_map/front/pallas_call | solution.py:1009
  64.8 58.8 %gather_spread.1 = (bf16[8,8,112,1280]{3,2,1,0:T(8,128)(2,1)}, f32[8,896,1]{2,1,0:T(8,128)}, s32[8,8,512]{2,1,0:T(8,128)}, bf16[1280,512]{1,0:T(8,128)(2,1)}) custom-call(bf16[512,1280]{1,0:T(8,128)(2,1)} %get-tuple-element.59.own_ref.normed_ref.normed2_ref, bf16[64,512]{1,0:T(8,128)(2,1)} %fusion.slots_ref, bf16[64,1280]{1,0:T(8,128)(2,1)} %fusion.2.router_ref, ...), custom_call_target="tpu_custom_call" | custom-call | bytes 186000000 | tf_op jit(solution)/shard_map/gather_spread/pallas_call | solution.py:768
  123.6 35.2 %experts_forward.1 = (bf16[8,8,112,1280]{3,2,1,0:T(8,128)(2,1)}, f32[8,896,256]{2,1,0:T(8,128)}, f32[8,896,256]{2,1,0:T(8,128)}, bf16[2,1280,512]{2,1,0:T(8,128)(2,1)}) custom-call(bf16[8,8,112,1280]{3,2,1,0:T(8,128)(2,1)} %get-tuple-element.60.x_ref, f32[8,896,1]{2,1,0:T(8,128)} %get-tuple-element.61.sw_ref, bf16[8,224,1280]{2,1,0:T(8,128)(2,1)} %bitcast.27, ...), custom_call_target="tpu_custom_call" | custom-call | bytes 93000000 | tf_op jit(solution)/shard_map/experts_forward/pallas_call | solution.py:289
  158.8 23.3 %collect_sending.1 = (bf16[8,512,1280]{2,1,0:T(8,128)(2,1)}, bf16[1280,512]{1,0:T(8,128)(2,1)}, bf16[4,1280,512]{2,1,0:T(8,128)(2,1)}) custom-call(bf16[8,8,112,1280]{3,2,1,0:T(8,128)(2,1)} %get-tuple-element.63.y_ref, s32[8,8,512]{2,1,0:T(8,128)} %get-tuple-element.64.slot_ref, bf16[1280,512]{1,0:T(8,128)(2,1)} %get-tuple-element.62.grad_ref, ...), custom_call_target="tpu_custom_call" | custom-call | bytes 60000000 | tf_op jit(solution)/shard_map/collect_sending/pallas_call | solution.py:386
  182.2 0.2 reduce-scatter.7.cloned.1.call-start
  182.4 18.1 %spread_grad.1.gx_ref = bf16[8,8,112,1280]{3,2,1,0:T(8,128)(2,1)} custom-call(bf16[1280,512]{1,0:T(8,128)(2,1)} %get-tuple-element.62.grad_ref, bf16[2,1280,512]{2,1,0:T(8,128)(2,1)} %get-tuple-element.65.near_ref, bf16[1280,512]{1,0:T(8,128)(2,1)} %get-tuple-element.67.far_ref, bf16[4,1280,512]{2,1,0:T(8,128)(2,1)} %get-tuple-element.68.given_ref, ...), custom_call_target="tpu_custom_call" | custom-call | bytes 48000000 | tf_op jit(solution)/shard_map/spread_grad/pallas_call | solution.py:451
  200.5 47.2 %experts_backward.1 = (bf16[8,8,112,1280]{3,2,1,0:T(8,128)(2,1)}, f32[8,224,1280]{2,1,0:T(8,128)}, f32[8,224,1280]{2,1,0:T(8,128)}, f32[8,224,1280]{2,1,0:T(8,128)}, f32[8,896,1]{2,1,0:T(8,128)}) custom-call(bf16[8,8,112,1280]{3,2,1,0:T(8,128)(2,1)} %get-tuple-element.60.x_ref, bf16[8,8,112,1280]{3,2,1,0:T(8,128)(2,1)} %spread_grad.1.gx_ref, ...), custom_call_target="tpu_custom_call" | custom-call | bytes 141000000 | tf_op jit(solution)/shard_map/experts_backward/pallas_call | solution.py:307
  247.7 106.0 %collect_sum.1 = (bf16[576,1280]{1,0:T(8,128)(2,1)}, bf16[176,1280]{1,0:T(8,128)(2,1)}, bf16[512,1280]{1,0:T(8,128)(2,1)}) custom-call(bf16[8,8,112,1280]{3,2,1,0:T(8,128)(2,1)} %get-tuple-element.71.y_ref, s32[8,8,512]{2,1,0:T(8,128)} %get-tuple-element.64.slot_ref, f32[8,896,1]{2,1,0:T(8,128)} %get-tuple-element.72.gsw_ref, ...), custom_call_target="tpu_custom_call" | custom-call | bytes 393000000 | tf_op jit(solution)/shard_map/collect_sum/pallas_call | solution.py:1292
  353.7 2.0 add_convert_fusion
  355.8 1.6 copy.39
  357.4 80.1 %back.1 = (f32[320,512]{1,0:T(8,128)}, bf16[384,1280]{1,0:T(8,128)(2,1)}, bf16[384,1280]{1,0:T(8,128)(2,1)}, bf16[384,1280]{1,0:T(8,128)(2,1)}, bf16[256,1280]{1,0:T(8,128)(2,1)}, /*index=5*/bf16[1408,1280]{1,0:T(8,128)(2,1)}) custom-call(bf16[576,1280]{1,0:T(8,128)(2,1)} %get-tuple-element.74.sums_ref, f32[512,1280]{1,0:T(8,128)} %get-tuple-element.58.residual_ref, ...), custom_call_target="tpu_custom_call" | custom-call | bytes 270000000 | tf_op jit(solution)/shard_map/back/pallas_call | solution.py:1568
  437.6 8.9 %widen.1 = (f32[320,1280]{1,0:T(8,128)}, f32[320,1280]{1,0:T(8,128)}, f32[320,1280]{1,0:T(8,128)}, f32[320,1280]{1,0:T(8,128)}, f32[64,1280]{1,0:T(8,128)}, /*in...) custom-call(bf16[384,1280]{1,0:T(8,128)(2,1)} %get-tuple-element.84.early_ref, ...), custom_call_target="tpu_custom_call" | custom-call | bytes 24000000 | tf_op jit(solution)/shard_map/widen/pallas_call | solution.py:1631
  446.5 1.5 slice_reduce_fusion
  448.0 1.2 copy.40
  449.2 1.5 add_convert_fusion.1
  450.7 0.9 copy.38
  451.6 0.8 copy.42
  (6 shorter events, 0.1 us)
Async XLA Ops:
  7.2 346.6 %reduce-scatter.5.cloned.1.call-start = ((), (), s32[]{:S(2)}) async-start(), calls=%async_computation.2 | async-start | bytes 11796480 | tf_op jit(solution)/shard_map/reduce_scatter | solution.py:1917
  182.2 265.8 %reduce-scatter.7.cloned.1.call-start = ((), (), s32[]{:S(2)}) async-start(), calls=%async_computation.3 | async-start | bytes 1638400
  446.5 5.1 %copy-start = (f32[320,512]{1,0:T(8,128)S(1)}, f32[320,512]{1,0:T(8,128)}, u32[]{:S(2)}) copy-start(f32[320,512]{1,0:T(8,128)} %get-tuple-element.83) | copy-start | bytes 1966084
Sparse Core Ops, SparseCore 0:
  182.3 80.0 reduce-scatter.4
  357.5 53.5 reduce-scatter.6

commit v6 on v5

--- a/solution.py
+++ b/solution.py
@@ -1039,14 +1039,20 @@
     y_ref,
     slot_ref,
     gsw_ref,
+    normed_in,
+    grad_in,
+    gate_in,
+    up_in,
+    down_in,
+    out_ref,
+    sum_ref,
+    forward_ref,
     normed_ref,
     grad_ref,
     gate_ref,
     up_ref,
     down_ref,
-    out_ref,
-    sum_ref,
-    forward_ref,
+    loaded,
     mine,
     pick,
     ybuf,
@@ -1117,9 +1123,16 @@
     y_top = [over(u, 5, sums.at[2, top(u)], land.at[1, top(u)], y_peer) for u in range(units)]
 
     in_copy(0).start()
+    late = (normed_in, grad_in, gate_in, up_in, down_in)
+    held = (normed_ref, grad_ref, gate_ref, up_ref, down_ref)
+    loads = [pltpu.make_async_copy(a, b, loaded.at[i]) for i, (a, b) in enumerate(zip(late, held))]
+    for load in loads:
+        load.start()
     start, share, _, end, total = weight_sum(grads, *more[:3], None, *more[3:])
 
     def shared_expert():
+        for load in loads:
+            load.wait()
         normed, grad_t = normed_ref[...], grad_ref[...]
         size = gate_ref.shape[0]
         gate, up = nt(gate_ref[...], normed), nt(up_ref[...], normed)
@@ -1289,9 +1302,10 @@
     most = max(b - a for a, b in zip(SUM_STARTS, (*SUM_STARTS[1:], tall)))
     weights = 128 * (-(-sum(a.shape[0] for a in shared) // 128))
     vmem = pl.BlockSpec(memory_space=pltpu.VMEM)
+    whole = pl.BlockSpec(memory_space=pl.ANY)
     return pl.pallas_call(
         collect_sum_kernel,
-        in_specs=[pl.BlockSpec(memory_space=pl.ANY)] + [vmem] * 7,
+        in_specs=[whole, vmem, vmem] + [whole] * 5,
         out_specs=[vmem, vmem, vmem],
         out_shape=[
             jax.ShapeDtypeStruct((tall, width), bf16),
@@ -1299,6 +1313,8 @@
             jax.ShapeDtypeStruct((rows, width), bf16),
         ],
         scratch_shapes=[
+            *[pltpu.VMEM(a.shape, a.dtype) for a in (normed, grad_t, *shared)],
+            dma((5,)),
             pltpu.VMEM((rows, width), bf16),
             pltpu.VMEM((local * cap, rows), bf16),
             pltpu.VMEM((2, local, cap, width), bf16),

time: 466 us -> 466 us (level)
  no operation moved by 1% of the time
where the time goes in v6:
time: 466 us; the launch traced here: 460 us
  Pallas kernels  430 us (92%)
  between operations  14.4 us (3%)
  local copies, waits for them, and re-layouts  7.45 us (2%)
  other arithmetic  6.6 us (1%)
    pallas_call x1, Pallas kernels, collect_sum(): pl.pallas_call(collect_sum_kernel, in_specs=[whole, vmem, vmem] + [whole]...  106 us
    pallas_call x1, Pallas kernels, back(): pl.pallas_call(back_kernel, in_specs=[vmem] * len(now) + [pl.BlockSpec(me...  80.2 us
    pallas_call x1, Pallas kernels, gather_spread(): pl.pallas_call(gather_spread_kernel, in_specs=[vmem] * 4, out_specs=[pl.B...  58.8 us
    pallas_call x1, Pallas kernels, front(): pl.pallas_call(front_kernel, in_specs=[vmem] * 9, out_specs=[pl.BlockSpec...  52.1 us
    pallas_call x1, Pallas kernels, experts_backward(): pl.pallas_call(functools.partial(experts_backward_kernel, groups), grid=(...  47.2 us
    pallas_call x1, Pallas kernels, experts_forward(): pl.pallas_call(kernel, grid=(local, groups), in_specs=in_specs, out_specs...  35.2 us
    pallas_call x1, Pallas kernels, collect_sending(): pl.pallas_call(collect_sending_kernel, grid=(s,), in_specs=[pl.BlockSpec(...  23.3 us
    pallas_call x1, Pallas kernels, spread_grad(): pl.pallas_call(spread_grad_kernel, in_specs=[whole] * 4 + [pl.BlockSpec(m...  18.1 us
  transfers between devices with their start and end apart: 2, of which 0 were waited for; matrix products, arithmetic and copies ran while one was open for 0% of the time, Pallas kernels for 57%

profile of v6, /device:TPU:9, one launch (start us, length us, event | category | flops | bytes accessed | tf_op | source)
XLA Modules:
  0.0 459.5 jit_solution(6694953381928981885)
XLA Ops:
  7.2 0.0 reduce-scatter.5.cloned.1.call-start
  7.3 0.7 stack.9
  8.0 0.7 stack.10
  8.7 0.8 fusion.1
  9.5 0.9 fusion.slots_ref
  10.4 0.6 pad_maximum_fusion.gain_ref
  11.0 1.6 fusion.2.router_ref
  12.7 52.1 %front.1 = (bf16[512,1280]{1,0:T(8,128)(2,1)}, bf16[3,128,512]{2,1,0:T(8,128)(2,1)}, bf16[3,128,512]{2,1,0:T(8,128)(2,1)}, bf16[3,128,512]{2,1,0:T(8,128)(2,1)},...) custom-call(bf16[512,1280]{1,0:T(8,128)(2,1)} %refs_9_.1, ...), custom_call_target="tpu_custom_call" | custom-call | bytes 150000000 | tf_op jit(solution)/shard_map/front/pallas_call | solution.py:1009
  64.8 58.8 %gather_spread.1 = (bf16[8,8,112,1280]{3,2,1,0:T(8,128)(2,1)}, f32[8,896,1]{2,1,0:T(8,128)}, s32[8,8,512]{2,1,0:T(8,128)}, bf16[1280,512]{1,0:T(8,128)(2,1)}) custom-call(bf16[512,1280]{1,0:T(8,128)(2,1)} %get-tuple-element.59.own_ref.normed_in.normed2_ref, bf16[64,512]{1,0:T(8,128)(2,1)} %fusion.slots_ref, bf16[64,1280]{1,0:T(8,128)(2,1)} %fusion.2.router_ref, ...), custom_call_target="tpu_custom_call" | custom-call | bytes 186000000 | tf_op jit(solution)/shard_map/gather_spread/pallas_call | solution.py:768
  123.6 35.2 %experts_forward.1 = (bf16[8,8,112,1280]{3,2,1,0:T(8,128)(2,1)}, f32[8,896,256]{2,1,0:T(8,128)}, f32[8,896,256]{2,1,0:T(8,128)}, bf16[2,1280,512]{2,1,0:T(8,128)(2,1)}) custom-call(bf16[8,8,112,1280]{3,2,1,0:T(8,128)(2,1)} %get-tuple-element.60.x_ref, f32[8,896,1]{2,1,0:T(8,128)} %get-tuple-element.61.sw_ref, bf16[8,224,1280]{2,1,0:T(8,128)(2,1)} %bitcast.27, ...), custom_call_target="tpu_custom_call" | custom-call | bytes 93000000 | tf_op jit(solution)/shard_map/experts_forward/pallas_call | solution.py:289
  158.8 23.3 %collect_sending.1 = (bf16[8,512,1280]{2,1,0:T(8,128)(2,1)}, bf16[1280,512]{1,0:T(8,128)(2,1)}, bf16[4,1280,512]{2,1,0:T(8,128)(2,1)}) custom-call(bf16[8,8,112,1280]{3,2,1,0:T(8,128)(2,1)} %get-tuple-element.63.y_ref, s32[8,8,512]{2,1,0:T(8,128)} %get-tuple-element.64.slot_ref, bf16[1280,512]{1,0:T(8,128)(2,1)} %get-tuple-element.62.grad_ref.grad_in, ...), custom_call_target="tpu_custom_call" | custom-call | bytes 60000000 | tf_op jit(solution)/shard_map/collect_sending/pallas_call | solution.py:386
  182.2 0.2 reduce-scatter.7.cloned.1.call-start
  182.4 18.1 %spread_grad.1.gx_ref = bf16[8,8,112,1280]{3,2,1,0:T(8,128)(2,1)} custom-call(bf16[1280,512]{1,0:T(8,128)(2,1)} %get-tuple-element.62.grad_ref.grad_in, bf16[2,1280,512]{2,1,0:T(8,128)(2,1)} %get-tuple-element.65.near_ref, bf16[1280,512]{1,0:T(8,128)(2,1)} %get-tuple-element.67.far_ref, bf16[4,1280,512]{2,1,0:T(8,128)(2,1)} %get-tuple-element.68.given_ref, ...), custom_call_target="tpu_custom_call" | custom-call | bytes 48000000 | tf_op jit(solution)/shard_map/spread_grad/pallas_call | solution.py:451
  200.5 47.2 %experts_backward.1 = (bf16[8,8,112,1280]{3,2,1,0:T(8,128)(2,1)}, f32[8,224,1280]{2,1,0:T(8,128)}, f32[8,224,1280]{2,1,0:T(8,128)}, f32[8,224,1280]{2,1,0:T(8,128)}, f32[8,896,1]{2,1,0:T(8,128)}) custom-call(bf16[8,8,112,1280]{3,2,1,0:T(8,128)(2,1)} %get-tuple-element.60.x_ref, bf16[8,8,112,1280]{3,2,1,0:T(8,128)(2,1)} %spread_grad.1.gx_ref, ...), custom_call_target="tpu_custom_call" | custom-call | bytes 141000000 | tf_op jit(solution)/shard_map/experts_backward/pallas_call | solution.py:307
  247.7 105.9 %collect_sum.1 = (bf16[576,1280]{1,0:T(8,128)(2,1)}, bf16[176,1280]{1,0:T(8,128)(2,1)}, bf16[512,1280]{1,0:T(8,128)(2,1)}) custom-call(bf16[8,8,112,1280]{3,2,1,0:T(8,128)(2,1)} %get-tuple-element.71.y_ref, s32[8,8,512]{2,1,0:T(8,128)} %get-tuple-element.64.slot_ref, f32[8,896,1]{2,1,0:T(8,128)} %get-tuple-element.72.gsw_ref, ...), custom_call_target="tpu_custom_call" | custom-call | bytes 393000000 | tf_op jit(solution)/shard_map/collect_sum/pallas_call | solution.py:1306
  353.7 2.0 add_convert_fusion
  355.7 1.6 copy.39
  357.4 80.2 %back.1 = (f32[320,512]{1,0:T(8,128)}, bf16[384,1280]{1,0:T(8,128)(2,1)}, bf16[384,1280]{1,0:T(8,128)(2,1)}, bf16[384,1280]{1,0:T(8,128)(2,1)}, bf16[256,1280]{1,0:T(8,128)(2,1)}, /*index=5*/bf16[1408,1280]{1,0:T(8,128)(2,1)}) custom-call(bf16[576,1280]{1,0:T(8,128)(2,1)} %get-tuple-element.74.sums_ref, f32[512,1280]{1,0:T(8,128)} %get-tuple-element.58.residual_ref, ...), custom_call_target="tpu_custom_call" | custom-call | bytes 270000000 | tf_op jit(solution)/shard_map/back/pallas_call | solution.py:1584
  437.7 8.9 %widen.1 = (f32[320,1280]{1,0:T(8,128)}, f32[320,1280]{1,0:T(8,128)}, f32[320,1280]{1,0:T(8,128)}, f32[320,1280]{1,0:T(8,128)}, f32[64,1280]{1,0:T(8,128)}, /*in...) custom-call(bf16[384,1280]{1,0:T(8,128)(2,1)} %get-tuple-element.84.early_ref, ...), custom_call_target="tpu_custom_call" | custom-call | bytes 24000000 | tf_op jit(solution)/shard_map/widen/pallas_call | solution.py:1647
  446.5 1.5 slice_reduce_fusion
  448.0 1.2 copy.40
  449.2 1.5 add_convert_fusion.1
  450.7 0.9 copy.38
  451.6 0.8 copy.42
  (6 shorter events, 0.1 us)
Async XLA Ops:
  7.2 346.5 %reduce-scatter.5.cloned.1.call-start = ((), (), s32[]{:S(2)}) async-start(), calls=%async_computation.2 | async-start | bytes 11796480 | tf_op jit(solution)/shard_map/reduce_scatter | solution.py:1933
  182.2 265.9 %reduce-scatter.7.cloned.1.call-start = ((), (), s32[]{:S(2)}) async-start(), calls=%async_computation.3 | async-start | bytes 1638400
  446.5 5.1 %copy-start = (f32[320,512]{1,0:T(8,128)S(1)}, f32[320,512]{1,0:T(8,128)}, u32[]{:S(2)}) copy-start(f32[320,512]{1,0:T(8,128)} %get-tuple-element.83) | copy-start | bytes 1966084
Sparse Core Ops, SparseCore 0:
  182.3 80.0 reduce-scatter.4
  357.5 53.7 reduce-scatter.6
